TPU v7x, 512 devices: a whole 4x8x8 slice. The times are simulated.
512 devices in a mesh: group: 16 (over x_lo, z), expert: 32 (over y, x_hi, core).
Axes of the slice: x: 4 (x_hi: 2, x_lo: 2; x = x_hi * 2 + x_lo), y: 8, z: 8, core: 2. Of those that a mesh axis runs over, the one named last changes fastest.
Arguments:
- tokens: bfloat16 [12288, 7168], P('expert', 'group'), may hold values from -6 to 6
- expert_ids: int32 [12288, 8], P('expert'), may hold values from 0 to 383, as said below
- combine: float32 [12288, 8], P('expert'), may hold values from 0.2 to 1
- w_in: bfloat16 [32, 2, 1024, 7168], P('expert', None, None, 'group'), may hold values from -0.0625 to 0.0625
- w_down: bfloat16 [32, 1024, 7168], P('expert', None, 'group'), may hold values from -0.1875 to 0.1875
Outputs:
- layer_out: bfloat16 [12288, 7168], P('expert', 'group')
Inputs may be any that keep to these rules, and one draw needn't show every extreme that they name: `expert_ids`: each row names 8 different experts of all 384. Among the 384 rows of one index of expert no expert is named by more than 18 rows, and one expert below 32 is named by exactly 18 rows in every such block.
All inputs are finite; a program needn't handle non-finite values.
Results may differ from a plain program's by a relative error of at most 0.03.
Values may be sent and summed in bfloat16 or wider, within the bound.
No kernel may reach another device: no remote copies, remote signals or barrier semaphores. Data moves between devices by JAX's collectives and lax.ppermute only.
A program may use at most 64 MiB of HBM per device.

v0:
```python
import jax
import jax.numpy as jnp
from jax import lax
from jax.sharding import PartitionSpec as P

CAP = 18


def routing(expert_ids, combine, experts, capacity):
    labels = jnp.arange(experts, dtype=jnp.int32)
    chosen = (expert_ids[:, :, None] == labels[None, None, :]).astype(jnp.int32)
    per_row = jnp.sum(chosen, axis=1)
    earlier = jnp.cumsum(per_row, axis=0) - per_row
    position = jnp.sum(earlier[:, None, :] * chosen, axis=2)
    target = expert_ids * capacity + position
    slot_labels = jnp.arange(experts * capacity, dtype=jnp.int32)
    placing = jnp.zeros((expert_ids.shape[0], experts * capacity), jnp.float32)
    weighting = jnp.zeros((expert_ids.shape[0], experts * capacity), jnp.float32)
    for pick in range(expert_ids.shape[1]):
        hit = target[:, pick, None] == slot_labels[None, :]
        placing = placing + hit.astype(jnp.float32)
        weighting = weighting + jnp.where(hit, combine[:, pick, None], 0.0)
    return (placing, weighting)


def local(tokens, expert_ids, combine, w_in, w_down):
    slice_width = tokens.shape[1]
    hidden_width = w_in.shape[2]
    experts = lax.axis_size("expert")
    groups = lax.axis_size("group")
    arrived_rows = experts * CAP
    placing, weighting = routing(expert_ids, combine, experts, CAP)
    outgoing = lax.dot_general(
        placing.astype(jnp.bfloat16),
        tokens,
        (((0,), (0,)), ((), ())),
        preferred_element_type=jnp.float32,
    )
    outgoing = outgoing.astype(jnp.bfloat16).reshape(experts, CAP, slice_width)
    arrived = lax.all_to_all(outgoing, "expert", split_axis=0, concat_axis=0, tiled=True)
    arrived = arrived.reshape(arrived_rows, slice_width)
    gate_up = w_in[0]
    down_proj = w_down[0]
    terms = jnp.einsum("rd,jhd->rjh", arrived, gate_up, preferred_element_type=jnp.float32)
    summed = lax.psum_scatter(
        terms.reshape(lax.axis_size("group") * (arrived_rows // groups), 2 * hidden_width).astype(
            jnp.bfloat16
        ),
        "group",
        scatter_dimension=0,
        tiled=True,
    ).astype(jnp.float32)
    summed = summed.reshape(-1, 2, hidden_width)
    expert_hidden = (jax.nn.silu(summed[:, 0]) * summed[:, 1]).astype(jnp.bfloat16)
    outputs = jnp.dot(
        lax.all_gather(expert_hidden, "group", axis=0, tiled=True),
        down_proj,
        preferred_element_type=jnp.float32,
    ).astype(jnp.bfloat16)
    returned = lax.all_to_all(
        outputs.reshape(experts, CAP, slice_width),
        "expert",
        split_axis=0,
        concat_axis=0,
        tiled=True,
    )
    flat_back = returned.reshape(arrived_rows, slice_width).astype(jnp.float32)
    routed = jnp.dot(
        weighting, flat_back, precision=lax.Precision.HIGHEST, preferred_element_type=jnp.float32
    )
    return routed.astype(jnp.bfloat16)


def solution(mesh):
    placed = (
        P("expert", "group"),
        P("expert", None),
        P("expert", None),
        P("expert", None, None, "group"),
        P("expert", None, "group"),
    )
    return jax.shard_map(
        local, mesh=mesh, in_specs=placed, out_specs=P("expert", "group"), check_vma=False
    )
```

profile of v0, /device:TPU:1, one launch (start us, length us, event | category | flops | bytes accessed | tf_op | source)
XLA Modules:
  0.0 232.0 jit_solution(3415796031018141137)
XLA Ops:
  6.5 0.8 convert_reduce_fusion
  7.4 0.9 reduce-window.6
  8.6 0.8 select_reduce_fusion
  9.4 0.7 multiply_add_fusion
  10.2 0.5 copy-done.3
  10.8 3.2 %convolution_convert_fusion.1 = bf16[576,448]{0,1:T(8,128)(2,1)} fusion(bf16[384,448]{0,1:T(8,128)(2,1)} %param.5, s32[384]{0:T(512)S(1)} %get-tuple-element.14, s32[384]{0:T(512)S(1)} %get-tuple-element.15, s32[384]{0:T(512)S(1)} %get-tuple-element.16, s32[384]{0:T(512)S(1)} %get-tuple-element.17, s32[384]{0:T(512)S(1)} %get-tuple-element.18, ...), kind=kOutput, calls=%fused_computation.1 | convolution fusion | flops 203747328 | bytes 872448 | tf_op jit(solution)/shard_map/dot_general | solution.py:33
  14.0 1.4 copy.28
  15.4 1.1 reshape.35
  16.5 11.2 %all-to-all-start = ((bf16[32,18,448]{2,1,0:T(8,128)(2,1)}), bf16[32,18,448]{2,1,0:T(8,128)(2,1)S(1)}, u32[]{:S(2)}, u32[]{:S(2)}) async-start(bf16[32,18,448]{2,1,0:T(8,128)(2,1)} %reshape.35), calls=%async_computation | async-start | bytes 1572864 | tf_op jit(solution)/shard_map/all_to_all | solution.py:40
  27.8 1.9 copy.29
  29.7 1.8 copy.37
  31.5 18.9 %all-to-all-done = bf16[32,18,448]{2,1,0:T(8,128)(2,1)S(1)} async-done(((bf16[32,18,448]{2,1,0:T(8,128)(2,1)}), bf16[32,18,448]{2,1,0:T(8,128)(2,1)S(1)}, u32[]{:S(2)}, u32[]{:S(2)}) %all-to-all-start) | async-done | bytes 516128 | tf_op jit(solution)/shard_map/all_to_all | solution.py:40
  50.3 1.2 reshape.36
  51.5 3.1 %convolution_convert_fusion = bf16[576,2048]{1,0:T(8,128)(2,1)S(1)} fusion(bf16[576,448]{1,0:T(8,128)(2,1)} %reshape.36, bf16[2048,448]{0,1:T(8,128)(2,1)} %bitcast.51), kind=kOutput, calls=%fused_computation | convolution fusion | flops 1058144256 | bytes 4710400 | tf_op jit(solution)/shard_map/rd,jhd->rjh/dot_general | solution.py:44
  54.6 44.3 %fusion = bf16[40,2048]{1,0:T(8,128)(2,1)S(1)} fusion(bf16[576,2048]{1,0:T(8,128)(2,1)S(1)} %convolution_convert_fusion), kind=kCustom, calls=%all-reduce-scatter | all-reduce-scatter fusion | flops 1310721 | bytes 2525184
  98.9 1.3 collective-permute-start
  100.2 1.9 collective-permute-start.1
  102.1 1.3 dynamic-slice.4
  104.1 0.5 collective-permute-done.1
  104.5 0.4 concatenate
  105.0 0.2 reshape.42
  105.3 0.2 fusion.47
  105.5 0.7 fusion.44
  106.3 68.0 %all-gather.3.cloned.1.call-done = bf16[16,36,1024]{2,1,0:T(8,128)(2,1)} async-done(((bf16[1,36,1024]{2,1,0:T(8,128)(2,1)}), bf16[16,36,1024]{2,1,0:T(8,128)(2,1)}) %all-gather.3.cloned.1.call-update) | async-done | bytes 1179664 | tf_op jit(solution)/shard_map/all_gather | solution.py:56
  174.3 1.4 reshape.44
  175.7 0.9 convolution_convert_fusion.2
  176.6 0.2 copy.32
  176.9 1.1 reshape.39
  178.0 20.0 %all-to-all-start.1 = ((bf16[32,18,448]{2,1,0:T(8,128)(2,1)}), bf16[32,18,448]{2,1,0:T(8,128)(2,1)S(1)}, u32[]{:S(2)}, u32[]{:S(2)}) async-start(bf16[32,18,448]{2,1,0:T(8,128)(2,1)} %reshape.39), calls=%async_computation.1 | async-start | bytes 1572864 | tf_op jit(solution)/shard_map/all_to_all | solution.py:60
  198.0 22.6 %all-to-all-done.1 = bf16[32,18,448]{2,1,0:T(8,128)(2,1)S(1)} async-done(((bf16[32,18,448]{2,1,0:T(8,128)(2,1)}), bf16[32,18,448]{2,1,0:T(8,128)(2,1)S(1)}, u32[]{:S(2)}, u32[]{:S(2)}) %all-to-all-start.1) | async-done | bytes 516128 | tf_op jit(solution)/shard_map/all_to_all | solution.py:60
  220.6 0.3 reshape.40
  220.9 4.2 %convolution_convert_fusion.3 = bf16[384,448]{0,1:T(8,128)(2,1)} fusion(bf16[576,448]{1,0:T(8,128)(2,1)S(1)} %reshape.40, f32[384]{0:T(512)S(1)} %get-tuple-element.11, s32[384]{0:T(512)S(1)} %get-tuple-element.14, f32[384]{0:T(512)S(1)} %get-tuple-element.12, s32[384]{0:T(512)S(1)} %get-tuple-element.15, f32[384]{0:T(512)S(1)} %get-tuple-element.6, ...), kind=kOutput, calls=%fused_computation.3 | convolution fusion | flops 1194344448 | bytes 884736 | tf_op jit(solution)/shard_map/dot_general | solution.py:68
  (32 shorter events, 0.6 us)
Async XLA Ops:
  6.5 169.1 %copy-start = (bf16[1,1024,448]{1,2,0:T(8,128)(2,1)S(1)}, bf16[1,1024,448]{1,2,0:T(8,128)(2,1)}, u32[]{:S(2)}) copy-start(bf16[1,1024,448]{1,2,0:T(8,128)(2,1)} %param.9) | copy-start | bytes 2752516
  10.2 0.6 copy-start.3
  10.2 0.6 copy-start.5
  10.2 0.6 copy-start.7
  10.2 0.6 copy-start.9
  14.0 13.8 %copy-start.1 = (bf16[1,2,1024,448]{2,3,1,0:T(8,128)(2,1)S(1)}, bf16[1,2,1024,448]{2,3,1,0:T(8,128)(2,1)}, u32[]{:S(2)}) copy-start(bf16[1,2,1024,448]{2,3,1,0:T(8,128)(2,1)} %param.8) | copy-start | bytes 5505028
  16.5 33.8 %all-to-all-start = ((bf16[32,18,448]{2,1,0:T(8,128)(2,1)}), bf16[32,18,448]{2,1,0:T(8,128)(2,1)S(1)}, u32[]{:S(2)}, u32[]{:S(2)}) async-start(bf16[32,18,448]{2,1,0:T(8,128)(2,1)} %reshape.35), calls=%async_computation | async-start | bytes 1572864 | tf_op jit(solution)/shard_map/all_to_all | solution.py:40
  27.7 146.5 %all-gather.3.cloned.1.call-start = ((), (), s32[]{:S(2)}) async-start(), calls=%async_computation.2 | async-start | bytes 1392640 | tf_op jit(solution)/shard_map/all_gather | solution.py:56
  98.9 5.7 %collective-permute-start = (bf16[40,2048]{1,0:T(8,128)(2,1)S(1)}, bf16[40,2048]{1,0:T(8,128)(2,1)S(1)}, u32[]{:S(2)}, u32[]{:S(2)}) collective-permute-start(bf16[40,2048]{1,0:T(8,128)(2,1)S(1)} %fusion), channel_id=1, source_target_pairs={{0,32},{32,64},{64,96},{96,128},{128,160},{160,192},{192,224},{224... | collective-permute-start | bytes 491528
  100.2 4.3 %collective-permute-start.1 = (bf16[20,2048]{1,0:T(8,128)(2,1)S(1)}, bf16[20,2048]{1,0:T(8,128)(2,1)S(1)}, u32[]{:S(2)}, u32[]{:S(2)}) collective-permute-start(bf16[20,2048]{1,0:T(8,128)(2,1)S(1)} %slice.91), channel_id=1, source_target_pairs={{0,64},{32,96},{64,128},{96,160},{128,192},{160,224},{192,256},{22... | collective-permute-start | bytes 245768
  176.6 21.4 %copy-start.2 = (f32[384,8]{0,1:T(8,128)S(1)}, f32[384,8]{0,1:T(8,128)}, u32[]{:S(2)}) copy-start(f32[384,8]{0,1:T(8,128)} %param.7) | copy-start | bytes 36868
  178.0 43.0 %copy-start.4 = (s32[384]{0:T(512)S(1)}, s32[384]{0:T(512)}, u32[]{:S(2)}) copy-start(s32[384]{0:T(512)} %copy-done.3) | copy-start | bytes 4612
  178.0 43.0 %copy-start.6 = (s32[384]{0:T(512)S(1)}, s32[384]{0:T(512)}, u32[]{:S(2)}) copy-start(s32[384]{0:T(512)} %copy-done.5) | copy-start | bytes 4612
  178.0 43.0 %copy-start.8 = (s32[384]{0:T(512)S(1)}, s32[384]{0:T(512)}, u32[]{:S(2)}) copy-start(s32[384]{0:T(512)} %copy-done.7) | copy-start | bytes 4612
  178.0 43.0 %copy-start.10 = (s32[384]{0:T(512)S(1)}, s32[384]{0:T(512)}, u32[]{:S(2)}) copy-start(s32[384]{0:T(512)} %copy-done.9) | copy-start | bytes 4612
  178.0 42.6 %all-to-all-start.1 = ((bf16[32,18,448]{2,1,0:T(8,128)(2,1)}), bf16[32,18,448]{2,1,0:T(8,128)(2,1)S(1)}, u32[]{:S(2)}, u32[]{:S(2)}) async-start(bf16[32,18,448]{2,1,0:T(8,128)(2,1)} %reshape.39), calls=%async_computation.1 | async-start | bytes 1572864 | tf_op jit(solution)/shard_map/all_to_all | solution.py:60
Sparse Core Ops, SparseCore 0:
  106.4 67.8 all-gather.2
where the time goes:
time: 233 us; the launch traced here: 232 us
  waiting for transfers between devices  110 us (47%)
  blocking collectives  44.3 us (19%)
  starting transfers between devices  34.4 us (15%)
  between operations  14.3 us (6%)
  local copies, waits for them, and re-layouts  13.5 us (6%)
  matrix products  11.4 us (5%)
  other arithmetic  4.07 us (2%)
    all_gather x1, waiting for transfers between devices, local(): lax.all_gather(expert_hidden, 'group', axis=0, tiled=True)  68 us
    unnamed x1, blocking collectives  44.3 us
    all_to_all x1, waiting for transfers between devices, local(): lax.all_to_all(outputs.reshape(experts, CAP, slice_width), 'expert', spli...  22.6 us
    all_to_all x1, starting transfers between devices, local(): lax.all_to_all(outputs.reshape(experts, CAP, slice_width), 'expert', spli...  20 us
    all_to_all x1, waiting for transfers between devices, local(): lax.all_to_all(outgoing, 'expert', split_axis=0, concat_axis=0, tiled=True)  18.9 us
    all_to_all x1, starting transfers between devices, local(): lax.all_to_all(outgoing, 'expert', split_axis=0, concat_axis=0, tiled=True)  11.2 us
    unnamed x28, local copies, waits for them, and re-layouts  7.42 us
  transfers between devices with their start and end apart: 5, of which 4 were waited for; matrix products, arithmetic and copies ran while one was open for 2% of the time, Pallas kernels for 0%

commit v1 on v0

v1 whole, which is shorter than its diff:
```python
import jax
import jax.numpy as jnp
from jax import lax
from jax.experimental import pallas as pl
from jax.experimental.pallas import tpu as pltpu
from jax.sharding import PartitionSpec as P

CAP = 18
HALF = 9
EXPERTS = 32
DEPTH = 8
PAIR = 2
WIDTH = 448
PADDED = 512
MAIN = EXPERTS * 8
ROWS = EXPERTS * HALF
F32 = jnp.float32
BF16 = jnp.bfloat16
NT = (((1,), (1,)), ((), ()))
TN = (((0,), (0,)), ((), ()))
VMEM_BYTES = 48 * 1024 * 1024


def row_of_eight(shape):
    return lax.broadcasted_iota(jnp.int32, shape, 0) & 7


def spread(count):
    row = lax.broadcasted_iota(jnp.int32, (8 * count, count), 0)
    column = lax.broadcasted_iota(jnp.int32, (8 * count, count), 1)
    return ((row >> 3) == column).astype(BF16)


def pack(main, last):
    row = row_of_eight((MAIN, 128))
    lane = lax.broadcasted_iota(jnp.int32, (MAIN, 128), 1)
    even = jnp.zeros((MAIN, 128), F32)
    odd = jnp.zeros((MAIN, 128), F32)
    for tile in range(4):
        piece = last[:, 128 * tile : 128 * tile + 128]
        even = jnp.where(row == 2 * tile, piece, even)
        odd = jnp.where(row == 2 * tile + 1, piece, odd)
    runs = odd + pltpu.roll(even, 64, 1)
    tail = jnp.where(lane < 64, main[:, 384:512], runs)
    tiles = [main[:, 128 * tile : 128 * tile + 128] for tile in range(3)] + [tail]
    return jnp.concatenate([t.reshape(EXPERTS, 8, 128) for t in tiles], axis=1).astype(BF16)


def unpack(block):
    wide = block.astype(F32)
    tiles = [wide[:, 8 * tile : 8 * tile + 8, :].reshape(MAIN, 128) for tile in range(4)]
    row = row_of_eight((MAIN, 128))
    lane = lax.broadcasted_iota(jnp.int32, (MAIN, 128), 1)
    tail = tiles[3]
    main = jnp.concatenate(tiles[:3] + [jnp.where(lane < 64, tail, 0.0)], axis=1).astype(BF16)
    turned = pltpu.roll(tail, 64, 1)
    runs = [
        jnp.where(
            (row == 2 * tile) & (lane < 64),
            turned,
            jnp.where((row == 2 * tile + 1) & (lane >= 64), tail, 0.0),
        )
        for tile in range(4)
    ]
    runs = jnp.concatenate(runs, axis=1).astype(BF16)
    last = lax.dot_general(spread(EXPERTS), runs, TN, preferred_element_type=F32).astype(BF16)
    return jnp.concatenate([main, last], axis=0)


def eightfold(x):
    return jnp.broadcast_to(x[:, None, :], (x.shape[0], 8, x.shape[1])).reshape(8 * x.shape[0], x.shape[1])


def dispatch_kernel(ids_ref, tokens_ref, send_ref, slot_ref):
    count = ids_ref.shape[1]
    label = lax.broadcasted_iota(jnp.int32, (EXPERTS, count), 0)
    chosen = jnp.zeros((EXPERTS, count), F32)
    for pick in range(ids_ref.shape[0]):
        chosen = jnp.where(ids_ref[pick : pick + 1, :] == label, 1.0, chosen)
    before = lax.broadcasted_iota(jnp.int32, (count, count), 0) < lax.broadcasted_iota(
        jnp.int32, (count, count), 1
    )
    earlier = jnp.dot(chosen.astype(BF16), before.astype(BF16), preferred_element_type=F32)
    slot = jnp.where(chosen > 0.0, earlier, -1.0)
    slot_ref[...] = slot
    every = eightfold(slot)
    place = row_of_eight(every.shape).astype(F32)
    tokens = jnp.concatenate(
        [tokens_ref[...], jnp.zeros((PADDED - WIDTH, count), BF16)], axis=0
    )
    for half in range(PAIR):
        main = (every == place + HALF * half).astype(BF16)
        last = (every == 1.0 * HALF * half + 8.0).astype(BF16)
        main = lax.dot_general(main, tokens, NT, preferred_element_type=F32)
        last = lax.dot_general(last, tokens, NT, preferred_element_type=F32)
        send_ref[EXPERTS * half : EXPERTS * half + EXPERTS] = pack(main, last)


def weights_kernel(ids_ref, combine_ref, slot_ref, high_ref, low_ref):
    slot = slot_ref[...]
    label = lax.broadcasted_iota(jnp.int32, slot.shape, 0)
    weight = jnp.zeros(slot.shape, F32)
    for pick in range(ids_ref.shape[0]):
        weight = jnp.where(
            ids_ref[pick : pick + 1, :] == label, combine_ref[pick : pick + 1, :], weight
        )
    every, each = eightfold(slot), eightfold(weight)
    place = row_of_eight(every.shape).astype(F32)
    for half in range(PAIR):
        main = jnp.where(every == place + HALF * half, each, 0.0)
        last = jnp.where(slot == 1.0 * HALF * half + 8.0, weight, 0.0)
        both = jnp.concatenate([main, last], axis=0)
        high = both.astype(BF16)
        high_ref[ROWS * half : ROWS * half + ROWS] = high
        low_ref[ROWS * half : ROWS * half + ROWS] = (both - high.astype(F32)).astype(BF16)


def gate_up_kernel(side_ref, arrived_ref, own_ref, other_ref, terms_ref, own_rows, other_rows):
    @pl.when(pl.program_id(0) == 0)
    def _():
        side = side_ref[0]
        own_rows[...] = unpack(arrived_ref[pl.ds(side * EXPERTS, EXPERTS)])
        other_rows[...] = unpack(arrived_ref[pl.ds((1 - side) * EXPERTS, EXPERTS)])

    own = jnp.concatenate([own_ref[0], own_ref[1]], axis=1)
    other = jnp.concatenate([other_ref[0], other_ref[1]], axis=1)
    terms = jnp.dot(own_rows[:, :WIDTH], own, preferred_element_type=F32)
    terms += jnp.dot(other_rows[:, :WIDTH], other, preferred_element_type=F32)
    terms_ref[0] = terms.astype(BF16)


def hidden_kernel(terms_ref, hidden_ref):
    both = terms_ref[0].astype(F32)
    for piece in range(1, DEPTH):
        both += terms_ref[piece].astype(F32)
    width = both.shape[1] // 2
    gate, up = both[:, :width], both[:, width:]
    hidden = (gate / (1.0 + jnp.exp(-gate)) * up).astype(BF16)
    for piece in range(DEPTH):
        hidden_ref[piece] = hidden


def down_kernel(side_ref, hidden_ref, own_ref, other_ref, send_ref):
    side = side_ref[0]
    hidden = jnp.concatenate([hidden_ref[piece] for piece in range(DEPTH)], axis=1)
    for ref, where in ((own_ref, side), (other_ref, 1 - side)):
        down = jnp.concatenate(
            [ref[...], jnp.zeros((PADDED - WIDTH, ref.shape[1]), BF16)], axis=0
        )
        result = lax.dot_general(hidden, down, NT, preferred_element_type=F32).astype(BF16)
        last = jnp.dot(spread(EXPERTS), result[MAIN:], preferred_element_type=F32)
        send_ref[pl.ds(where * EXPERTS, EXPERTS)] = pack(result[:MAIN].astype(F32), last)


def combine_kernel(back_ref, high_ref, low_ref, out_ref):
    rows = jnp.concatenate([unpack(back_ref[:EXPERTS]), unpack(back_ref[EXPERTS:])], axis=0)
    routed = lax.dot_general(rows, high_ref[...], TN, preferred_element_type=F32)
    routed += lax.dot_general(rows, low_ref[...], TN, preferred_element_type=F32)
    out_ref[...] = routed[:WIDTH].astype(BF16)


def call(kernel, out, **more):
    return pl.pallas_call(
        kernel,
        out_shape=out,
        compiler_params=pltpu.CompilerParams(vmem_limit_bytes=VMEM_BYTES),
        **more,
    )


def local(tokens, expert_ids, combine, w_in, w_down):
    count = tokens.shape[0]
    hidden_units = w_down.shape[1]
    block = hidden_units // DEPTH
    group = lax.axis_index("group")
    side = (group // DEPTH).astype(jnp.int32).reshape(1)
    swap = [(g, (g + DEPTH) % (PAIR * DEPTH)) for g in range(PAIR * DEPTH)]
    along_z = [[x * DEPTH + z for z in range(DEPTH)] for x in range(PAIR)]
    along_pair = [
        [(x * DEPTH + z) * EXPERTS + e for x in range(PAIR) for e in range(EXPERTS)]
        for z in range(DEPTH)
    ]
    tokens, ids, combine = tokens.T, expert_ids.T, combine.T
    w_in = jnp.swapaxes(w_in[0], 1, 2)
    w_down = w_down[0].T
    scalar = pl.BlockSpec(memory_space=pltpu.SMEM)
    whole = pl.BlockSpec(memory_space=pltpu.VMEM)

    other_in = lax.ppermute(w_in, "group", swap)
    packed = (PAIR * EXPERTS, EXPERTS, 128)
    send, slot = call(
        dispatch_kernel,
        (jax.ShapeDtypeStruct(packed, BF16), jax.ShapeDtypeStruct((EXPERTS, count), F32)),
    )(ids, tokens)
    arrived = lax.all_to_all(
        send, ("group", "expert"), 0, 0, axis_index_groups=along_pair, tiled=True
    )
    high, low = call(
        weights_kernel, (jax.ShapeDtypeStruct((PAIR * ROWS, count), BF16),) * 2
    )(ids, combine, slot)
    w_down_sent, arrived = lax.optimization_barrier((w_down, arrived))
    other_down = lax.ppermute(w_down_sent, "group", swap)

    weight_spec = pl.BlockSpec((2, WIDTH, block), lambda z: (0, 0, z))
    terms = call(
        gate_up_kernel,
        jax.ShapeDtypeStruct((DEPTH, ROWS, 2 * block), BF16),
        grid=(DEPTH,),
        in_specs=[scalar, whole, weight_spec, weight_spec],
        out_specs=pl.BlockSpec((1, ROWS, 2 * block), lambda z: (z, 0, 0)),
        scratch_shapes=[pltpu.VMEM((ROWS, PADDED), BF16)] * 2,
    )(side, arrived, w_in, other_in)
    terms = lax.all_to_all(terms, "group", 0, 0, axis_index_groups=along_z, tiled=True)
    hidden = call(hidden_kernel, jax.ShapeDtypeStruct((DEPTH, ROWS, block), BF16))(terms)
    hidden = lax.all_to_all(hidden, "group", 0, 0, axis_index_groups=along_z, tiled=True)
    send = call(
        down_kernel,
        jax.ShapeDtypeStruct(packed, BF16),
        in_specs=[scalar, whole, whole, whole],
    )(side, hidden, w_down, other_down)
    back = lax.all_to_all(
        send, ("group", "expert"), 0, 0, axis_index_groups=along_pair, tiled=True
    )
    routed = call(combine_kernel, jax.ShapeDtypeStruct((WIDTH, count), BF16))(back, high, low)
    return routed.T


def solution(mesh):
    placed = (
        P("expert", "group"),
        P("expert", None),
        P("expert", None),
        P("expert", None, None, "group"),
        P("expert", None, "group"),
    )
    return jax.shard_map(
        local, mesh=mesh, in_specs=placed, out_specs=P("expert", "group"), check_vma=False
    )
```

time: 233 us -> 158 us (0.68)
  waiting for transfers between devices: 110 us -> 70.9 us
  between operations: 14.3 us -> 0.13 us
  matrix products: 11.4 us -> 0 us
  Pallas kernels: 0 us -> 11.4 us
  local copies, waits for them, and re-layouts: 13.5 us -> 3.19 us
  other arithmetic: 4.07 us -> 0 us
  blocking collectives: 44.3 us -> 40.4 us
  starting transfers between devices: 34.4 us -> 30.7 us
    all_gather x1 -> x0, waiting for transfers between devices: 68 us -> none  [local(): lax.all_gather(expert_hidden, 'group', axis=0, tiled=True)]
    unnamed x1 -> x0, blocking collectives: 44.3 us -> none
    all_to_all x0 -> x1, blocking collectives: none -> 40.4 us  [local(): lax.all_to_all(terms, 'group', 0, 0, axis_index_groups=along_z, tiled=True)]
    ppermute x0 -> x2, waiting for transfers between devices: none -> 19.9 us  [the longest x1 19.9 us: local(): other_down = lax.ppermute(w_down_sent, 'group', swap)]
    dot_general x4 -> x0, matrix products: 11.4 us -> none  [the longest x1 4.21 us: local(): jnp.dot(weighting, flat_back, precision=lax.Precision.HIGHEST, preferred_...]
    pallas_call x0 -> x6, Pallas kernels: none -> 11.4 us  [the longest x1 4.1 us: local(): call(gate_up_kernel, jax.ShapeDtypeStruct((DEPTH, ROWS, 2 * block), BF16)...]
    all_to_all x2 -> x3, waiting for transfers between devices: 41.4 us -> 51 us  [the longest x2 51 us: local(): lax.all_to_all(send, ('group', 'expert'), 0, 0, axis_index_groups=along_p...]
    all_to_all x2 -> x3, starting transfers between devices: 31.2 us -> 24.9 us  [the longest x2 21.3 us: local(): lax.all_to_all(send, ('group', 'expert'), 0, 0, axis_index_groups=along_p...]
  transfers between devices with their start and end apart: 5 -> 5, of which waited for: 4 -> 3; matrix products, arithmetic and copies ran while one was open for 2% -> 0% of each run, Pallas kernels for 0% -> 1%
where the time goes in v1:
time: 158 us; the launch traced here: 157 us
  waiting for transfers between devices  70.9 us (45%)
  blocking collectives  40.4 us (26%)
  starting transfers between devices  30.7 us (19%)
  Pallas kernels  11.4 us (7%)
  local copies, waits for them, and re-layouts  3.19 us (2%)
    all_to_all x2, waiting for transfers between devices, local(): lax.all_to_all(send, ('group', 'expert'), 0, 0, axis_index_groups=along_p...  51 us
    all_to_all x1, blocking collectives, local(): lax.all_to_all(terms, 'group', 0, 0, axis_index_groups=along_z, tiled=True)  40.4 us
    all_to_all x2, starting transfers between devices, local(): lax.all_to_all(send, ('group', 'expert'), 0, 0, axis_index_groups=along_p...  21.3 us
    ppermute x1, waiting for transfers between devices, local(): other_down = lax.ppermute(w_down_sent, 'group', swap)  19.9 us
    pallas_call x1, Pallas kernels, local(): call(gate_up_kernel, jax.ShapeDtypeStruct((DEPTH, ROWS, 2 * block), BF16)...  4.1 us
    ppermute x1, starting transfers between devices, local(): other_in = lax.ppermute(w_in, 'group', swap)  3.94 us
    all_to_all x1, starting transfers between devices, local(): lax.all_to_all(hidden, 'group', 0, 0, axis_index_groups=along_z, tiled=True)  3.54 us
    unnamed x12, local copies, waits for them, and re-layouts  3.19 us
  transfers between devices with their start and end apart: 5, of which 3 were waited for; matrix products, arithmetic and copies ran while one was open for 0% of the time, Pallas kernels for 1%

profile of v1, /device:TPU:1, one launch (start us, length us, event | category | flops | bytes accessed | tf_op | source)
XLA Modules:
  0.0 156.8 jit_solution(7270861007140185115)
XLA Ops:
  0.0 3.9 %collective-permute-start = (bf16[2,448,1024]{2,1,0:T(8,128)(2,1)}, bf16[2,448,1024]{2,1,0:T(8,128)(2,1)S(1)}, u32[]{:S(2)}, u32[]{:S(2)}) collective-permute-start(bf16[2,448,1024]{2,1,0:T(8,128)(2,1)} %bitcast.11), channel_id=1, source_target_pairs={{0,256},{32,288},{64,320},{96,352},{128,384},{160,416},{192,448},{... | collective-permute-start | bytes 5505032 | tf_op jit(solution)/shard_map/ppermute | solution.py:189
  3.9 0.0 copy-start.2
  4.0 1.0 copy-done.2
  4.9 0.0 copy-start.3
  4.9 0.7 copy-done.3
  5.6 1.8 %shard_map.55 = (bf16[64,32,128]{2,1,0:T(8,128)(2,1)}, f32[32,384]{1,0:T(8,128)S(1)}) custom-call(s32[8,384]{1,0:T(8,128)S(1)} %bitcast.16, bf16[448,384]{1,0:T(8,128)(2,1)S(1)} %bitcast.15), custom_call_target="tpu_custom_call" | custom-call | tf_op jit(solution)/shard_map/pallas_call | solution.py:191
  7.4 10.8 %all-to-all-start = ((bf16[64,32,128]{2,1,0:T(8,128)(2,1)}), bf16[64,32,128]{2,1,0:T(8,128)(2,1)S(1)}, u32[]{:S(2)}, u32[]{:S(2)}) async-start(bf16[64,32,128]{2,1,0:T(8,128)(2,1)} %get-tuple-element.11), calls=%async_computation | async-start | bytes 1048576 | tf_op jit(solution)/shard_map/all_to_all | solution.py:195
  18.2 34.4 %all-to-all-done.arrived_ref = bf16[64,32,128]{2,1,0:T(8,128)(2,1)S(1)} async-done(((bf16[64,32,128]{2,1,0:T(8,128)(2,1)}), bf16[64,32,128]{2,1,0:T(8,128)(2,1)S(1)}, u32[]{:S(2)}, u32[]{:S(2)}) %all-to-all-start) | async-done | bytes 524320 | tf_op jit(solution)/shard_map/all_to_all | solution.py:195
  52.6 0.0 collective-permute-done.other_ref
  52.6 0.0 copy-start
  52.6 1.5 copy-done
  54.1 4.1 %shard_map.56 = bf16[8,288,256]{2,1,0:T(8,128)(2,1)S(1)} custom-call(s32[1]{0:T(128)} %bitcast.side_ref, bf16[64,32,128]{2,1,0:T(8,128)(2,1)S(1)} %all-to-all-done.arrived_ref, bf16[2,448,1024]{2,1,0:T(8,128)(2,1)S(1)} %bitcast.12, bf16[2,448,1024]{2,1,0:T(8,128)(2,1)S(1)} %collective-permute-done.other_ref), custom_call_target="tpu_custom_call" | custom-call | tf_op jit(solution)/shard_map/pallas_call | solution.py:205
  58.2 40.4 %all_to_all.20.terms_ref = bf16[8,288,256]{2,1,0:T(8,128)(2,1)S(1)} all-to-all(bf16[8,288,256]{2,1,0:T(8,128)(2,1)S(1)} %shard_map.56), channel_id=1, replica_groups={{0,32,64,96,128,160,192,224},{256,288,320,352,384,416,448,480},{1,33,65..., dimensions={0} | all-to-all | bytes 2359296 | tf_op jit(solution)/shard_map/all_to_all | solution.py:213
  98.6 0.0 copy-start.1
  98.6 1.0 shard_map.57
  99.6 3.5 %all-to-all-start.2 = ((bf16[8,288,128]{2,1,0:T(8,128)(2,1)}), bf16[8,288,128]{2,1,0:T(8,128)(2,1)S(1)}, u32[]{:S(2)}, u32[]{:S(2)}) async-start(bf16[8,288,128]{2,1,0:T(8,128)(2,1)} %shard_map.57), calls=%async_computation.2 | async-start | bytes 1179648 | tf_op jit(solution)/shard_map/all_to_all | solution.py:215
  103.2 0.0 copy-done.1
  103.2 0.0 copy-start.4
  103.2 0.0 copy-start.5
  103.2 1.9 %collective-permute-start.1 = (bf16[448,1024]{1,0:T(8,128)(2,1)S(1)}, bf16[448,1024]{1,0:T(8,128)(2,1)S(1)}, u32[]{:S(2)}, u32[]{:S(2)}) collective-permute-start(bf16[448,1024]{1,0:T(8,128)(2,1)S(1)} %bitcast.13), channel_id=1, source_target_pairs={{0,256},{32,288},{64,320},{96,352},{128,384},{160,416},{192,448},{... | collective-permute-start | bytes 2752520 | tf_op jit(solution)/shard_map/ppermute | solution.py:202
  105.1 19.9 %collective-permute-done.1.other_ref = bf16[448,1024]{1,0:T(8,128)(2,1)S(1)} collective-permute-done((bf16[448,1024]{1,0:T(8,128)(2,1)S(1)}, bf16[448,1024]{1,0:T(8,128)(2,1)S(1)}, u32[]{:S(2)}, u32[]{:S(2)}) %collective-permute-start.1) | collective-permute-done | bytes 917536 | tf_op jit(solution)/shard_map/ppermute | solution.py:202
  125.1 0.0 all-to-all-done.2.hidden_ref
  125.1 2.1 %shard_map.58 = bf16[64,32,128]{2,1,0:T(8,128)(2,1)} custom-call(s32[1]{0:T(128)} %bitcast.side_ref, bf16[8,288,128]{2,1,0:T(8,128)(2,1)S(1)} %all-to-all-done.2.hidden_ref, bf16[448,1024]{1,0:T(8,128)(2,1)S(1)} %bitcast.14, bf16[448,1024]{1,0:T(8,128)(2,1)S(1)} %collective-permute-done.1.other_ref), custom_call_target="tpu_custom_call" | custom-call | tf_op jit(solution)/shard_map/pallas_call | solution.py:216
  127.1 10.6 %all-to-all-start.3 = ((bf16[64,32,128]{2,1,0:T(8,128)(2,1)}), bf16[64,32,128]{2,1,0:T(8,128)(2,1)S(1)}, u32[]{:S(2)}, u32[]{:S(2)}) async-start(bf16[64,32,128]{2,1,0:T(8,128)(2,1)} %shard_map.58), calls=%async_computation.3 | async-start | bytes 1048576 | tf_op jit(solution)/shard_map/all_to_all | solution.py:221
  137.7 0.0 copy-done.4
  137.7 0.0 copy-done.5
  137.7 0.3 shard_map.59
  138.1 16.6 %all-to-all-done.3.back_ref = bf16[64,32,128]{2,1,0:T(8,128)(2,1)S(1)} async-done(((bf16[64,32,128]{2,1,0:T(8,128)(2,1)}), bf16[64,32,128]{2,1,0:T(8,128)(2,1)S(1)}, u32[]{:S(2)}, u32[]{:S(2)}) %all-to-all-start.3) | async-done | bytes 524320 | tf_op jit(solution)/shard_map/all_to_all | solution.py:221
  154.6 2.2 %shard_map.60 = bf16[448,384]{1,0:T(8,128)(2,1)} custom-call(bf16[64,32,128]{2,1,0:T(8,128)(2,1)S(1)} %all-to-all-done.3.back_ref, bf16[576,384]{1,0:T(8,128)(2,1)S(1)} %get-tuple-element.15.high_ref, bf16[576,384]{1,0:T(8,128)(2,1)S(1)} %get-tuple-element.16.low_ref), custom_call_target="tpu_custom_call" | custom-call | tf_op jit(solution)/shard_map/pallas_call | solution.py:224
Async XLA Ops:
  0.0 52.6 %collective-permute-start = (bf16[2,448,1024]{2,1,0:T(8,128)(2,1)}, bf16[2,448,1024]{2,1,0:T(8,128)(2,1)S(1)}, u32[]{:S(2)}, u32[]{:S(2)}) collective-permute-start(bf16[2,448,1024]{2,1,0:T(8,128)(2,1)} %bitcast.11), channel_id=1, source_target_pairs={{0,256},{32,288},{64,320},{96,352},{128,384},{160,416},{192,448},{... | collective-permute-start | bytes 5505032 | tf_op jit(solution)/shard_map/ppermute | solution.py:189
  3.9 1.0 copy-start.2
  4.9 0.7 copy-start.3
  7.4 45.2 %all-to-all-start = ((bf16[64,32,128]{2,1,0:T(8,128)(2,1)}), bf16[64,32,128]{2,1,0:T(8,128)(2,1)S(1)}, u32[]{:S(2)}, u32[]{:S(2)}) async-start(bf16[64,32,128]{2,1,0:T(8,128)(2,1)} %get-tuple-element.11), calls=%async_computation | async-start | bytes 1048576 | tf_op jit(solution)/shard_map/all_to_all | solution.py:195
  52.6 1.5 copy-start
  98.6 4.6 %copy-start.1 = (bf16[1,1024,448]{1,2,0:T(8,128)(2,1)S(1)}, bf16[1,1024,448]{1,2,0:T(8,128)(2,1)}, u32[]{:S(2)}) copy-start(bf16[1,1024,448]{1,2,0:T(8,128)(2,1)} %param.9) | copy-start | bytes 2752516
  99.6 25.4 %all-to-all-start.2 = ((bf16[8,288,128]{2,1,0:T(8,128)(2,1)}), bf16[8,288,128]{2,1,0:T(8,128)(2,1)S(1)}, u32[]{:S(2)}, u32[]{:S(2)}) async-start(bf16[8,288,128]{2,1,0:T(8,128)(2,1)} %shard_map.57), calls=%async_computation.2 | async-start | bytes 1179648 | tf_op jit(solution)/shard_map/all_to_all | solution.py:215
  103.2 34.5 %copy-start.4 = (s32[384,8]{0,1:T(8,128)S(1)}, s32[384,8]{0,1:T(8,128)}, u32[]{:S(2)}) copy-start(s32[384,8]{0,1:T(8,128)} %param.6) | copy-start | bytes 36868
  103.2 34.5 %copy-start.5 = (f32[384,8]{0,1:T(8,128)S(1)}, f32[384,8]{0,1:T(8,128)}, u32[]{:S(2)}) copy-start(f32[384,8]{0,1:T(8,128)} %param.7) | copy-start | bytes 36868
  103.2 21.8 %collective-permute-start.1 = (bf16[448,1024]{1,0:T(8,128)(2,1)S(1)}, bf16[448,1024]{1,0:T(8,128)(2,1)S(1)}, u32[]{:S(2)}, u32[]{:S(2)}) collective-permute-start(bf16[448,1024]{1,0:T(8,128)(2,1)S(1)} %bitcast.13), channel_id=1, source_target_pairs={{0,256},{32,288},{64,320},{96,352},{128,384},{160,416},{192,448},{... | collective-permute-start | bytes 2752520 | tf_op jit(solution)/shard_map/ppermute | solution.py:202
  127.1 27.5 %all-to-all-start.3 = ((bf16[64,32,128]{2,1,0:T(8,128)(2,1)}), bf16[64,32,128]{2,1,0:T(8,128)(2,1)S(1)}, u32[]{:S(2)}, u32[]{:S(2)}) async-start(bf16[64,32,128]{2,1,0:T(8,128)(2,1)} %shard_map.58), calls=%async_computation.3 | async-start | bytes 1048576 | tf_op jit(solution)/shard_map/all_to_all | solution.py:221

commit v2 on v1

--- a/solution.py
+++ b/solution.py
@@ -46,7 +46,7 @@
     return jnp.concatenate([t.reshape(EXPERTS, 8, 128) for t in tiles], axis=1).astype(BF16)
 
 
-def unpack(block):
+def opened(block):
     wide = block.astype(F32)
     tiles = [wide[:, 8 * tile : 8 * tile + 8, :].reshape(MAIN, 128) for tile in range(4)]
     row = row_of_eight((MAIN, 128))
@@ -62,7 +62,11 @@
         )
         for tile in range(4)
     ]
-    runs = jnp.concatenate(runs, axis=1).astype(BF16)
+    return main, jnp.concatenate(runs, axis=1).astype(BF16)
+
+
+def unpack(block):
+    main, runs = opened(block)
     last = lax.dot_general(spread(EXPERTS), runs, TN, preferred_element_type=F32).astype(BF16)
     return jnp.concatenate([main, last], axis=0)
 
@@ -93,7 +97,7 @@
         last = (every == 1.0 * HALF * half + 8.0).astype(BF16)
         main = lax.dot_general(main, tokens, NT, preferred_element_type=F32)
         last = lax.dot_general(last, tokens, NT, preferred_element_type=F32)
-        send_ref[EXPERTS * half : EXPERTS * half + EXPERTS] = pack(main, last)
+        send_ref[:, 32 * half : 32 * half + 32, :] = pack(main, last)
 
 
 def weights_kernel(ids_ref, combine_ref, slot_ref, high_ref, low_ref):
@@ -115,34 +119,85 @@
         low_ref[ROWS * half : ROWS * half + ROWS] = (both - high.astype(F32)).astype(BF16)
 
 
-def gate_up_kernel(side_ref, arrived_ref, own_ref, other_ref, terms_ref, own_rows, other_rows):
-    @pl.when(pl.program_id(0) == 0)
-    def _():
-        side = side_ref[0]
-        own_rows[...] = unpack(arrived_ref[pl.ds(side * EXPERTS, EXPERTS)])
-        other_rows[...] = unpack(arrived_ref[pl.ds((1 - side) * EXPERTS, EXPERTS)])
-
-    own = jnp.concatenate([own_ref[0], own_ref[1]], axis=1)
-    other = jnp.concatenate([other_ref[0], other_ref[1]], axis=1)
-    terms = jnp.dot(own_rows[:, :WIDTH], own, preferred_element_type=F32)
-    terms += jnp.dot(other_rows[:, :WIDTH], other, preferred_element_type=F32)
-    terms_ref[0] = terms.astype(BF16)
-
-
-def hidden_kernel(terms_ref, hidden_ref):
-    both = terms_ref[0].astype(F32)
-    for piece in range(1, DEPTH):
-        both += terms_ref[piece].astype(F32)
-    width = both.shape[1] // 2
-    gate, up = both[:, :width], both[:, width:]
+def ordered(count, blocks, column, last):
+    per = count // blocks
+    mains = per * 8 // 9
+    row = lax.broadcasted_iota(jnp.int32, (count, MAIN), 0)
+    block = lax.div(row, per)
+    inside = row - block * per
+    if last:
+        chosen = (inside >= mains) & ((column >> 3) == block * (per - mains) + inside - mains)
+    else:
+        chosen = (inside < mains) & (column == block * mains + inside)
+    return chosen.astype(BF16)
+
+
+def gate_up_kernel(side_ref, arrived_ref, w_ref, terms_ref):
+    side = side_ref[0]
+    column = lax.broadcasted_iota(jnp.int32, (ROWS, MAIN), 1)
+    take_main = ordered(ROWS, DEPTH, column, False)
+    take_last = ordered(ROWS, DEPTH, column, True)
+    rows = []
+    for place in range(PAIR):
+        half = side if place == 0 else 1 - side
+        main, runs = opened(arrived_ref[:, pl.ds(half * 32, 32), :])
+        taken = jnp.dot(take_main, main, preferred_element_type=F32)
+        taken += jnp.dot(take_last, runs, preferred_element_type=F32)
+        rows.append(taken.astype(BF16))
+    rows = jnp.concatenate(rows, axis=0)[:, :WIDTH]
+    units = w_ref.shape[2]
+    for index in range(2):
+        for start in range(0, units, PADDED):
+            part = jnp.dot(rows, w_ref[index, :, start : start + PADDED], preferred_element_type=F32)
+            part = part.astype(BF16)
+            for place in range(PAIR):
+                at = (2 * place + index) * units + start
+                terms_ref[:, at : at + PADDED] = part[ROWS * place : ROWS * place + ROWS]
+
+
+def hidden_kernel(kept_ref, came_ref, hidden_ref):
+    units = came_ref.shape[1] // 2
+    count = came_ref.shape[0]
+    mains = count * 8 // 9
+    both = kept_ref[:, : 2 * units].astype(F32) + came_ref[...].astype(F32)
+    gate, up = both[:, :units], both[:, units:]
     hidden = (gate / (1.0 + jnp.exp(-gate)) * up).astype(BF16)
+    lasts = count - mains
+    row = lax.broadcasted_iota(jnp.int32, (mains, count), 0)
+    column = lax.broadcasted_iota(jnp.int32, (mains, count), 1)
+    pick = (column == mains + lax.rem(row, lasts)).astype(BF16)
+    again = jnp.dot(pick, hidden, preferred_element_type=F32)
+    run = lax.div(lax.broadcasted_iota(jnp.int32, (mains, 128), 0), lasts)
+    extra = jnp.zeros((mains, 128), F32)
+    for tile in range(units // 128):
+        extra = jnp.where(run == tile, again[:, 128 * tile : 128 * tile + 128], extra)
+    block = jnp.concatenate([hidden[:mains], extra.astype(BF16)], axis=1)
     for piece in range(DEPTH):
-        hidden_ref[piece] = hidden
+        hidden_ref[piece] = block
+
+
+def gathered_hidden(hidden_ref):
+    mains = hidden_ref.shape[1]
+    units = hidden_ref.shape[2] - 128
+    lasts = EXPERTS // DEPTH
+    main = jnp.concatenate([hidden_ref[piece, :, :units] for piece in range(DEPTH)], axis=0)
+    extra = jnp.concatenate([hidden_ref[piece, :, units:] for piece in range(DEPTH)], axis=0)
+    row = lax.broadcasted_iota(jnp.int32, extra.shape, 0)
+    run = lax.div(lax.rem(row, mains), lasts)
+    wide = extra.astype(F32)
+    runs = jnp.concatenate(
+        [jnp.where(run == tile, wide, 0.0) for tile in range(units // 128)], axis=1
+    ).astype(BF16)
+    source = lax.broadcasted_iota(jnp.int32, (EXPERTS, DEPTH * mains), 0)
+    column = lax.broadcasted_iota(jnp.int32, (EXPERTS, DEPTH * mains), 1)
+    pick = source == lax.div(column, mains) * lasts + lax.rem(column, lasts)
+    last = jnp.dot(pick.astype(BF16), runs, preferred_element_type=F32).astype(BF16)
+    return jnp.concatenate([main, last], axis=0)
 
 
 def down_kernel(side_ref, hidden_ref, own_ref, other_ref, send_ref):
     side = side_ref[0]
-    hidden = jnp.concatenate([hidden_ref[piece] for piece in range(DEPTH)], axis=1)
+    hidden = gathered_hidden(hidden_ref)
     for ref, where in ((own_ref, side), (other_ref, 1 - side)):
         down = jnp.concatenate(
             [ref[...], jnp.zeros((PADDED - WIDTH, ref.shape[1]), BF16)], axis=0
@@ -171,7 +226,6 @@
 def local(tokens, expert_ids, combine, w_in, w_down):
     count = tokens.shape[0]
     hidden_units = w_down.shape[1]
-    block = hidden_units // DEPTH
     group = lax.axis_index("group")
     side = (group // DEPTH).astype(jnp.int32).reshape(1)
     swap = [(g, (g + DEPTH) % (PAIR * DEPTH)) for g in range(PAIR * DEPTH)]
@@ -186,36 +240,37 @@
     scalar = pl.BlockSpec(memory_space=pltpu.SMEM)
     whole = pl.BlockSpec(memory_space=pltpu.VMEM)
 
-    other_in = lax.ppermute(w_in, "group", swap)
-    packed = (PAIR * EXPERTS, EXPERTS, 128)
     send, slot = call(
         dispatch_kernel,
-        (jax.ShapeDtypeStruct(packed, BF16), jax.ShapeDtypeStruct((EXPERTS, count), F32)),
+        (
+            jax.ShapeDtypeStruct((EXPERTS, 64, 128), BF16),
+            jax.ShapeDtypeStruct((EXPERTS, count), F32),
+        ),
     )(ids, tokens)
-    arrived = lax.all_to_all(
-        send, ("group", "expert"), 0, 0, axis_index_groups=along_pair, tiled=True
-    )
+    arrived = lax.all_to_all(send, "expert", 0, 0, tiled=True)
     high, low = call(
         weights_kernel, (jax.ShapeDtypeStruct((PAIR * ROWS, count), BF16),) * 2
     )(ids, combine, slot)
     w_down_sent, arrived = lax.optimization_barrier((w_down, arrived))
     other_down = lax.ppermute(w_down_sent, "group", swap)
-
-    weight_spec = pl.BlockSpec((2, WIDTH, block), lambda z: (0, 0, z))
     terms = call(
         gate_up_kernel,
-        jax.ShapeDtypeStruct((DEPTH, ROWS, 2 * block), BF16),
-        grid=(DEPTH,),
-        in_specs=[scalar, whole, weight_spec, weight_spec],
-        out_specs=pl.BlockSpec((1, ROWS, 2 * block), lambda z: (z, 0, 0)),
-        scratch_shapes=[pltpu.VMEM((ROWS, PADDED), BF16)] * 2,
-    )(side, arrived, w_in, other_in)
-    terms = lax.all_to_all(terms, "group", 0, 0, axis_index_groups=along_z, tiled=True)
-    hidden = call(hidden_kernel, jax.ShapeDtypeStruct((DEPTH, ROWS, block), BF16))(terms)
+        jax.ShapeDtypeStruct((ROWS, PAIR * 2 * hidden_units), BF16),
+        in_specs=[scalar, whole, whole],
+    )(side, arrived, w_in)
+    terms = lax.psum_scatter(
+        terms, "group", scatter_dimension=0, axis_index_groups=along_z, tiled=True
+    )
+    terms, other_down = lax.optimization_barrier((terms, other_down))
+    came = lax.ppermute(terms[:, 2 * hidden_units :], "group", swap)
+    mains = EXPERTS // DEPTH * 8
+    hidden = call(
+        hidden_kernel, jax.ShapeDtypeStruct((DEPTH, mains, hidden_units + 128), BF16)
+    )(terms, came)
     hidden = lax.all_to_all(hidden, "group", 0, 0, axis_index_groups=along_z, tiled=True)
     send = call(
         down_kernel,
-        jax.ShapeDtypeStruct(packed, BF16),
+        jax.ShapeDtypeStruct((PAIR * EXPERTS, 32, 128), BF16),
         in_specs=[scalar, whole, whole, whole],
     )(side, hidden, w_down, other_down)
     back = lax.all_to_all(

time: 158 us -> 144 us (0.911)
  waiting for transfers between devices: 70.9 us -> 37.8 us
  blocking collectives: 40.4 us -> 55.6 us
  starting transfers between devices: 30.7 us -> 34 us
  local copies, waits for them, and re-layouts: 3.19 us -> 5.2 us
    unnamed x0 -> x1, blocking collectives: none -> 38.3 us
    all_to_all x2 -> x1, waiting for transfers between devices: 51 us -> 16.6 us  [local(): lax.all_to_all(send, ('group', 'expert'), 0, 0, axis_index_groups=along_p...]
    all_to_all x1, blocking collectives: 40.4 us -> 17.3 us  [local(): lax.all_to_all(hidden, 'group', 0, 0, axis_index_groups=along_z, tiled=True)]
    ppermute x1, waiting for transfers between devices: 19.9 us -> 0.01 us  [local(): other_down = lax.ppermute(w_down_sent, 'group', swap)]
    all_to_all x1, waiting for transfers between devices: 0.01 us -> 17 us  [local(): arrived = lax.all_to_all(send, 'expert', 0, 0, tiled=True)]
    all_to_all x1, starting transfers between devices: 3.54 us -> 11.2 us  [local(): arrived = lax.all_to_all(send, 'expert', 0, 0, tiled=True)]
    all_to_all x2 -> x1, starting transfers between devices: 21.3 us -> 14.3 us  [local(): lax.all_to_all(send, ('group', 'expert'), 0, 0, axis_index_groups=along_p...]
    unnamed x0 -> x1, starting transfers between devices: none -> 3.2 us
  transfers between devices with their start and end apart: 5 -> 5, of which waited for: 3 -> 4; matrix products, arithmetic and copies ran while one was open for 0% -> 28% of each run, Pallas kernels for 1% -> 2%
where the time goes in v2:
time: 144 us; the launch traced here: 143 us
  blocking collectives  55.6 us (39%)
  waiting for transfers between devices  37.8 us (26%)
  starting transfers between devices  34 us (24%)
  Pallas kernels  9.83 us (7%)
  local copies, waits for them, and re-layouts  5.2 us (4%)
    unnamed x1, blocking collectives  38.3 us
    all_to_all x1, blocking collectives, local(): lax.all_to_all(hidden, 'group', 0, 0, axis_index_groups=along_z, tiled=True)  17.3 us
    all_to_all x1, waiting for transfers between devices, local(): arrived = lax.all_to_all(send, 'expert', 0, 0, tiled=True)  17 us
    all_to_all x1, waiting for transfers between devices, local(): lax.all_to_all(send, ('group', 'expert'), 0, 0, axis_index_groups=along_p...  16.6 us
    all_to_all x1, starting transfers between devices, local(): lax.all_to_all(send, ('group', 'expert'), 0, 0, axis_index_groups=along_p...  14.3 us
    all_to_all x1, starting transfers between devices, local(): arrived = lax.all_to_all(send, 'expert', 0, 0, tiled=True)  11.2 us
    unnamed x15, local copies, waits for them, and re-layouts  5.1 us
    pallas_call x1, Pallas kernels, local(): call(down_kernel, jax.ShapeDtypeStruct((PAIR * EXPERTS, 32, 128), BF16),...  3.36 us
  transfers between devices with their start and end apart: 5, of which 4 were waited for; matrix products, arithmetic and copies ran while one was open for 28% of the time, Pallas kernels for 2%

profile of v2, /device:TPU:1, one launch (start us, length us, event | category | flops | bytes accessed | tf_op | source)
XLA Modules:
  0.0 143.4 jit_solution(17811476798132127443)
XLA Ops:
  0.0 1.0 copy-done.2
  1.0 0.7 copy-done.3
  1.7 1.8 %shard_map.55 = (bf16[32,64,128]{2,1,0:T(8,128)(2,1)}, f32[32,384]{1,0:T(8,128)S(1)}) custom-call(s32[8,384]{1,0:T(8,128)S(1)} %bitcast.18, bf16[448,384]{1,0:T(8,128)(2,1)S(1)} %bitcast.17), custom_call_target="tpu_custom_call" | custom-call | tf_op jit(solution)/shard_map/pallas_call | solution.py:243
  3.5 11.2 %all-to-all-start = ((bf16[32,64,128]{2,1,0:T(8,128)(2,1)}), bf16[32,64,128]{2,1,0:T(8,128)(2,1)S(1)}, u32[]{:S(2)}, u32[]{:S(2)}) async-start(bf16[32,64,128]{2,1,0:T(8,128)(2,1)} %get-tuple-element.13), calls=%async_computation | async-start | bytes 1048576 | tf_op jit(solution)/shard_map/all_to_all | solution.py:250
  14.7 17.0 %all-to-all-done.arrived_ref = bf16[32,64,128]{2,1,0:T(8,128)(2,1)S(1)} async-done(((bf16[32,64,128]{2,1,0:T(8,128)(2,1)}), bf16[32,64,128]{2,1,0:T(8,128)(2,1)S(1)}, u32[]{:S(2)}, u32[]{:S(2)}) %all-to-all-start) | async-done | bytes 524320 | tf_op jit(solution)/shard_map/all_to_all | solution.py:250
  31.7 2.2 %collective-permute-start = (bf16[448,1024]{1,0:T(8,128)(2,1)}, bf16[448,1024]{1,0:T(8,128)(2,1)}, u32[]{:S(2)}, u32[]{:S(2)}) collective-permute-start(bf16[448,1024]{1,0:T(8,128)(2,1)} %bitcast.15), channel_id=1, source_target_pairs={{0,256},{32,288},{64,320},{96,352},{128,384},{160,416},{192,448},{... | collective-permute-start | bytes 2752520 | tf_op jit(solution)/shard_map/ppermute | solution.py:255
  33.9 0.0 copy-start
  33.9 1.5 %copy-done = bf16[1,2,1024,448]{2,3,1,0:T(8,128)(2,1)S(1)} copy-done((bf16[1,2,1024,448]{2,3,1,0:T(8,128)(2,1)S(1)}, bf16[1,2,1024,448]{2,3,1,0:T(8,128)(2,1)}, u32[]{:S(2)}) %copy-start) | copy-done | bytes 1835032
  35.4 2.0 %shard_map.56 = bf16[288,4096]{1,0:T(8,128)(2,1)S(1)} custom-call(s32[1]{0:T(128)} %bitcast.side_ref, bf16[32,64,128]{2,1,0:T(8,128)(2,1)S(1)} %all-to-all-done.arrived_ref, bf16[2,448,1024]{2,1,0:T(8,128)(2,1)S(1)} %bitcast.14), custom_call_target="tpu_custom_call" | custom-call | tf_op jit(solution)/shard_map/pallas_call | solution.py:256
  37.4 38.3 %fusion = bf16[40,4096]{1,0:T(8,128)(2,1)S(1)} fusion(bf16[288,4096]{1,0:T(8,128)(2,1)S(1)} %shard_map.56), kind=kCustom, calls=%all-reduce-scatter | all-reduce-scatter fusion | flops 1310721 | bytes 2689024
  75.8 0.1 slice.4
  75.8 0.0 copy-start.1
  75.8 3.2 %collective-permute-start.2 = (bf16[28,4096]{1,0:T(8,128)(2,1)S(1)}, bf16[28,4096]{1,0:T(8,128)(2,1)S(1)}, u32[]{:S(2)}, u32[]{:S(2)}) collective-permute-start(bf16[28,4096]{1,0:T(8,128)(2,1)S(1)} %slice.4), channel_id=1, source_target_pairs={{0,32},{32,64},{64,96},{96,128},{128,160},{160,192},{192,224},{256... | collective-permute-start | bytes 688136
  79.1 1.3 dynamic-slice.4
  81.1 1.3 collective-permute-done.2
  82.3 0.5 concatenate
  82.8 0.1 constant_dynamic-slice_fusion.kept_ref
  82.9 0.0 collective-permute-done.other_ref
  83.0 3.1 %collective-permute-start.1 = (bf16[36,2048]{1,0:T(8,128)(2,1)S(1)}, bf16[36,2048]{1,0:T(8,128)(2,1)S(1)}, u32[]{:S(2)}, u32[]{:S(2)}) collective-permute-start(bf16[36,2048]{1,0:T(8,128)(2,1)S(1)} %slice.3), channel_id=1, source_target_pairs={{0,256},{32,288},{64,320},{96,352},{128,384},{160,416},{192,448},{... | collective-permute-start | bytes 442376 | tf_op jit(solution)/shard_map/ppermute | solution.py:265
  86.0 3.0 %collective-permute-done.1.came_ref = bf16[36,2048]{1,0:T(8,128)(2,1)S(1)} collective-permute-done((bf16[36,2048]{1,0:T(8,128)(2,1)S(1)}, bf16[36,2048]{1,0:T(8,128)(2,1)S(1)}, u32[]{:S(2)}, u32[]{:S(2)}) %collective-permute-start.1) | collective-permute-done | bytes 147488 | tf_op jit(solution)/shard_map/ppermute | solution.py:265
  89.0 0.2 shard_map.57
  89.3 0.0 copy-start.4
  89.3 0.0 copy-start.5
  89.3 17.3 %all_to_all.15.hidden_ref = bf16[8,32,1152]{2,1,0:T(8,128)(2,1)S(1)} all-to-all(bf16[8,32,1152]{2,1,0:T(8,128)(2,1)S(1)} %shard_map.57), channel_id=1, replica_groups={{0,32,64,96,128,160,192,224},{256,288,320,352,384,416,448,480},{1,33,65..., dimensions={0} | all-to-all | bytes 1179648 | tf_op jit(solution)/shard_map/all_to_all | solution.py:270
  106.6 0.0 copy-done.1
  106.6 3.4 %shard_map.58 = bf16[64,32,128]{2,1,0:T(8,128)(2,1)} custom-call(s32[1]{0:T(128)} %bitcast.side_ref, bf16[8,32,1152]{2,1,0:T(8,128)(2,1)S(1)} %all_to_all.15.hidden_ref, bf16[448,1024]{1,0:T(8,128)(2,1)S(1)} %bitcast.16, bf16[448,1024]{1,0:T(8,128)(2,1)} %collective-permute-done.other_ref), custom_call_target="tpu_custom_call" | custom-call | tf_op jit(solution)/shard_map/pallas_call | solution.py:271
  109.9 14.3 %all-to-all-start.2 = ((bf16[64,32,128]{2,1,0:T(8,128)(2,1)}), bf16[64,32,128]{2,1,0:T(8,128)(2,1)S(1)}, u32[]{:S(2)}, u32[]{:S(2)}) async-start(bf16[64,32,128]{2,1,0:T(8,128)(2,1)} %shard_map.58), calls=%async_computation.2 | async-start | bytes 1048576 | tf_op jit(solution)/shard_map/all_to_all | solution.py:276
  124.3 0.0 copy-done.4
  124.3 0.0 copy-done.5
  124.3 0.3 shard_map.59
  124.6 16.6 %all-to-all-done.2.back_ref = bf16[64,32,128]{2,1,0:T(8,128)(2,1)S(1)} async-done(((bf16[64,32,128]{2,1,0:T(8,128)(2,1)}), bf16[64,32,128]{2,1,0:T(8,128)(2,1)S(1)}, u32[]{:S(2)}, u32[]{:S(2)}) %all-to-all-start.2) | async-done | bytes 524320 | tf_op jit(solution)/shard_map/all_to_all | solution.py:276
  141.2 2.2 %shard_map.60 = bf16[448,384]{1,0:T(8,128)(2,1)} custom-call(bf16[64,32,128]{2,1,0:T(8,128)(2,1)S(1)} %all-to-all-done.2.back_ref, bf16[576,384]{1,0:T(8,128)(2,1)S(1)} %get-tuple-element.19.high_ref, bf16[576,384]{1,0:T(8,128)(2,1)S(1)} %get-tuple-element.20.low_ref), custom_call_target="tpu_custom_call" | custom-call | tf_op jit(solution)/shard_map/pallas_call | solution.py:279
  (3 shorter events, 0.0 us)
Async XLA Ops:
  0.0 1.0 copy-start.2
  1.0 0.7 copy-start.3
  3.5 28.2 %all-to-all-start = ((bf16[32,64,128]{2,1,0:T(8,128)(2,1)}), bf16[32,64,128]{2,1,0:T(8,128)(2,1)S(1)}, u32[]{:S(2)}, u32[]{:S(2)}) async-start(bf16[32,64,128]{2,1,0:T(8,128)(2,1)} %get-tuple-element.13), calls=%async_computation | async-start | bytes 1048576 | tf_op jit(solution)/shard_map/all_to_all | solution.py:250
  31.7 51.2 %collective-permute-start = (bf16[448,1024]{1,0:T(8,128)(2,1)}, bf16[448,1024]{1,0:T(8,128)(2,1)}, u32[]{:S(2)}, u32[]{:S(2)}) collective-permute-start(bf16[448,1024]{1,0:T(8,128)(2,1)} %bitcast.15), channel_id=1, source_target_pairs={{0,256},{32,288},{64,320},{96,352},{128,384},{160,416},{192,448},{... | collective-permute-start | bytes 2752520 | tf_op jit(solution)/shard_map/ppermute | solution.py:255
  33.9 1.5 %copy-start = (bf16[1,2,1024,448]{2,3,1,0:T(8,128)(2,1)S(1)}, bf16[1,2,1024,448]{2,3,1,0:T(8,128)(2,1)}, u32[]{:S(2)}) copy-start(bf16[1,2,1024,448]{2,3,1,0:T(8,128)(2,1)} %param.8) | copy-start | bytes 5505028
  75.8 30.7 %copy-start.1 = (bf16[1,1024,448]{1,2,0:T(8,128)(2,1)S(1)}, bf16[1,1024,448]{1,2,0:T(8,128)(2,1)}, u32[]{:S(2)}) copy-start(bf16[1,1024,448]{1,2,0:T(8,128)(2,1)} %param.9) | copy-start | bytes 2752516
  75.8 6.5 %collective-permute-start.2 = (bf16[28,4096]{1,0:T(8,128)(2,1)S(1)}, bf16[28,4096]{1,0:T(8,128)(2,1)S(1)}, u32[]{:S(2)}, u32[]{:S(2)}) collective-permute-start(bf16[28,4096]{1,0:T(8,128)(2,1)S(1)} %slice.4), channel_id=1, source_target_pairs={{0,32},{32,64},{64,96},{96,128},{128,160},{160,192},{192,224},{256... | collective-permute-start | bytes 688136
  83.0 6.1 %collective-permute-start.1 = (bf16[36,2048]{1,0:T(8,128)(2,1)S(1)}, bf16[36,2048]{1,0:T(8,128)(2,1)S(1)}, u32[]{:S(2)}, u32[]{:S(2)}) collective-permute-start(bf16[36,2048]{1,0:T(8,128)(2,1)S(1)} %slice.3), channel_id=1, source_target_pairs={{0,256},{32,288},{64,320},{96,352},{128,384},{160,416},{192,448},{... | collective-permute-start | bytes 442376 | tf_op jit(solution)/shard_map/ppermute | solution.py:265
  89.3 35.0 %copy-start.4 = (s32[384,8]{0,1:T(8,128)S(1)}, s32[384,8]{0,1:T(8,128)}, u32[]{:S(2)}) copy-start(s32[384,8]{0,1:T(8,128)} %param.6) | copy-start | bytes 36868
  89.3 35.0 %copy-start.5 = (f32[384,8]{0,1:T(8,128)S(1)}, f32[384,8]{0,1:T(8,128)}, u32[]{:S(2)}) copy-start(f32[384,8]{0,1:T(8,128)} %param.7) | copy-start | bytes 36868
  109.9 31.2 %all-to-all-start.2 = ((bf16[64,32,128]{2,1,0:T(8,128)(2,1)}), bf16[64,32,128]{2,1,0:T(8,128)(2,1)S(1)}, u32[]{:S(2)}, u32[]{:S(2)}) async-start(bf16[64,32,128]{2,1,0:T(8,128)(2,1)} %shard_map.58), calls=%async_computation.2 | async-start | bytes 1048576 | tf_op jit(solution)/shard_map/all_to_all | solution.py:276

commit v3 on v2

--- a/solution.py
+++ b/solution.py
@@ -75,10 +75,20 @@
     return jnp.broadcast_to(x[:, None, :], (x.shape[0], 8, x.shape[1])).reshape(8 * x.shape[0], x.shape[1])
 
 
+def halves(rows, shift):
+    index = lax.broadcasted_iota(jnp.int32, (rows, 1), 0)
+    return ((index >> shift) & 1) * HALF
+
+
+def labels(shape):
+    index = lax.broadcasted_iota(jnp.int32, shape, 0)
+    return (index & (EXPERTS - PAIR)) | (index >> 5)
+
+
 def dispatch_kernel(ids_ref, tokens_ref, send_ref, slot_ref):
     count = ids_ref.shape[1]
-    label = lax.broadcasted_iota(jnp.int32, (EXPERTS, count), 0)
-    chosen = jnp.zeros((EXPERTS, count), F32)
+    label = labels((PAIR * EXPERTS, count))
+    chosen = jnp.zeros(label.shape, F32)
     for pick in range(ids_ref.shape[0]):
         chosen = jnp.where(ids_ref[pick : pick + 1, :] == label, 1.0, chosen)
     before = lax.broadcasted_iota(jnp.int32, (count, count), 0) < lax.broadcasted_iota(
@@ -88,35 +98,40 @@
     slot = jnp.where(chosen > 0.0, earlier, -1.0)
     slot_ref[...] = slot
     every = eightfold(slot)
-    place = row_of_eight(every.shape).astype(F32)
+    first = halves(every.shape[0], 3)
+    place = (row_of_eight((every.shape[0], 1)) + first).astype(F32)
     tokens = jnp.concatenate(
         [tokens_ref[...], jnp.zeros((PADDED - WIDTH, count), BF16)], axis=0
     )
-    for half in range(PAIR):
-        main = (every == place + HALF * half).astype(BF16)
-        last = (every == 1.0 * HALF * half + 8.0).astype(BF16)
-        main = lax.dot_general(main, tokens, NT, preferred_element_type=F32)
-        last = lax.dot_general(last, tokens, NT, preferred_element_type=F32)
-        send_ref[:, 32 * half : 32 * half + 32, :] = pack(main, last)
+    main = (every == place).astype(BF16)
+    last = (every == (first + 8).astype(F32)).astype(BF16)
+    main = lax.dot_general(main, tokens, NT, preferred_element_type=F32)
+    last = lax.dot_general(last, tokens, NT, preferred_element_type=F32)
+    for chip in range(PAIR):
+        rows = slice(MAIN * chip, MAIN * chip + MAIN)
+        send_ref[EXPERTS * chip : EXPERTS * chip + EXPERTS] = pack(main[rows], last[rows])
 
 
 def weights_kernel(ids_ref, combine_ref, slot_ref, high_ref, low_ref):
     slot = slot_ref[...]
-    label = lax.broadcasted_iota(jnp.int32, slot.shape, 0)
+    label = labels(slot.shape)
     weight = jnp.zeros(slot.shape, F32)
     for pick in range(ids_ref.shape[0]):
         weight = jnp.where(
             ids_ref[pick : pick + 1, :] == label, combine_ref[pick : pick + 1, :], weight
         )
     every, each = eightfold(slot), eightfold(weight)
-    place = row_of_eight(every.shape).astype(F32)
-    for half in range(PAIR):
-        main = jnp.where(every == place + HALF * half, each, 0.0)
-        last = jnp.where(slot == 1.0 * HALF * half + 8.0, weight, 0.0)
-        both = jnp.concatenate([main, last], axis=0)
+    place = (row_of_eight((every.shape[0], 1)) + halves(every.shape[0], 3)).astype(F32)
+    main = jnp.where(every == place, each, 0.0)
+    last = jnp.where(slot == (halves(slot.shape[0], 0) + 8).astype(F32), weight, 0.0)
+    for chip in range(PAIR):
+        both = jnp.concatenate(
+            [main[MAIN * chip : MAIN * chip + MAIN], last[EXPERTS * chip : EXPERTS * chip + EXPERTS]],
+            axis=0,
+        )
         high = both.astype(BF16)
-        high_ref[ROWS * half : ROWS * half + ROWS] = high
-        low_ref[ROWS * half : ROWS * half + ROWS] = (both - high.astype(F32)).astype(BF16)
+        high_ref[ROWS * chip : ROWS * chip + ROWS] = high
+        low_ref[ROWS * chip : ROWS * chip + ROWS] = (both - high.astype(F32)).astype(BF16)
 
 
 def ordered(count, blocks, column, last):
@@ -132,34 +147,47 @@
     return chosen.astype(BF16)
 
 
-def gate_up_kernel(side_ref, arrived_ref, w_ref, terms_ref):
+def own_gate_up_kernel(side_ref, arrived_ref, own_ref, partial_ref, rows_ref):
     side = side_ref[0]
     column = lax.broadcasted_iota(jnp.int32, (ROWS, MAIN), 1)
     take_main = ordered(ROWS, DEPTH, column, False)
     take_last = ordered(ROWS, DEPTH, column, True)
     rows = []
-    for place in range(PAIR):
-        half = side if place == 0 else 1 - side
-        main, runs = opened(arrived_ref[:, pl.ds(half * 32, 32), :])
+    for which in (side, 1 - side):
+        main, runs = opened(arrived_ref[pl.ds(which * EXPERTS, EXPERTS)])
         taken = jnp.dot(take_main, main, preferred_element_type=F32)
         taken += jnp.dot(take_last, runs, preferred_element_type=F32)
         rows.append(taken.astype(BF16))
-    rows = jnp.concatenate(rows, axis=0)[:, :WIDTH]
-    units = w_ref.shape[2]
+    rows_ref[...] = rows[1]
+    units = own_ref.shape[2]
     for index in range(2):
         for start in range(0, units, PADDED):
-            part = jnp.dot(rows, w_ref[index, :, start : start + PADDED], preferred_element_type=F32)
-            part = part.astype(BF16)
-            for place in range(PAIR):
-                at = (2 * place + index) * units + start
-                terms_ref[:, at : at + PADDED] = part[ROWS * place : ROWS * place + ROWS]
-
-
-def hidden_kernel(kept_ref, came_ref, hidden_ref):
-    units = came_ref.shape[1] // 2
-    count = came_ref.shape[0]
+            part = jnp.dot(
+                rows[0][:, :WIDTH],
+                own_ref[index, :, start : start + PADDED],
+                preferred_element_type=F32,
+            )
+            partial_ref[:, index * units + start : index * units + start + PADDED] = part
+
+
+def other_gate_up_kernel(partial_ref, rows_ref, other_ref, terms_ref):
+    units = other_ref.shape[2]
+    for index in range(2):
+        for start in range(0, units, PADDED):
+            at = slice(index * units + start, index * units + start + PADDED)
+            part = jnp.dot(
+                rows_ref[:, :WIDTH],
+                other_ref[index, :, start : start + PADDED],
+                preferred_element_type=F32,
+            )
+            terms_ref[:, at] = (partial_ref[:, at] + part).astype(BF16)
+
+
+def hidden_kernel(sums_ref, hidden_ref):
+    units = sums_ref.shape[1] // 2
+    count = sums_ref.shape[0]
     mains = count * 8 // 9
-    both = kept_ref[:, : 2 * units].astype(F32) + came_ref[...].astype(F32)
+    both = sums_ref[...].astype(F32)
     gate, up = both[:, :units], both[:, units:]
     hidden = (gate / (1.0 + jnp.exp(-gate)) * up).astype(BF16)
     lasts = count - mains
@@ -226,55 +254,73 @@
 def local(tokens, expert_ids, combine, w_in, w_down):
     count = tokens.shape[0]
     hidden_units = w_down.shape[1]
-    group = lax.axis_index("group")
-    side = (group // DEPTH).astype(jnp.int32).reshape(1)
-    swap = [(g, (g + DEPTH) % (PAIR * DEPTH)) for g in range(PAIR * DEPTH)]
+    side = (lax.axis_index("expert") & 1).astype(jnp.int32).reshape(1)
+    everyone = ("group", "expert")
     along_z = [[x * DEPTH + z for z in range(DEPTH)] for x in range(PAIR)]
-    along_pair = [
+    along_plane = [
         [(x * DEPTH + z) * EXPERTS + e for x in range(PAIR) for e in range(EXPERTS)]
         for z in range(DEPTH)
     ]
+    turn = [
+        ((x * DEPTH + z) * EXPERTS + 2 * y + c, (c * DEPTH + z) * EXPERTS + 2 * y + x)
+        for x in range(PAIR)
+        for z in range(DEPTH)
+        for y in range(EXPERTS // 2)
+        for c in range(2)
+    ]
+    cores = [(e, e ^ 1) for e in range(EXPERTS)]
     tokens, ids, combine = tokens.T, expert_ids.T, combine.T
     w_in = jnp.swapaxes(w_in[0], 1, 2)
     w_down = w_down[0].T
     scalar = pl.BlockSpec(memory_space=pltpu.SMEM)
     whole = pl.BlockSpec(memory_space=pltpu.VMEM)
-
+    packed = (PAIR * EXPERTS, 32, 128)
+
+    own_in = lax.ppermute(w_in, everyone, turn)
     send, slot = call(
         dispatch_kernel,
         (
-            jax.ShapeDtypeStruct((EXPERTS, 64, 128), BF16),
-            jax.ShapeDtypeStruct((EXPERTS, count), F32),
+            jax.ShapeDtypeStruct(packed, BF16),
+            jax.ShapeDtypeStruct((PAIR * EXPERTS, count), F32),
         ),
     )(ids, tokens)
-    arrived = lax.all_to_all(send, "expert", 0, 0, tiled=True)
+    arrived = lax.all_to_all(
+        send, everyone, 0, 0, axis_index_groups=along_plane, tiled=True
+    )
     high, low = call(
         weights_kernel, (jax.ShapeDtypeStruct((PAIR * ROWS, count), BF16),) * 2
     )(ids, combine, slot)
-    w_down_sent, arrived = lax.optimization_barrier((w_down, arrived))
-    other_down = lax.ppermute(w_down_sent, "group", swap)
+    own_in, w_down, arrived = lax.optimization_barrier((own_in, w_down, arrived))
+    other_in = lax.ppermute(own_in, "expert", cores)
+    own_down = lax.ppermute(w_down, everyone, turn)
+    partial, rows = call(
+        own_gate_up_kernel,
+        (
+            jax.ShapeDtypeStruct((ROWS, 2 * hidden_units), F32),
+            jax.ShapeDtypeStruct((ROWS, PADDED), BF16),
+        ),
+        in_specs=[scalar, whole, whole],
+    )(side, arrived, own_in)
     terms = call(
-        gate_up_kernel,
-        jax.ShapeDtypeStruct((ROWS, PAIR * 2 * hidden_units), BF16),
-        in_specs=[scalar, whole, whole],
-    )(side, arrived, w_in)
-    terms = lax.psum_scatter(
+        other_gate_up_kernel, jax.ShapeDtypeStruct((ROWS, 2 * hidden_units), BF16)
+    )(partial, rows, other_in)
+    sums = lax.psum_scatter(
         terms, "group", scatter_dimension=0, axis_index_groups=along_z, tiled=True
     )
-    terms, other_down = lax.optimization_barrier((terms, other_down))
-    came = lax.ppermute(terms[:, 2 * hidden_units :], "group", swap)
+    sums, own_down = lax.optimization_barrier((sums, own_down))
+    other_down = lax.ppermute(own_down, "expert", cores)
     mains = EXPERTS // DEPTH * 8
     hidden = call(
         hidden_kernel, jax.ShapeDtypeStruct((DEPTH, mains, hidden_units + 128), BF16)
-    )(terms, came)
+    )(sums)
     hidden = lax.all_to_all(hidden, "group", 0, 0, axis_index_groups=along_z, tiled=True)
     send = call(
         down_kernel,
-        jax.ShapeDtypeStruct((PAIR * EXPERTS, 32, 128), BF16),
+        jax.ShapeDtypeStruct(packed, BF16),
         in_specs=[scalar, whole, whole, whole],
-    )(side, hidden, w_down, other_down)
+    )(side, hidden, own_down, other_down)
     back = lax.all_to_all(
-        send, ("group", "expert"), 0, 0, axis_index_groups=along_pair, tiled=True
+        send, everyone, 0, 0, axis_index_groups=along_plane, tiled=True
     )
     routed = call(combine_kernel, jax.ShapeDtypeStruct((WIDTH, count), BF16))(back, high, low)
     return routed.T

time: 144 us -> 130 us (0.903)
  waiting for transfers between devices: 37.8 us -> 24.7 us
  starting transfers between devices: 34 us -> 37.3 us
  blocking collectives: 55.6 us -> 52.6 us
  local copies, waits for them, and re-layouts: 5.2 us -> 3.27 us
    unnamed x1, blocking collectives: 38.3 us -> 25.9 us
    all_to_all x2, waiting for transfers between devices: 33.6 us -> 22.3 us  [the longest x1 16.5 us: local(): lax.all_to_all(send, everyone, 0, 0, axis_index_groups=along_plane, tiled...]
    ppermute x2 -> x4, starting transfers between devices: 5.27 us -> 15.7 us  [the longest x1 6.52 us: local(): other_down = lax.ppermute(own_down, 'expert', cores)]
    all_to_all x1, blocking collectives: 17.3 us -> 26.7 us  [local(): lax.all_to_all(send, everyone, 0, 0, axis_index_groups=along_plane, tiled...]
    all_to_all x2, starting transfers between devices: 25.5 us -> 18.9 us  [the longest x1 12.9 us: local(): lax.all_to_all(send, everyone, 0, 0, axis_index_groups=along_plane, tiled...]
    unnamed x15 -> x11, local copies, waits for them, and re-layouts: 5.1 us -> 3.22 us
    ppermute x2 -> x4, waiting for transfers between devices: 3 us -> 2.29 us  [the longest x1 2.08 us: local(): other_down = lax.ppermute(own_down, 'expert', cores)]
    pallas_call x3 -> x4, Pallas kernels: 7.12 us -> 6.83 us  [the longest x1 2.27 us: local(): call(other_gate_up_kernel, jax.ShapeDtypeStruct((ROWS, 2 * hidden_units),...]
  transfers between devices with their start and end apart: 5 -> 7, of which waited for: 4 -> 5; matrix products, arithmetic and copies ran while one was open for 28% -> 21% of each run, Pallas kernels for 2% -> 4%
where the time goes in v3:
time: 130 us; the launch traced here: 129 us
  blocking collectives  52.6 us (40%)
  starting transfers between devices  37.3 us (29%)
  waiting for transfers between devices  24.7 us (19%)
  Pallas kernels  10.4 us (8%)
  local copies, waits for them, and re-layouts  3.27 us (3%)
    all_to_all x1, blocking collectives, local(): lax.all_to_all(send, everyone, 0, 0, axis_index_groups=along_plane, tiled...  26.7 us
    unnamed x1, blocking collectives  25.9 us
    all_to_all x1, waiting for transfers between devices, local(): lax.all_to_all(send, everyone, 0, 0, axis_index_groups=along_plane, tiled...  16.5 us
    all_to_all x1, starting transfers between devices, local(): lax.all_to_all(send, everyone, 0, 0, axis_index_groups=along_plane, tiled...  12.9 us
    ppermute x1, starting transfers between devices, local(): other_down = lax.ppermute(own_down, 'expert', cores)  6.52 us
    all_to_all x1, starting transfers between devices, local(): lax.all_to_all(hidden, 'group', 0, 0, axis_index_groups=along_z, tiled=True)  5.97 us
    all_to_all x1, waiting for transfers between devices, local(): lax.all_to_all(hidden, 'group', 0, 0, axis_index_groups=along_z, tiled=True)  5.82 us
    ppermute x1, starting transfers between devices, local(): own_in = lax.ppermute(w_in, everyone, turn)  4.5 us
  transfers between devices with their start and end apart: 7, of which 5 were waited for; matrix products, arithmetic and copies ran while one was open for 21% of the time, Pallas kernels for 4%

profile of v3, /device:TPU:1, one launch (start us, length us, event | category | flops | bytes accessed | tf_op | source)
XLA Modules:
  0.0 128.9 jit_solution(6092320333899676558)
XLA Ops:
  0.0 4.5 %collective-permute-start = (bf16[2,448,1024]{2,1,0:T(8,128)(2,1)}, bf16[2,448,1024]{2,1,0:T(8,128)(2,1)S(1)}, u32[]{:S(2)}, u32[]{:S(2)}) collective-permute-start(bf16[2,448,1024]{2,1,0:T(8,128)(2,1)} %bitcast.18), channel_id=1, source_target_pairs={{0,0},{1,256},{2,2},{3,258},{4,4},{5,260},{6,6},{7,262},{8,8},{9,2... | collective-permute-start | bytes 5505032 | tf_op jit(solution)/shard_map/ppermute | solution.py:279
  4.5 0.0 copy-start
  4.5 1.0 copy-done
  5.5 0.0 copy-start.1
  5.5 0.7 copy-done.1
  6.2 1.0 shard_map.55
  7.2 26.7 %all_to_all.15.arrived_ref = bf16[64,32,128]{2,1,0:T(8,128)(2,1)S(1)} all-to-all(bf16[64,32,128]{2,1,0:T(8,128)(2,1)S(1)} %get-tuple-element.16), channel_id=1, replica_groups={{0,1,2,3,4,5,6,7,8,9,10,11,12,13,14,15,16,17,18,19,20,21,22,23,24,25,26..., dimensions={0} | all-to-all | bytes 1048576 | tf_op jit(solution)/shard_map/all_to_all | solution.py:287
  33.9 0.0 collective-permute-done.own_ref
  33.9 2.8 %collective-permute-start.1 = (bf16[2,448,1024]{2,1,0:T(8,128)(2,1)S(1)}, bf16[2,448,1024]{2,1,0:T(8,128)(2,1)}, u32[]{:S(2)}, u32[]{:S(2)}) collective-permute-start(bf16[2,448,1024]{2,1,0:T(8,128)(2,1)S(1)} %collective-permute-done.own_ref), channel_id=1, source_target_pairs={{0,1},{1,0},{2,3},{3,2},{4,5},{5,4},{6,7},{7,6},{8,9},{9,8},{10,11... | collective-permute-start | bytes 5505032 | tf_op jit(solution)/shard_map/ppermute | solution.py:294
  36.6 1.9 %collective-permute-start.2 = (bf16[448,1024]{1,0:T(8,128)(2,1)}, bf16[448,1024]{1,0:T(8,128)(2,1)S(1)}, u32[]{:S(2)}, u32[]{:S(2)}) collective-permute-start(bf16[448,1024]{1,0:T(8,128)(2,1)} %bitcast.19), channel_id=1, source_target_pairs={{0,0},{1,256},{2,2},{3,258},{4,4},{5,260},{6,6},{7,262},{8,8},{9,2... | collective-permute-start | bytes 2752520 | tf_op jit(solution)/shard_map/ppermute | solution.py:295
  38.6 1.4 %shard_map.56 = (f32[288,2048]{1,0:T(8,128)S(1)}, bf16[288,512]{1,0:T(8,128)(2,1)S(1)}) custom-call(s32[1]{0:T(128)} %bitcast.side_ref, bf16[64,32,128]{2,1,0:T(8,128)(2,1)S(1)} %all_to_all.15.arrived_ref, bf16[2,448,1024]{2,1,0:T(8,128)(2,1)S(1)} %collective-permute-done.own_ref), custom_call_target="tpu_custom_call" | custom-call | tf_op jit(solution)/shard_map/pallas_call | solution.py:296
  40.0 0.2 collective-permute-done.1.other_ref
  40.2 2.3 %shard_map.57 = bf16[288,2048]{1,0:T(8,128)(2,1)S(1)} custom-call(f32[288,2048]{1,0:T(8,128)S(1)} %get-tuple-element.19.partial_ref, bf16[288,512]{1,0:T(8,128)(2,1)S(1)} %get-tuple-element.20.rows_ref, bf16[2,448,1024]{2,1,0:T(8,128)(2,1)} %collective-permute-done.1.other_ref), custom_call_target="tpu_custom_call" | custom-call | tf_op jit(solution)/shard_map/pallas_call | solution.py:304
  42.4 25.9 %fusion = bf16[40,2048]{1,0:T(8,128)(2,1)S(1)} fusion(bf16[288,2048]{1,0:T(8,128)(2,1)S(1)} %shard_map.57), kind=kCustom, calls=%all-reduce-scatter | all-reduce-scatter fusion | flops 655361 | bytes 1345536
  68.4 2.7 %collective-permute-start.4 = (bf16[28,2048]{1,0:T(8,128)(2,1)S(1)}, bf16[28,2048]{1,0:T(8,128)(2,1)S(1)}, u32[]{:S(2)}, u32[]{:S(2)}) collective-permute-start(bf16[28,2048]{1,0:T(8,128)(2,1)S(1)} %slice), channel_id=1, source_target_pairs={{0,32},{32,64},{64,96},{96,128},{128,160},{160,192},{192,224},{256... | collective-permute-start | bytes 344072
  71.1 1.3 dynamic-slice.4
  72.9 0.1 collective-permute-done.4
  73.0 0.2 concatenate
  73.3 0.0 collective-permute-done.2.own_ref
  73.3 1.0 shard_map.58
  74.3 6.0 %all-to-all-start.1 = ((bf16[8,32,1152]{2,1,0:T(8,128)(2,1)}), bf16[8,32,1152]{2,1,0:T(8,128)(2,1)S(1)}, u32[]{:S(2)}, u32[]{:S(2)}) async-start(bf16[8,32,1152]{2,1,0:T(8,128)(2,1)} %shard_map.58), calls=%async_computation.1 | async-start | bytes 1179648 | tf_op jit(solution)/shard_map/all_to_all | solution.py:316
  80.3 0.0 copy-start.3
  80.3 6.5 %collective-permute-start.3 = (bf16[448,1024]{1,0:T(8,128)(2,1)S(1)}, bf16[448,1024]{1,0:T(8,128)(2,1)S(1)}, u32[]{:S(2)}, u32[]{:S(2)}) collective-permute-start(bf16[448,1024]{1,0:T(8,128)(2,1)S(1)} %collective-permute-done.2.own_ref), channel_id=1, source_target_pairs={{0,1},{1,0},{2,3},{3,2},{4,5},{5,4},{6,7},{7,6},{8,9},{9,8},{10,11... | collective-permute-start | bytes 2752520 | tf_op jit(solution)/shard_map/ppermute | solution.py:311
  86.9 2.1 %collective-permute-done.3.other_ref = bf16[448,1024]{1,0:T(8,128)(2,1)S(1)} collective-permute-done((bf16[448,1024]{1,0:T(8,128)(2,1)S(1)}, bf16[448,1024]{1,0:T(8,128)(2,1)S(1)}, u32[]{:S(2)}, u32[]{:S(2)}) %collective-permute-start.3) | collective-permute-done | bytes 917536 | tf_op jit(solution)/shard_map/ppermute | solution.py:311
  88.9 5.8 %all-to-all-done.1.hidden_ref = bf16[8,32,1152]{2,1,0:T(8,128)(2,1)S(1)} async-done(((bf16[8,32,1152]{2,1,0:T(8,128)(2,1)}), bf16[8,32,1152]{2,1,0:T(8,128)(2,1)S(1)}, u32[]{:S(2)}, u32[]{:S(2)}) %all-to-all-start.1) | async-done | bytes 589856 | tf_op jit(solution)/shard_map/all_to_all | solution.py:316
  94.8 2.2 %shard_map.59 = bf16[64,32,128]{2,1,0:T(8,128)(2,1)} custom-call(s32[1]{0:T(128)} %bitcast.side_ref, bf16[8,32,1152]{2,1,0:T(8,128)(2,1)S(1)} %all-to-all-done.1.hidden_ref, bf16[448,1024]{1,0:T(8,128)(2,1)S(1)} %collective-permute-done.2.own_ref, bf16[448,1024]{1,0:T(8,128)(2,1)S(1)} %collective-permute-done.3.other_ref), custom_call_target="tpu_custom_call" | custom-call | tf_op jit(solution)/shard_map/pallas_call | solution.py:317
  96.9 12.9 %all-to-all-start.2 = ((bf16[64,32,128]{2,1,0:T(8,128)(2,1)}), bf16[64,32,128]{2,1,0:T(8,128)(2,1)S(1)}, u32[]{:S(2)}, u32[]{:S(2)}) async-start(bf16[64,32,128]{2,1,0:T(8,128)(2,1)} %shard_map.59), calls=%async_computation.2 | async-start | bytes 1048576 | tf_op jit(solution)/shard_map/all_to_all | solution.py:322
  109.8 0.0 copy-done.2
  109.9 0.0 copy-done.3
  109.9 0.4 shard_map.60
  110.3 16.5 %all-to-all-done.2.back_ref = bf16[64,32,128]{2,1,0:T(8,128)(2,1)S(1)} async-done(((bf16[64,32,128]{2,1,0:T(8,128)(2,1)}), bf16[64,32,128]{2,1,0:T(8,128)(2,1)S(1)}, u32[]{:S(2)}, u32[]{:S(2)}) %all-to-all-start.2) | async-done | bytes 524320 | tf_op jit(solution)/shard_map/all_to_all | solution.py:322
  126.8 2.2 %shard_map.61 = bf16[448,384]{1,0:T(8,128)(2,1)} custom-call(bf16[64,32,128]{2,1,0:T(8,128)(2,1)S(1)} %all-to-all-done.2.back_ref, bf16[576,384]{1,0:T(8,128)(2,1)S(1)} %get-tuple-element.25.high_ref, bf16[576,384]{1,0:T(8,128)(2,1)S(1)} %get-tuple-element.26.low_ref), custom_call_target="tpu_custom_call" | custom-call | tf_op jit(solution)/shard_map/pallas_call | solution.py:325
  (3 shorter events, 0.1 us)
Async XLA Ops:
  0.0 33.9 %collective-permute-start = (bf16[2,448,1024]{2,1,0:T(8,128)(2,1)}, bf16[2,448,1024]{2,1,0:T(8,128)(2,1)S(1)}, u32[]{:S(2)}, u32[]{:S(2)}) collective-permute-start(bf16[2,448,1024]{2,1,0:T(8,128)(2,1)} %bitcast.18), channel_id=1, source_target_pairs={{0,0},{1,256},{2,2},{3,258},{4,4},{5,260},{6,6},{7,262},{8,8},{9,2... | collective-permute-start | bytes 5505032 | tf_op jit(solution)/shard_map/ppermute | solution.py:279
  4.5 1.0 copy-start
  5.5 0.7 copy-start.1
  33.9 6.3 %collective-permute-start.1 = (bf16[2,448,1024]{2,1,0:T(8,128)(2,1)S(1)}, bf16[2,448,1024]{2,1,0:T(8,128)(2,1)}, u32[]{:S(2)}, u32[]{:S(2)}) collective-permute-start(bf16[2,448,1024]{2,1,0:T(8,128)(2,1)S(1)} %collective-permute-done.own_ref), channel_id=1, source_target_pairs={{0,1},{1,0},{2,3},{3,2},{4,5},{5,4},{6,7},{7,6},{8,9},{9,8},{10,11... | collective-permute-start | bytes 5505032 | tf_op jit(solution)/shard_map/ppermute | solution.py:294
  36.6 36.7 %collective-permute-start.2 = (bf16[448,1024]{1,0:T(8,128)(2,1)}, bf16[448,1024]{1,0:T(8,128)(2,1)S(1)}, u32[]{:S(2)}, u32[]{:S(2)}) collective-permute-start(bf16[448,1024]{1,0:T(8,128)(2,1)} %bitcast.19), channel_id=1, source_target_pairs={{0,0},{1,256},{2,2},{3,258},{4,4},{5,260},{6,6},{7,262},{8,8},{9,2... | collective-permute-start | bytes 2752520 | tf_op jit(solution)/shard_map/ppermute | solution.py:295
  68.4 4.6 %collective-permute-start.4 = (bf16[28,2048]{1,0:T(8,128)(2,1)S(1)}, bf16[28,2048]{1,0:T(8,128)(2,1)S(1)}, u32[]{:S(2)}, u32[]{:S(2)}) collective-permute-start(bf16[28,2048]{1,0:T(8,128)(2,1)S(1)} %slice), channel_id=1, source_target_pairs={{0,32},{32,64},{64,96},{96,128},{128,160},{160,192},{192,224},{256... | collective-permute-start | bytes 344072
  74.3 20.4 %all-to-all-start.1 = ((bf16[8,32,1152]{2,1,0:T(8,128)(2,1)}), bf16[8,32,1152]{2,1,0:T(8,128)(2,1)S(1)}, u32[]{:S(2)}, u32[]{:S(2)}) async-start(bf16[8,32,1152]{2,1,0:T(8,128)(2,1)} %shard_map.58), calls=%async_computation.1 | async-start | bytes 1179648 | tf_op jit(solution)/shard_map/all_to_all | solution.py:316
  80.3 29.5 %copy-start.2 = (s32[384,8]{0,1:T(8,128)S(1)}, s32[384,8]{0,1:T(8,128)}, u32[]{:S(2)}) copy-start(s32[384,8]{0,1:T(8,128)} %param.6) | copy-start | bytes 36868
  80.3 29.5 %copy-start.3 = (f32[384,8]{0,1:T(8,128)S(1)}, f32[384,8]{0,1:T(8,128)}, u32[]{:S(2)}) copy-start(f32[384,8]{0,1:T(8,128)} %param.7) | copy-start | bytes 36868
  80.3 8.6 %collective-permute-start.3 = (bf16[448,1024]{1,0:T(8,128)(2,1)S(1)}, bf16[448,1024]{1,0:T(8,128)(2,1)S(1)}, u32[]{:S(2)}, u32[]{:S(2)}) collective-permute-start(bf16[448,1024]{1,0:T(8,128)(2,1)S(1)} %collective-permute-done.2.own_ref), channel_id=1, source_target_pairs={{0,1},{1,0},{2,3},{3,2},{4,5},{5,4},{6,7},{7,6},{8,9},{9,8},{10,11... | collective-permute-start | bytes 2752520 | tf_op jit(solution)/shard_map/ppermute | solution.py:311
  96.9 29.8 %all-to-all-start.2 = ((bf16[64,32,128]{2,1,0:T(8,128)(2,1)}), bf16[64,32,128]{2,1,0:T(8,128)(2,1)S(1)}, u32[]{:S(2)}, u32[]{:S(2)}) async-start(bf16[64,32,128]{2,1,0:T(8,128)(2,1)} %shard_map.59), calls=%async_computation.2 | async-start | bytes 1048576 | tf_op jit(solution)/shard_map/all_to_all | solution.py:322

commit v4 on v3

--- a/solution.py
+++ b/solution.py
@@ -14,11 +14,12 @@
 PADDED = 512
 MAIN = EXPERTS * 8
 ROWS = EXPERTS * HALF
+SHARD = 39
 F32 = jnp.float32
 BF16 = jnp.bfloat16
 NT = (((1,), (1,)), ((), ()))
 TN = (((0,), (0,)), ((), ()))
-VMEM_BYTES = 48 * 1024 * 1024
+VMEM_BYTES = 32 * 1024 * 1024
 
 
 def row_of_eight(shape):
@@ -85,8 +86,13 @@
     return (index & (EXPERTS - PAIR)) | (index >> 5)
 
 
-def dispatch_kernel(ids_ref, tokens_ref, send_ref, slot_ref):
+def dispatch_kernel(ids_hbm, tokens_hbm, send_ref, slot_ref, ids_ref, tokens_ref, ids_sem, tokens_sem):
+    ids_copy = pltpu.make_async_copy(ids_hbm, ids_ref, ids_sem)
+    tokens_copy = pltpu.make_async_copy(tokens_hbm, tokens_ref, tokens_sem)
+    ids_copy.start()
+    tokens_copy.start()
     count = ids_ref.shape[1]
+    ids_copy.wait()
     label = labels((PAIR * EXPERTS, count))
     chosen = jnp.zeros(label.shape, F32)
     for pick in range(ids_ref.shape[0]):
@@ -100,6 +106,7 @@
     every = eightfold(slot)
     first = halves(every.shape[0], 3)
     place = (row_of_eight((every.shape[0], 1)) + first).astype(F32)
+    tokens_copy.wait()
     tokens = jnp.concatenate(
         [tokens_ref[...], jnp.zeros((PADDED - WIDTH, count), BF16)], axis=0
     )
@@ -112,7 +119,7 @@
         send_ref[EXPERTS * chip : EXPERTS * chip + EXPERTS] = pack(main[rows], last[rows])
 
 
-def weights_kernel(ids_ref, combine_ref, slot_ref, high_ref, low_ref):
+def weights_kernel(ids_ref, combine_ref, slot_ref, weights_ref):
     slot = slot_ref[...]
     label = labels(slot.shape)
     weight = jnp.zeros(slot.shape, F32)
@@ -130,18 +137,23 @@
             axis=0,
         )
         high = both.astype(BF16)
-        high_ref[ROWS * chip : ROWS * chip + ROWS] = high
-        low_ref[ROWS * chip : ROWS * chip + ROWS] = (both - high.astype(F32)).astype(BF16)
+        low = (both - high.astype(F32)).astype(BF16)
+        weights_ref[ROWS * chip : ROWS * chip + ROWS] = jnp.concatenate([high, low], axis=1)
 
 
 def ordered(count, blocks, column, last):
     per = count // blocks
-    mains = per * 8 // 9
+    lasts = EXPERTS // blocks
+    mains = lasts * 8
     row = lax.broadcasted_iota(jnp.int32, (count, MAIN), 0)
     block = lax.div(row, per)
     inside = row - block * per
     if last:
-        chosen = (inside >= mains) & ((column >> 3) == block * (per - mains) + inside - mains)
+        chosen = (
+            (inside >= mains)
+            & (inside < mains + lasts)
+            & ((column >> 3) == block * lasts + inside - mains)
+        )
     else:
         chosen = (inside < mains) & (column == block * mains + inside)
     return chosen.astype(BF16)
@@ -149,9 +161,9 @@
 
 def own_gate_up_kernel(side_ref, arrived_ref, own_ref, partial_ref, rows_ref):
     side = side_ref[0]
-    column = lax.broadcasted_iota(jnp.int32, (ROWS, MAIN), 1)
-    take_main = ordered(ROWS, DEPTH, column, False)
-    take_last = ordered(ROWS, DEPTH, column, True)
+    column = lax.broadcasted_iota(jnp.int32, (SHARD * DEPTH, MAIN), 1)
+    take_main = ordered(SHARD * DEPTH, DEPTH, column, False)
+    take_last = ordered(SHARD * DEPTH, DEPTH, column, True)
     rows = []
     for which in (side, 1 - side):
         main, runs = opened(arrived_ref[pl.ds(which * EXPERTS, EXPERTS)])
@@ -186,11 +198,11 @@
 def hidden_kernel(sums_ref, hidden_ref):
     units = sums_ref.shape[1] // 2
     count = sums_ref.shape[0]
-    mains = count * 8 // 9
+    lasts = EXPERTS // DEPTH
+    mains = lasts * 8
     both = sums_ref[...].astype(F32)
     gate, up = both[:, :units], both[:, units:]
     hidden = (gate / (1.0 + jnp.exp(-gate)) * up).astype(BF16)
-    lasts = count - mains
     row = lax.broadcasted_iota(jnp.int32, (mains, count), 0)
     column = lax.broadcasted_iota(jnp.int32, (mains, count), 1)
     pick = (column == mains + lax.rem(row, lasts)).astype(BF16)
@@ -235,11 +247,11 @@
         send_ref[pl.ds(where * EXPERTS, EXPERTS)] = pack(result[:MAIN].astype(F32), last)
 
 
-def combine_kernel(back_ref, high_ref, low_ref, out_ref):
+def combine_kernel(back_ref, weights_ref, out_ref):
     rows = jnp.concatenate([unpack(back_ref[:EXPERTS]), unpack(back_ref[EXPERTS:])], axis=0)
-    routed = lax.dot_general(rows, high_ref[...], TN, preferred_element_type=F32)
-    routed += lax.dot_general(rows, low_ref[...], TN, preferred_element_type=F32)
-    out_ref[...] = routed[:WIDTH].astype(BF16)
+    routed = lax.dot_general(rows, weights_ref[...], TN, preferred_element_type=F32)
+    count = out_ref.shape[1]
+    out_ref[...] = (routed[:WIDTH, :count] + routed[:WIDTH, count:]).astype(BF16)
 
 
 def call(kernel, out, **more):
@@ -283,26 +295,36 @@
             jax.ShapeDtypeStruct(packed, BF16),
             jax.ShapeDtypeStruct((PAIR * EXPERTS, count), F32),
         ),
-    )(ids, tokens)
+        in_specs=[pl.BlockSpec(memory_space=pltpu.HBM)] * 2,
+        scratch_shapes=[
+            pltpu.VMEM(ids.shape, jnp.int32),
+            pltpu.VMEM(tokens.shape, BF16),
+            pltpu.SemaphoreType.DMA,
+            pltpu.SemaphoreType.DMA,
+        ],
+    )(
+        pltpu.with_memory_space_constraint(ids, pltpu.HBM),
+        pltpu.with_memory_space_constraint(tokens, pltpu.HBM),
+    )
     arrived = lax.all_to_all(
         send, everyone, 0, 0, axis_index_groups=along_plane, tiled=True
     )
-    high, low = call(
-        weights_kernel, (jax.ShapeDtypeStruct((PAIR * ROWS, count), BF16),) * 2
-    )(ids, combine, slot)
+    weights = call(weights_kernel, jax.ShapeDtypeStruct((PAIR * ROWS, 2 * count), BF16))(
+        ids, combine, slot
+    )
     own_in, w_down, arrived = lax.optimization_barrier((own_in, w_down, arrived))
     other_in = lax.ppermute(own_in, "expert", cores)
     own_down = lax.ppermute(w_down, everyone, turn)
     partial, rows = call(
         own_gate_up_kernel,
         (
-            jax.ShapeDtypeStruct((ROWS, 2 * hidden_units), F32),
-            jax.ShapeDtypeStruct((ROWS, PADDED), BF16),
+            jax.ShapeDtypeStruct((SHARD * DEPTH, 2 * hidden_units), F32),
+            jax.ShapeDtypeStruct((SHARD * DEPTH, PADDED), BF16),
         ),
         in_specs=[scalar, whole, whole],
     )(side, arrived, own_in)
     terms = call(
-        other_gate_up_kernel, jax.ShapeDtypeStruct((ROWS, 2 * hidden_units), BF16)
+        other_gate_up_kernel, jax.ShapeDtypeStruct((SHARD * DEPTH, 2 * hidden_units), BF16)
     )(partial, rows, other_in)
     sums = lax.psum_scatter(
         terms, "group", scatter_dimension=0, axis_index_groups=along_z, tiled=True
@@ -322,7 +344,7 @@
     back = lax.all_to_all(
         send, everyone, 0, 0, axis_index_groups=along_plane, tiled=True
     )
-    routed = call(combine_kernel, jax.ShapeDtypeStruct((WIDTH, count), BF16))(back, high, low)
+    routed = call(combine_kernel, jax.ShapeDtypeStruct((WIDTH, count), BF16))(back, weights)
     return routed.T
 
 

time: 130 us -> 129 us (level)
  local copies, waits for them, and re-layouts: 3.27 us -> 1.6 us
    unnamed x11 -> x7, local copies, waits for them, and re-layouts: 3.22 us -> 1.55 us
    all_to_all x1, starting transfers between devices: 12.9 us -> 14.2 us  [local(): lax.all_to_all(send, everyone, 0, 0, axis_index_groups=along_plane, tiled...]
  transfers between devices with their start and end apart: 7 -> 7, of which waited for: 5 -> 4; matrix products, arithmetic and copies ran while one was open for 21% -> 21% of each run, Pallas kernels for 4% -> 5%
where the time goes in v4:
time: 129 us; the launch traced here: 128 us
  blocking collectives  52.9 us (41%)
  starting transfers between devices  37.1 us (29%)
  waiting for transfers between devices  24.4 us (19%)
  Pallas kernels  11.2 us (9%)
  local copies, waits for them, and re-layouts  1.6 us (1%)
    all_to_all x1, blocking collectives, local(): lax.all_to_all(send, everyone, 0, 0, axis_index_groups=along_plane, tiled...  27 us
    unnamed x1, blocking collectives  25.9 us
    all_to_all x1, waiting for transfers between devices, local(): lax.all_to_all(send, everyone, 0, 0, axis_index_groups=along_plane, tiled...  16.5 us
    all_to_all x1, starting transfers between devices, local(): lax.all_to_all(send, everyone, 0, 0, axis_index_groups=along_plane, tiled...  14.2 us
    ppermute x1, starting transfers between devices, local(): other_down = lax.ppermute(own_down, 'expert', cores)  6.57 us
    all_to_all x1, waiting for transfers between devices, local(): lax.all_to_all(hidden, 'group', 0, 0, axis_index_groups=along_z, tiled=True)  5.67 us
    all_to_all x1, starting transfers between devices, local(): lax.all_to_all(hidden, 'group', 0, 0, axis_index_groups=along_z, tiled=True)  4.84 us
    ppermute x1, starting transfers between devices, local(): own_in = lax.ppermute(w_in, everyone, turn)  4.5 us
  transfers between devices with their start and end apart: 7, of which 4 were waited for; matrix products, arithmetic and copies ran while one was open for 21% of the time, Pallas kernels for 5%

profile of v4, /device:TPU:1, one launch (start us, length us, event | category | flops | bytes accessed | tf_op | source)
XLA Modules:
  0.0 128.0 jit_solution(14727430851200660364)
XLA Ops:
  0.0 4.5 %collective-permute-start = (bf16[2,448,1024]{2,1,0:T(8,128)(2,1)}, bf16[2,448,1024]{2,1,0:T(8,128)(2,1)S(1)}, u32[]{:S(2)}, u32[]{:S(2)}) collective-permute-start(bf16[2,448,1024]{2,1,0:T(8,128)(2,1)} %bitcast.18), channel_id=1, source_target_pairs={{0,0},{1,256},{2,2},{3,258},{4,4},{5,260},{6,6},{7,262},{8,8},{9,2... | collective-permute-start | bytes 5505032 | tf_op jit(solution)/shard_map/ppermute | solution.py:291
  4.5 1.8 %shard_map.55 = (bf16[64,32,128]{2,1,0:T(8,128)(2,1)S(1)}, f32[64,384]{1,0:T(8,128)S(1)}) custom-call(s32[8,384]{1,0:T(8,128)} %bitcast.14, bf16[448,384]{1,0:T(8,128)(2,1)} %bitcast.17), custom_call_target="tpu_custom_call" | custom-call | tf_op jit(solution)/shard_map/pallas_call | solution.py:292
  6.3 27.0 %all_to_all.15.arrived_ref = bf16[64,32,128]{2,1,0:T(8,128)(2,1)S(1)} all-to-all(bf16[64,32,128]{2,1,0:T(8,128)(2,1)S(1)} %get-tuple-element.14), channel_id=1, replica_groups={{0,1,2,3,4,5,6,7,8,9,10,11,12,13,14,15,16,17,18,19,20,21,22,23,24,25,26..., dimensions={0} | all-to-all | bytes 1048576 | tf_op jit(solution)/shard_map/all_to_all | solution.py:309
  33.3 0.0 collective-permute-done.own_ref
  33.3 2.4 %collective-permute-start.1 = (bf16[2,448,1024]{2,1,0:T(8,128)(2,1)S(1)}, bf16[2,448,1024]{2,1,0:T(8,128)(2,1)}, u32[]{:S(2)}, u32[]{:S(2)}) collective-permute-start(bf16[2,448,1024]{2,1,0:T(8,128)(2,1)S(1)} %collective-permute-done.own_ref), channel_id=1, source_target_pairs={{0,1},{1,0},{2,3},{3,2},{4,5},{5,4},{6,7},{7,6},{8,9},{9,8},{10,11... | collective-permute-start | bytes 5505032 | tf_op jit(solution)/shard_map/ppermute | solution.py:316
  35.8 1.9 %collective-permute-start.2 = (bf16[448,1024]{1,0:T(8,128)(2,1)}, bf16[448,1024]{1,0:T(8,128)(2,1)S(1)}, u32[]{:S(2)}, u32[]{:S(2)}) collective-permute-start(bf16[448,1024]{1,0:T(8,128)(2,1)} %bitcast.19), channel_id=1, source_target_pairs={{0,0},{1,256},{2,2},{3,258},{4,4},{5,260},{6,6},{7,262},{8,8},{9,2... | collective-permute-start | bytes 2752520 | tf_op jit(solution)/shard_map/ppermute | solution.py:317
  37.7 1.5 %shard_map.56 = (f32[312,2048]{1,0:T(8,128)S(1)}, bf16[312,512]{1,0:T(8,128)(2,1)S(1)}) custom-call(s32[1]{0:T(128)} %bitcast.side_ref, bf16[64,32,128]{2,1,0:T(8,128)(2,1)S(1)} %all_to_all.15.arrived_ref, bf16[2,448,1024]{2,1,0:T(8,128)(2,1)S(1)} %collective-permute-done.own_ref), custom_call_target="tpu_custom_call" | custom-call | tf_op jit(solution)/shard_map/pallas_call | solution.py:318
  39.2 0.1 collective-permute-done.1.other_ref
  39.3 2.3 %shard_map.57 = bf16[312,2048]{1,0:T(8,128)(2,1)S(1)} custom-call(f32[312,2048]{1,0:T(8,128)S(1)} %get-tuple-element.17.partial_ref, bf16[312,512]{1,0:T(8,128)(2,1)S(1)} %get-tuple-element.18.rows_ref, bf16[2,448,1024]{2,1,0:T(8,128)(2,1)} %collective-permute-done.1.other_ref), custom_call_target="tpu_custom_call" | custom-call | tf_op jit(solution)/shard_map/pallas_call | solution.py:326
  41.6 25.9 %fusion = bf16[40,2048]{1,0:T(8,128)(2,1)S(1)} fusion(bf16[312,2048]{1,0:T(8,128)(2,1)S(1)} %shard_map.57), kind=kCustom, calls=%all-reduce-scatter | all-reduce-scatter fusion | flops 655361 | bytes 1443840
  67.6 2.7 %collective-permute-start.4 = (bf16[7,2048]{1,0:T(8,128)(2,1)S(1)}, bf16[7,2048]{1,0:T(8,128)(2,1)S(1)}, u32[]{:S(2)}, u32[]{:S(2)}) collective-permute-start(bf16[7,2048]{1,0:T(8,128)(2,1)S(1)} %slice), channel_id=1, source_target_pairs={{0,32},{32,64},{64,96},{96,128},{128,160},{160,192},{192,224},{256... | collective-permute-start | bytes 86024
  70.2 1.3 %dynamic-slice.4 = u32[1]{0:T(128)} dynamic-slice(u32[512]{0:T(512)} %constant.10, u32[]{:S(6)} %partition-id.2), dynamic_slice_sizes={1} | dynamic-slice | bytes 12
  72.2 0.0 collective-permute-done.4
  72.2 0.2 concatenate
  72.4 0.1 constant_dynamic-slice_fusion.sums_ref
  72.5 0.0 collective-permute-done.2.own_ref
  72.5 1.0 shard_map.58
  73.5 4.8 %all-to-all-start.1 = ((bf16[8,32,1152]{2,1,0:T(8,128)(2,1)}), bf16[8,32,1152]{2,1,0:T(8,128)(2,1)S(1)}, u32[]{:S(2)}, u32[]{:S(2)}) async-start(bf16[8,32,1152]{2,1,0:T(8,128)(2,1)} %shard_map.58), calls=%async_computation.1 | async-start | bytes 1179648 | tf_op jit(solution)/shard_map/all_to_all | solution.py:338
  78.4 0.0 copy-start
  78.4 0.0 copy-start.1
  78.4 6.6 %collective-permute-start.3 = (bf16[448,1024]{1,0:T(8,128)(2,1)S(1)}, bf16[448,1024]{1,0:T(8,128)(2,1)S(1)}, u32[]{:S(2)}, u32[]{:S(2)}) collective-permute-start(bf16[448,1024]{1,0:T(8,128)(2,1)S(1)} %collective-permute-done.2.own_ref), channel_id=1, source_target_pairs={{0,1},{1,0},{2,3},{3,2},{4,5},{5,4},{6,7},{7,6},{8,9},{9,8},{10,11... | collective-permute-start | bytes 2752520 | tf_op jit(solution)/shard_map/ppermute | solution.py:333
  85.0 2.1 %collective-permute-done.3.other_ref = bf16[448,1024]{1,0:T(8,128)(2,1)S(1)} collective-permute-done((bf16[448,1024]{1,0:T(8,128)(2,1)S(1)}, bf16[448,1024]{1,0:T(8,128)(2,1)S(1)}, u32[]{:S(2)}, u32[]{:S(2)}) %collective-permute-start.3) | collective-permute-done | bytes 917536 | tf_op jit(solution)/shard_map/ppermute | solution.py:333
  87.0 5.7 %all-to-all-done.1.hidden_ref = bf16[8,32,1152]{2,1,0:T(8,128)(2,1)S(1)} async-done(((bf16[8,32,1152]{2,1,0:T(8,128)(2,1)}), bf16[8,32,1152]{2,1,0:T(8,128)(2,1)S(1)}, u32[]{:S(2)}, u32[]{:S(2)}) %all-to-all-start.1) | async-done | bytes 589856 | tf_op jit(solution)/shard_map/all_to_all | solution.py:338
  92.7 2.2 %shard_map.59 = bf16[64,32,128]{2,1,0:T(8,128)(2,1)} custom-call(s32[1]{0:T(128)} %bitcast.side_ref, bf16[8,32,1152]{2,1,0:T(8,128)(2,1)S(1)} %all-to-all-done.1.hidden_ref, bf16[448,1024]{1,0:T(8,128)(2,1)S(1)} %collective-permute-done.2.own_ref, bf16[448,1024]{1,0:T(8,128)(2,1)S(1)} %collective-permute-done.3.other_ref), custom_call_target="tpu_custom_call" | custom-call | tf_op jit(solution)/shard_map/pallas_call | solution.py:339
  94.9 14.2 %all-to-all-start.2 = ((bf16[64,32,128]{2,1,0:T(8,128)(2,1)}), bf16[64,32,128]{2,1,0:T(8,128)(2,1)S(1)}, u32[]{:S(2)}, u32[]{:S(2)}) async-start(bf16[64,32,128]{2,1,0:T(8,128)(2,1)} %shard_map.59), calls=%async_computation.2 | async-start | bytes 1048576 | tf_op jit(solution)/shard_map/all_to_all | solution.py:344
  109.1 0.0 copy-done
  109.1 0.0 copy-done.1
  109.1 0.4 shard_map.60.weights_ref
  109.5 16.5 %all-to-all-done.2.back_ref = bf16[64,32,128]{2,1,0:T(8,128)(2,1)S(1)} async-done(((bf16[64,32,128]{2,1,0:T(8,128)(2,1)}), bf16[64,32,128]{2,1,0:T(8,128)(2,1)S(1)}, u32[]{:S(2)}, u32[]{:S(2)}) %all-to-all-start.2) | async-done | bytes 524320 | tf_op jit(solution)/shard_map/all_to_all | solution.py:344
  126.0 2.0 %shard_map.61 = bf16[448,384]{1,0:T(8,128)(2,1)} custom-call(bf16[64,32,128]{2,1,0:T(8,128)(2,1)S(1)} %all-to-all-done.2.back_ref, bf16[576,768]{1,0:T(8,128)(2,1)S(1)} %shard_map.60.weights_ref), custom_call_target="tpu_custom_call" | custom-call | tf_op jit(solution)/shard_map/pallas_call | solution.py:347
  (1 shorter events, 0.0 us)
Async XLA Ops:
  0.0 33.3 %collective-permute-start = (bf16[2,448,1024]{2,1,0:T(8,128)(2,1)}, bf16[2,448,1024]{2,1,0:T(8,128)(2,1)S(1)}, u32[]{:S(2)}, u32[]{:S(2)}) collective-permute-start(bf16[2,448,1024]{2,1,0:T(8,128)(2,1)} %bitcast.18), channel_id=1, source_target_pairs={{0,0},{1,256},{2,2},{3,258},{4,4},{5,260},{6,6},{7,262},{8,8},{9,2... | collective-permute-start | bytes 5505032 | tf_op jit(solution)/shard_map/ppermute | solution.py:291
  33.3 6.0 %collective-permute-start.1 = (bf16[2,448,1024]{2,1,0:T(8,128)(2,1)S(1)}, bf16[2,448,1024]{2,1,0:T(8,128)(2,1)}, u32[]{:S(2)}, u32[]{:S(2)}) collective-permute-start(bf16[2,448,1024]{2,1,0:T(8,128)(2,1)S(1)} %collective-permute-done.own_ref), channel_id=1, source_target_pairs={{0,1},{1,0},{2,3},{3,2},{4,5},{5,4},{6,7},{7,6},{8,9},{9,8},{10,11... | collective-permute-start | bytes 5505032 | tf_op jit(solution)/shard_map/ppermute | solution.py:316
  35.8 36.7 %collective-permute-start.2 = (bf16[448,1024]{1,0:T(8,128)(2,1)}, bf16[448,1024]{1,0:T(8,128)(2,1)S(1)}, u32[]{:S(2)}, u32[]{:S(2)}) collective-permute-start(bf16[448,1024]{1,0:T(8,128)(2,1)} %bitcast.19), channel_id=1, source_target_pairs={{0,0},{1,256},{2,2},{3,258},{4,4},{5,260},{6,6},{7,262},{8,8},{9,2... | collective-permute-start | bytes 2752520 | tf_op jit(solution)/shard_map/ppermute | solution.py:317
  67.6 4.6 %collective-permute-start.4 = (bf16[7,2048]{1,0:T(8,128)(2,1)S(1)}, bf16[7,2048]{1,0:T(8,128)(2,1)S(1)}, u32[]{:S(2)}, u32[]{:S(2)}) collective-permute-start(bf16[7,2048]{1,0:T(8,128)(2,1)S(1)} %slice), channel_id=1, source_target_pairs={{0,32},{32,64},{64,96},{96,128},{128,160},{160,192},{192,224},{256... | collective-permute-start | bytes 86024
  73.5 19.2 %all-to-all-start.1 = ((bf16[8,32,1152]{2,1,0:T(8,128)(2,1)}), bf16[8,32,1152]{2,1,0:T(8,128)(2,1)S(1)}, u32[]{:S(2)}, u32[]{:S(2)}) async-start(bf16[8,32,1152]{2,1,0:T(8,128)(2,1)} %shard_map.58), calls=%async_computation.1 | async-start | bytes 1179648 | tf_op jit(solution)/shard_map/all_to_all | solution.py:338
  78.4 30.7 %copy-start = (s32[384,8]{0,1:T(8,128)S(1)}, s32[384,8]{0,1:T(8,128)}, u32[]{:S(2)}) copy-start(s32[384,8]{0,1:T(8,128)} %param.6) | copy-start | bytes 36868
  78.4 30.7 %copy-start.1 = (f32[384,8]{0,1:T(8,128)S(1)}, f32[384,8]{0,1:T(8,128)}, u32[]{:S(2)}) copy-start(f32[384,8]{0,1:T(8,128)} %param.7) | copy-start | bytes 36868
  78.4 8.7 %collective-permute-start.3 = (bf16[448,1024]{1,0:T(8,128)(2,1)S(1)}, bf16[448,1024]{1,0:T(8,128)(2,1)S(1)}, u32[]{:S(2)}, u32[]{:S(2)}) collective-permute-start(bf16[448,1024]{1,0:T(8,128)(2,1)S(1)} %collective-permute-done.2.own_ref), channel_id=1, source_target_pairs={{0,1},{1,0},{2,3},{3,2},{4,5},{5,4},{6,7},{7,6},{8,9},{9,8},{10,11... | collective-permute-start | bytes 2752520 | tf_op jit(solution)/shard_map/ppermute | solution.py:333
  94.9 31.1 %all-to-all-start.2 = ((bf16[64,32,128]{2,1,0:T(8,128)(2,1)}), bf16[64,32,128]{2,1,0:T(8,128)(2,1)S(1)}, u32[]{:S(2)}, u32[]{:S(2)}) async-start(bf16[64,32,128]{2,1,0:T(8,128)(2,1)} %shard_map.59), calls=%async_computation.2 | async-start | bytes 1048576 | tf_op jit(solution)/shard_map/all_to_all | solution.py:344

commit v5 on v4

--- a/solution.py
+++ b/solution.py
@@ -86,24 +86,26 @@
     return (index & (EXPERTS - PAIR)) | (index >> 5)
 
 
-def dispatch_kernel(ids_hbm, tokens_hbm, send_ref, slot_ref, ids_ref, tokens_ref, ids_sem, tokens_sem):
+def slots(ids_ref, label):
+    count = ids_ref.shape[1]
+    chosen = jnp.zeros(label.shape, F32)
+    for pick in range(ids_ref.shape[0]):
+        chosen = jnp.where(ids_ref[pick : pick + 1, :] == label, 1.0, chosen)
+    before = lax.broadcasted_iota(jnp.int32, (count, count), 0) < lax.broadcasted_iota(
+        jnp.int32, (count, count), 1
+    )
+    earlier = jnp.dot(chosen.astype(BF16), before.astype(BF16), preferred_element_type=F32)
+    return jnp.where(chosen > 0.0, earlier, -1.0)
+
+
+def dispatch_kernel(ids_hbm, tokens_hbm, send_ref, ids_ref, tokens_ref, ids_sem, tokens_sem):
     ids_copy = pltpu.make_async_copy(ids_hbm, ids_ref, ids_sem)
     tokens_copy = pltpu.make_async_copy(tokens_hbm, tokens_ref, tokens_sem)
     ids_copy.start()
     tokens_copy.start()
     count = ids_ref.shape[1]
     ids_copy.wait()
-    label = labels((PAIR * EXPERTS, count))
-    chosen = jnp.zeros(label.shape, F32)
-    for pick in range(ids_ref.shape[0]):
-        chosen = jnp.where(ids_ref[pick : pick + 1, :] == label, 1.0, chosen)
-    before = lax.broadcasted_iota(jnp.int32, (count, count), 0) < lax.broadcasted_iota(
-        jnp.int32, (count, count), 1
-    )
-    earlier = jnp.dot(chosen.astype(BF16), before.astype(BF16), preferred_element_type=F32)
-    slot = jnp.where(chosen > 0.0, earlier, -1.0)
-    slot_ref[...] = slot
-    every = eightfold(slot)
+    every = eightfold(slots(ids_ref, labels((PAIR * EXPERTS, count))))
     first = halves(every.shape[0], 3)
     place = (row_of_eight((every.shape[0], 1)) + first).astype(F32)
     tokens_copy.wait()
@@ -119,26 +121,27 @@
         send_ref[EXPERTS * chip : EXPERTS * chip + EXPERTS] = pack(main[rows], last[rows])
 
 
-def weights_kernel(ids_ref, combine_ref, slot_ref, weights_ref):
-    slot = slot_ref[...]
-    label = labels(slot.shape)
+def weights_kernel(core_ref, ids_ref, combine_ref, weights_ref):
+    core = core_ref[0]
+    index = lax.broadcasted_iota(jnp.int32, (PAIR * EXPERTS, ids_ref.shape[1]), 0)
+    label = 2 * (index & 15) + ((index >> 4) & 1)
+    slot = slots(ids_ref, label)
     weight = jnp.zeros(slot.shape, F32)
     for pick in range(ids_ref.shape[0]):
         weight = jnp.where(
             ids_ref[pick : pick + 1, :] == label, combine_ref[pick : pick + 1, :], weight
         )
-    every, each = eightfold(slot), eightfold(weight)
-    place = (row_of_eight((every.shape[0], 1)) + halves(every.shape[0], 3)).astype(F32)
-    main = jnp.where(every == place, each, 0.0)
-    last = jnp.where(slot == (halves(slot.shape[0], 0) + 8).astype(F32), weight, 0.0)
-    for chip in range(PAIR):
-        both = jnp.concatenate(
-            [main[MAIN * chip : MAIN * chip + MAIN], last[EXPERTS * chip : EXPERTS * chip + EXPERTS]],
-            axis=0,
-        )
+    for part in range(PAIR):
+        first = (HALF * (core if part == 0 else 1 - core)).astype(F32)
+        own = slice(EXPERTS * part, EXPERTS * part + EXPERTS)
+        every, each = eightfold(slot[own]), eightfold(weight[own])
+        place = row_of_eight((MAIN, 1)).astype(F32) + first
+        main = jnp.where(every == place, each, 0.0)
+        last = jnp.where(slot[own] == first + 8.0, weight[own], 0.0)
+        both = jnp.concatenate([main, last], axis=0)
         high = both.astype(BF16)
         low = (both - high.astype(F32)).astype(BF16)
-        weights_ref[ROWS * chip : ROWS * chip + ROWS] = jnp.concatenate([high, low], axis=1)
+        weights_ref[part] = jnp.concatenate([high, low], axis=1)
 
 
 def ordered(count, blocks, column, last):
@@ -159,8 +162,8 @@
     return chosen.astype(BF16)
 
 
-def own_gate_up_kernel(side_ref, arrived_ref, own_ref, partial_ref, rows_ref):
-    side = side_ref[0]
+def own_gate_up_kernel(core_ref, arrived_ref, own_ref, partial_ref, rows_ref):
+    side = 1 - core_ref[0]
     column = lax.broadcasted_iota(jnp.int32, (SHARD * DEPTH, MAIN), 1)
     take_main = ordered(SHARD * DEPTH, DEPTH, column, False)
     take_last = ordered(SHARD * DEPTH, DEPTH, column, True)
@@ -235,23 +238,35 @@
     return jnp.concatenate([main, last], axis=0)
 
 
-def down_kernel(side_ref, hidden_ref, own_ref, other_ref, send_ref):
-    side = side_ref[0]
+def down_kernel(core_ref, hidden_ref, own_ref, other_ref, send_ref):
+    core = core_ref[0]
     hidden = gathered_hidden(hidden_ref)
-    for ref, where in ((own_ref, side), (other_ref, 1 - side)):
+    chips = EXPERTS // 2
+    for ref, where in ((own_ref, 1 - core), (other_ref, core)):
         down = jnp.concatenate(
             [ref[...], jnp.zeros((PADDED - WIDTH, ref.shape[1]), BF16)], axis=0
         )
         result = lax.dot_general(hidden, down, NT, preferred_element_type=F32).astype(BF16)
         last = jnp.dot(spread(EXPERTS), result[MAIN:], preferred_element_type=F32)
-        send_ref[pl.ds(where * EXPERTS, EXPERTS)] = pack(result[:MAIN].astype(F32), last)
-
-
-def combine_kernel(back_ref, weights_ref, out_ref):
-    rows = jnp.concatenate([unpack(back_ref[:EXPERTS]), unpack(back_ref[EXPERTS:])], axis=0)
-    routed = lax.dot_general(rows, weights_ref[...], TN, preferred_element_type=F32)
+        blocks = pack(result[:MAIN].astype(F32), last).reshape(chips, 2, 32, 128)
+        at = pl.ds(where * chips, chips)
+        send_ref[at, pl.ds(core, 1)] = blocks[:, 0:1]
+        send_ref[at, pl.ds(1 - core, 1)] = blocks[:, 1:2]
+
+
+def kept_kernel(back_ref, weights_ref, partial_ref):
+    partial_ref[...] = lax.dot_general(
+        unpack(back_ref[:, 0]), weights_ref[0], TN, preferred_element_type=F32
+    )[:WIDTH]
+
+
+def combine_kernel(partial_ref, came_ref, weights_ref, out_ref):
+    routed = partial_ref[...]
+    routed += lax.dot_general(
+        unpack(came_ref[...]), weights_ref[1], TN, preferred_element_type=F32
+    )[:WIDTH]
     count = out_ref.shape[1]
-    out_ref[...] = (routed[:WIDTH, :count] + routed[:WIDTH, count:]).astype(BF16)
+    out_ref[...] = (routed[:, :count] + routed[:, count:]).astype(BF16)
 
 
 def call(kernel, out, **more):
@@ -266,15 +281,20 @@
 def local(tokens, expert_ids, combine, w_in, w_down):
     count = tokens.shape[0]
     hidden_units = w_down.shape[1]
-    side = (lax.axis_index("expert") & 1).astype(jnp.int32).reshape(1)
+    core = (lax.axis_index("expert") & 1).astype(jnp.int32).reshape(1)
     everyone = ("group", "expert")
     along_z = [[x * DEPTH + z for z in range(DEPTH)] for x in range(PAIR)]
     along_plane = [
         [(x * DEPTH + z) * EXPERTS + e for x in range(PAIR) for e in range(EXPERTS)]
         for z in range(DEPTH)
     ]
+    along_core = [
+        [(x * DEPTH + z) * EXPERTS + 2 * y + c for x in range(PAIR) for y in range(EXPERTS // 2)]
+        for z in range(DEPTH)
+        for c in range(2)
+    ]
     turn = [
-        ((x * DEPTH + z) * EXPERTS + 2 * y + c, (c * DEPTH + z) * EXPERTS + 2 * y + x)
+        ((x * DEPTH + z) * EXPERTS + 2 * y + c, (c * DEPTH + z) * EXPERTS + 2 * y + 1 - x)
         for x in range(PAIR)
         for z in range(DEPTH)
         for y in range(EXPERTS // 2)
@@ -289,12 +309,9 @@
     packed = (PAIR * EXPERTS, 32, 128)
 
     own_in = lax.ppermute(w_in, everyone, turn)
-    send, slot = call(
+    send = call(
         dispatch_kernel,
-        (
-            jax.ShapeDtypeStruct(packed, BF16),
-            jax.ShapeDtypeStruct((PAIR * EXPERTS, count), F32),
-        ),
+        jax.ShapeDtypeStruct(packed, BF16),
         in_specs=[pl.BlockSpec(memory_space=pltpu.HBM)] * 2,
         scratch_shapes=[
             pltpu.VMEM(ids.shape, jnp.int32),
@@ -309,9 +326,6 @@
     arrived = lax.all_to_all(
         send, everyone, 0, 0, axis_index_groups=along_plane, tiled=True
     )
-    weights = call(weights_kernel, jax.ShapeDtypeStruct((PAIR * ROWS, 2 * count), BF16))(
-        ids, combine, slot
-    )
     own_in, w_down, arrived = lax.optimization_barrier((own_in, w_down, arrived))
     other_in = lax.ppermute(own_in, "expert", cores)
     own_down = lax.ppermute(w_down, everyone, turn)
@@ -322,7 +336,7 @@
             jax.ShapeDtypeStruct((SHARD * DEPTH, PADDED), BF16),
         ),
         in_specs=[scalar, whole, whole],
-    )(side, arrived, own_in)
+    )(core, arrived, own_in)
     terms = call(
         other_gate_up_kernel, jax.ShapeDtypeStruct((SHARD * DEPTH, 2 * hidden_units), BF16)
     )(partial, rows, other_in)
@@ -338,13 +352,20 @@
     hidden = lax.all_to_all(hidden, "group", 0, 0, axis_index_groups=along_z, tiled=True)
     send = call(
         down_kernel,
-        jax.ShapeDtypeStruct(packed, BF16),
+        jax.ShapeDtypeStruct((EXPERTS, 2, 32, 128), BF16),
         in_specs=[scalar, whole, whole, whole],
-    )(side, hidden, own_down, other_down)
-    back = lax.all_to_all(
-        send, everyone, 0, 0, axis_index_groups=along_plane, tiled=True
-    )
-    routed = call(combine_kernel, jax.ShapeDtypeStruct((WIDTH, count), BF16))(back, weights)
+    )(core, hidden, own_down, other_down)
+    back = lax.all_to_all(send, everyone, 0, 0, axis_index_groups=along_core, tiled=True)
+    came = lax.ppermute(back[:, 1], "expert", cores)
+    weights = call(
+        weights_kernel,
+        jax.ShapeDtypeStruct((PAIR, ROWS, 2 * count), BF16),
+        in_specs=[scalar, whole, whole],
+    )(core, ids, combine)
+    partial = call(kept_kernel, jax.ShapeDtypeStruct((WIDTH, 2 * count), F32))(back, weights)
+    routed = call(combine_kernel, jax.ShapeDtypeStruct((WIDTH, count), BF16))(
+        partial, came, weights
+    )
     return routed.T
 
 

time: 129 us -> 128 us (level)
  blocking collectives: 52.9 us -> 75.2 us
  waiting for transfers between devices: 24.4 us -> 9.21 us
  starting transfers between devices: 37.1 us -> 29.9 us
    all_to_all x0 -> x1, blocking collectives: none -> 20.2 us  [local(): lax.all_to_all(send, everyone, 0, 0, axis_index_groups=along_core, tiled=...]
    all_to_all x1 -> x0, waiting for transfers between devices: 16.5 us -> none  [local(): lax.all_to_all(send, everyone, 0, 0, axis_index_groups=along_plane, tiled...]
    all_to_all x1 -> x0, starting transfers between devices: 14.2 us -> none  [local(): lax.all_to_all(send, everyone, 0, 0, axis_index_groups=along_plane, tiled...]
    ppermute x0 -> x1, starting transfers between devices: none -> 8.45 us  [local(): came = lax.ppermute(back[:, 1], 'expert', cores)]
    all_to_all x1, blocking collectives: 27 us -> 31.3 us  [local(): lax.all_to_all(send, everyone, 0, 0, axis_index_groups=along_plane, tiled...]
    unnamed x1, blocking collectives: 25.9 us -> 23.7 us
    unnamed x1, starting transfers between devices: 2.66 us -> 1.29 us
    all_to_all x1, waiting for transfers between devices: 5.67 us -> 7.03 us  [local(): lax.all_to_all(hidden, 'group', 0, 0, axis_index_groups=along_z, tiled=True)]
  transfers between devices with their start and end apart: 7 -> 7, of which waited for: 4 -> 3; matrix products, arithmetic and copies ran while one was open for 21% -> 20% of each run, Pallas kernels for 5% -> 5%
where the time goes in v5:
time: 128 us
  blocking collectives  75.2 us (59%)
  starting transfers between devices  29.9 us (23%)
  Pallas kernels  10.9 us (9%)
  waiting for transfers between devices  9.21 us (7%)
  local copies, waits for them, and re-layouts  1.67 us (1%)
    all_to_all x1, blocking collectives, local(): lax.all_to_all(send, everyone, 0, 0, axis_index_groups=along_plane, tiled...  31.3 us
    unnamed x1, blocking collectives  23.7 us
    all_to_all x1, blocking collectives, local(): lax.all_to_all(send, everyone, 0, 0, axis_index_groups=along_core, tiled=...  20.2 us
    ppermute x1, starting transfers between devices, local(): came = lax.ppermute(back[:, 1], 'expert', cores)  8.45 us
    all_to_all x1, waiting for transfers between devices, local(): lax.all_to_all(hidden, 'group', 0, 0, axis_index_groups=along_z, tiled=True)  7.03 us
    ppermute x1, starting transfers between devices, local(): other_down = lax.ppermute(own_down, 'expert', cores)  5.95 us
    all_to_all x1, starting transfers between devices, local(): lax.all_to_all(hidden, 'group', 0, 0, axis_index_groups=along_z, tiled=True)  5.73 us
    ppermute x1, starting transfers between devices, local(): own_in = lax.ppermute(w_in, everyone, turn)  3.94 us
  transfers between devices with their start and end apart: 7, of which 3 were waited for; matrix products, arithmetic and copies ran while one was open for 20% of the time, Pallas kernels for 5%

profile of v5, /device:TPU:1, one launch (start us, length us, event | category | flops | bytes accessed | tf_op | source)
XLA Modules:
  0.0 127.8 jit_solution(16411243576553895907)
XLA Ops:
  0.0 3.9 %collective-permute-start = (bf16[2,448,1024]{2,1,0:T(8,128)(2,1)}, bf16[2,448,1024]{2,1,0:T(8,128)(2,1)S(1)}, u32[]{:S(2)}, u32[]{:S(2)}) collective-permute-start(bf16[2,448,1024]{2,1,0:T(8,128)(2,1)} %bitcast.22), channel_id=1, source_target_pairs={{0,1},{1,257},{2,3},{3,259},{4,5},{5,261},{6,7},{7,263},{8,9},{9,2... | collective-permute-start | bytes 5505032 | tf_op jit(solution)/shard_map/ppermute | solution.py:311
  3.9 1.8 %shard_map.55 = bf16[64,32,128]{2,1,0:T(8,128)(2,1)S(1)} custom-call(s32[8,384]{1,0:T(8,128)} %bitcast.18, bf16[448,384]{1,0:T(8,128)(2,1)} %bitcast.21), custom_call_target="tpu_custom_call" | custom-call | tf_op jit(solution)/shard_map/pallas_call | solution.py:312
  5.8 31.3 %all_to_all.15.arrived_ref = bf16[64,32,128]{2,1,0:T(8,128)(2,1)S(1)} all-to-all(bf16[64,32,128]{2,1,0:T(8,128)(2,1)S(1)} %shard_map.55), channel_id=1, replica_groups={{0,1,2,3,4,5,6,7,8,9,10,11,12,13,14,15,16,17,18,19,20,21,22,23,24,25,26..., dimensions={0} | all-to-all | bytes 1048576 | tf_op jit(solution)/shard_map/all_to_all | solution.py:326
  37.1 0.0 collective-permute-done.own_ref
  37.1 2.6 %collective-permute-start.1 = (bf16[2,448,1024]{2,1,0:T(8,128)(2,1)S(1)}, bf16[2,448,1024]{2,1,0:T(8,128)(2,1)}, u32[]{:S(2)}, u32[]{:S(2)}) collective-permute-start(bf16[2,448,1024]{2,1,0:T(8,128)(2,1)S(1)} %collective-permute-done.own_ref), channel_id=1, source_target_pairs={{0,1},{1,0},{2,3},{3,2},{4,5},{5,4},{6,7},{7,6},{8,9},{9,8},{10,11... | collective-permute-start | bytes 5505032 | tf_op jit(solution)/shard_map/ppermute | solution.py:330
  39.7 1.9 %collective-permute-start.2 = (bf16[448,1024]{1,0:T(8,128)(2,1)}, bf16[448,1024]{1,0:T(8,128)(2,1)S(1)}, u32[]{:S(2)}, u32[]{:S(2)}) collective-permute-start(bf16[448,1024]{1,0:T(8,128)(2,1)} %bitcast.23), channel_id=1, source_target_pairs={{0,1},{1,257},{2,3},{3,259},{4,5},{5,261},{6,7},{7,263},{8,9},{9,2... | collective-permute-start | bytes 2752520 | tf_op jit(solution)/shard_map/ppermute | solution.py:331
  41.7 1.5 %shard_map.56 = (f32[312,2048]{1,0:T(8,128)S(1)}, bf16[312,512]{1,0:T(8,128)(2,1)S(1)}) custom-call(s32[1]{0:T(128)} %bitcast.core_ref, bf16[64,32,128]{2,1,0:T(8,128)(2,1)S(1)} %all_to_all.15.arrived_ref, bf16[2,448,1024]{2,1,0:T(8,128)(2,1)S(1)} %collective-permute-done.own_ref), custom_call_target="tpu_custom_call" | custom-call | tf_op jit(solution)/shard_map/pallas_call | solution.py:332
  43.1 0.1 collective-permute-done.1.other_ref
  43.2 2.3 %shard_map.57 = bf16[312,2048]{1,0:T(8,128)(2,1)S(1)} custom-call(f32[312,2048]{1,0:T(8,128)S(1)} %get-tuple-element.14.partial_ref, bf16[312,512]{1,0:T(8,128)(2,1)S(1)} %get-tuple-element.15.rows_ref, bf16[2,448,1024]{2,1,0:T(8,128)(2,1)} %collective-permute-done.1.other_ref), custom_call_target="tpu_custom_call" | custom-call | tf_op jit(solution)/shard_map/pallas_call | solution.py:340
  45.6 23.7 %fusion = bf16[40,2048]{1,0:T(8,128)(2,1)S(1)} fusion(bf16[312,2048]{1,0:T(8,128)(2,1)S(1)} %shard_map.57), kind=kCustom, calls=%all-reduce-scatter | all-reduce-scatter fusion | flops 655361 | bytes 1443840
  69.3 1.3 %collective-permute-start.5 = (bf16[7,2048]{1,0:T(8,128)(2,1)S(1)}, bf16[7,2048]{1,0:T(8,128)(2,1)S(1)}, u32[]{:S(2)}, u32[]{:S(2)}) collective-permute-start(bf16[7,2048]{1,0:T(8,128)(2,1)S(1)} %slice.5), channel_id=1, source_target_pairs={{0,32},{32,64},{64,96},{96,128},{128,160},{160,192},{192,224},{256... | collective-permute-start | bytes 86024
  70.6 1.3 %dynamic-slice.4 = u32[1]{0:T(128)} dynamic-slice(u32[512]{0:T(512)} %constant.10, u32[]{:S(6)} %partition-id.2), dynamic_slice_sizes={1} | dynamic-slice | bytes 12
  72.6 0.0 collective-permute-done.5
  72.6 0.2 concatenate
  72.9 0.1 constant_dynamic-slice_fusion.sums_ref
  72.9 0.0 collective-permute-done.2.own_ref
  72.9 1.0 shard_map.58
  74.0 5.7 %all-to-all-start.1 = ((bf16[8,32,1152]{2,1,0:T(8,128)(2,1)}), bf16[8,32,1152]{2,1,0:T(8,128)(2,1)S(1)}, u32[]{:S(2)}, u32[]{:S(2)}) async-start(bf16[8,32,1152]{2,1,0:T(8,128)(2,1)} %shard_map.58), calls=%async_computation.1 | async-start | bytes 1179648 | tf_op jit(solution)/shard_map/all_to_all | solution.py:352
  79.7 6.0 %collective-permute-start.3 = (bf16[448,1024]{1,0:T(8,128)(2,1)S(1)}, bf16[448,1024]{1,0:T(8,128)(2,1)S(1)}, u32[]{:S(2)}, u32[]{:S(2)}) collective-permute-start(bf16[448,1024]{1,0:T(8,128)(2,1)S(1)} %collective-permute-done.2.own_ref), channel_id=1, source_target_pairs={{0,1},{1,0},{2,3},{3,2},{4,5},{5,4},{6,7},{7,6},{8,9},{9,8},{10,11... | collective-permute-start | bytes 2752520 | tf_op jit(solution)/shard_map/ppermute | solution.py:347
  85.7 2.1 %collective-permute-done.3.other_ref = bf16[448,1024]{1,0:T(8,128)(2,1)S(1)} collective-permute-done((bf16[448,1024]{1,0:T(8,128)(2,1)S(1)}, bf16[448,1024]{1,0:T(8,128)(2,1)S(1)}, u32[]{:S(2)}, u32[]{:S(2)}) %collective-permute-start.3) | collective-permute-done | bytes 917536 | tf_op jit(solution)/shard_map/ppermute | solution.py:347
  87.7 7.0 %all-to-all-done.1.hidden_ref = bf16[8,32,1152]{2,1,0:T(8,128)(2,1)S(1)} async-done(((bf16[8,32,1152]{2,1,0:T(8,128)(2,1)}), bf16[8,32,1152]{2,1,0:T(8,128)(2,1)S(1)}, u32[]{:S(2)}, u32[]{:S(2)}) %all-to-all-start.1) | async-done | bytes 589856 | tf_op jit(solution)/shard_map/all_to_all | solution.py:352
  94.8 1.4 %shard_map.59 = bf16[32,2,32,128]{3,2,1,0:T(8,128)(2,1)S(1)} custom-call(s32[1]{0:T(128)} %bitcast.core_ref, bf16[8,32,1152]{2,1,0:T(8,128)(2,1)S(1)} %all-to-all-done.1.hidden_ref, bf16[448,1024]{1,0:T(8,128)(2,1)S(1)} %collective-permute-done.2.own_ref, bf16[448,1024]{1,0:T(8,128)(2,1)S(1)} %collective-permute-done.3.other_ref), custom_call_target="tpu_custom_call" | custom-call | tf_op jit(solution)/shard_map/pallas_call | solution.py:353
  96.1 0.0 copy-start
  96.1 0.0 copy-start.1
  96.2 20.2 %all_to_all.16.back_ref = bf16[32,2,32,128]{3,2,1,0:T(8,128)(2,1)S(1)} all-to-all(bf16[32,2,32,128]{3,2,1,0:T(8,128)(2,1)S(1)} %shard_map.59), channel_id=1, replica_groups={{0,2,4,6,8,10,12,14,16,18,20,22,24,26,28,30,256,258,260,262,264,266,268..., dimensions={0} | all-to-all | bytes 1048576 | tf_op jit(solution)/shard_map/all_to_all | solution.py:358
  116.4 8.5 %collective-permute-start.4 = (bf16[32,32,128]{2,1,0:T(8,128)(2,1)S(1)}, bf16[32,32,128]{2,1,0:T(8,128)(2,1)S(1)}, u32[]{:S(2)}, u32[]{:S(2)}) collective-permute-start(bf16[32,32,128]{2,1,0:T(8,128)(2,1)S(1)} %slice_bitcast_fusion), channel_id=1, source_target_pairs={{0,1},{1,0},{2,3},{3,2},{4,5},{5,4},{6,7},{7,6},{8,9},{9,8},{10,11... | collective-permute-start | bytes 786440 | tf_op jit(solution)/shard_map/ppermute | solution.py:359
  124.9 0.0 copy-done
  124.9 0.0 copy-done.1
  124.9 0.5 shard_map.60.weights_ref
  125.4 0.8 shard_map.61.partial_ref
  126.3 0.0 collective-permute-done.4.came_ref
  126.3 1.6 %shard_map.62 = bf16[448,384]{1,0:T(8,128)(2,1)} custom-call(f32[448,768]{1,0:T(8,128)S(1)} %shard_map.61.partial_ref, bf16[32,32,128]{2,1,0:T(8,128)(2,1)S(1)} %collective-permute-done.4.came_ref, bf16[2,288,768]{2,1,0:T(8,128)(2,1)S(1)} %shard_map.60.weights_ref), custom_call_target="tpu_custom_call" | custom-call | tf_op jit(solution)/shard_map/pallas_call | solution.py:366
  (2 shorter events, 0.0 us)
Async XLA Ops:
  0.0 37.1 %collective-permute-start = (bf16[2,448,1024]{2,1,0:T(8,128)(2,1)}, bf16[2,448,1024]{2,1,0:T(8,128)(2,1)S(1)}, u32[]{:S(2)}, u32[]{:S(2)}) collective-permute-start(bf16[2,448,1024]{2,1,0:T(8,128)(2,1)} %bitcast.22), channel_id=1, source_target_pairs={{0,1},{1,257},{2,3},{3,259},{4,5},{5,261},{6,7},{7,263},{8,9},{9,2... | collective-permute-start | bytes 5505032 | tf_op jit(solution)/shard_map/ppermute | solution.py:311
  37.1 6.2 %collective-permute-start.1 = (bf16[2,448,1024]{2,1,0:T(8,128)(2,1)S(1)}, bf16[2,448,1024]{2,1,0:T(8,128)(2,1)}, u32[]{:S(2)}, u32[]{:S(2)}) collective-permute-start(bf16[2,448,1024]{2,1,0:T(8,128)(2,1)S(1)} %collective-permute-done.own_ref), channel_id=1, source_target_pairs={{0,1},{1,0},{2,3},{3,2},{4,5},{5,4},{6,7},{7,6},{8,9},{9,8},{10,11... | collective-permute-start | bytes 5505032 | tf_op jit(solution)/shard_map/ppermute | solution.py:330
  39.7 33.2 %collective-permute-start.2 = (bf16[448,1024]{1,0:T(8,128)(2,1)}, bf16[448,1024]{1,0:T(8,128)(2,1)S(1)}, u32[]{:S(2)}, u32[]{:S(2)}) collective-permute-start(bf16[448,1024]{1,0:T(8,128)(2,1)} %bitcast.23), channel_id=1, source_target_pairs={{0,1},{1,257},{2,3},{3,259},{4,5},{5,261},{6,7},{7,263},{8,9},{9,2... | collective-permute-start | bytes 2752520 | tf_op jit(solution)/shard_map/ppermute | solution.py:331
  69.3 3.3 %collective-permute-start.5 = (bf16[7,2048]{1,0:T(8,128)(2,1)S(1)}, bf16[7,2048]{1,0:T(8,128)(2,1)S(1)}, u32[]{:S(2)}, u32[]{:S(2)}) collective-permute-start(bf16[7,2048]{1,0:T(8,128)(2,1)S(1)} %slice.5), channel_id=1, source_target_pairs={{0,32},{32,64},{64,96},{96,128},{128,160},{160,192},{192,224},{256... | collective-permute-start | bytes 86024
  74.0 20.8 %all-to-all-start.1 = ((bf16[8,32,1152]{2,1,0:T(8,128)(2,1)}), bf16[8,32,1152]{2,1,0:T(8,128)(2,1)S(1)}, u32[]{:S(2)}, u32[]{:S(2)}) async-start(bf16[8,32,1152]{2,1,0:T(8,128)(2,1)} %shard_map.58), calls=%async_computation.1 | async-start | bytes 1179648 | tf_op jit(solution)/shard_map/all_to_all | solution.py:352
  79.7 8.0 %collective-permute-start.3 = (bf16[448,1024]{1,0:T(8,128)(2,1)S(1)}, bf16[448,1024]{1,0:T(8,128)(2,1)S(1)}, u32[]{:S(2)}, u32[]{:S(2)}) collective-permute-start(bf16[448,1024]{1,0:T(8,128)(2,1)S(1)} %collective-permute-done.2.own_ref), channel_id=1, source_target_pairs={{0,1},{1,0},{2,3},{3,2},{4,5},{5,4},{6,7},{7,6},{8,9},{9,8},{10,11... | collective-permute-start | bytes 2752520 | tf_op jit(solution)/shard_map/ppermute | solution.py:347
  96.1 28.8 %copy-start = (s32[384,8]{0,1:T(8,128)S(1)}, s32[384,8]{0,1:T(8,128)}, u32[]{:S(2)}) copy-start(s32[384,8]{0,1:T(8,128)} %param.6) | copy-start | bytes 36868
  96.1 28.8 %copy-start.1 = (f32[384,8]{0,1:T(8,128)S(1)}, f32[384,8]{0,1:T(8,128)}, u32[]{:S(2)}) copy-start(f32[384,8]{0,1:T(8,128)} %param.7) | copy-start | bytes 36868
  116.4 9.8 %collective-permute-start.4 = (bf16[32,32,128]{2,1,0:T(8,128)(2,1)S(1)}, bf16[32,32,128]{2,1,0:T(8,128)(2,1)S(1)}, u32[]{:S(2)}, u32[]{:S(2)}) collective-permute-start(bf16[32,32,128]{2,1,0:T(8,128)(2,1)S(1)} %slice_bitcast_fusion), channel_id=1, source_target_pairs={{0,1},{1,0},{2,3},{3,2},{4,5},{5,4},{6,7},{7,6},{8,9},{9,8},{10,11... | collective-permute-start | bytes 786440 | tf_op jit(solution)/shard_map/ppermute | solution.py:359

commit v6 on v5

--- a/solution.py
+++ b/solution.py
@@ -98,12 +98,13 @@
     return jnp.where(chosen > 0.0, earlier, -1.0)
 
 
-def dispatch_kernel(ids_hbm, tokens_hbm, send_ref, ids_ref, tokens_ref, ids_sem, tokens_sem):
+def dispatch_kernel(ids_hbm, tokens_hbm, send_ref, mark_ref, ids_ref, tokens_ref, ids_sem, tokens_sem):
     ids_copy = pltpu.make_async_copy(ids_hbm, ids_ref, ids_sem)
     tokens_copy = pltpu.make_async_copy(tokens_hbm, tokens_ref, tokens_sem)
     ids_copy.start()
     tokens_copy.start()
     count = ids_ref.shape[1]
+    mark_ref[...] = jnp.zeros(mark_ref.shape, F32)
     ids_copy.wait()
     every = eightfold(slots(ids_ref, labels((PAIR * EXPERTS, count))))
     first = halves(every.shape[0], 3)
@@ -121,7 +122,8 @@
         send_ref[EXPERTS * chip : EXPERTS * chip + EXPERTS] = pack(main[rows], last[rows])
 
 
-def weights_kernel(core_ref, ids_ref, combine_ref, weights_ref):
+def weights_kernel(core_ref, mark_ref, ids_ref, combine_ref, weights_ref):
+    del mark_ref
     core = core_ref[0]
     index = lax.broadcasted_iota(jnp.int32, (PAIR * EXPERTS, ids_ref.shape[1]), 0)
     label = 2 * (index & 15) + ((index >> 4) & 1)
@@ -162,7 +164,13 @@
     return chosen.astype(BF16)
 
 
-def own_gate_up_kernel(core_ref, arrived_ref, own_ref, partial_ref, rows_ref):
+def own_gate_up_kernel(core_ref, arrived_ref, own_hbm, partial_ref, rows_ref, own_ref, sems):
+    copies = [
+        pltpu.make_async_copy(own_hbm.at[index], own_ref.at[index], sems.at[index])
+        for index in range(2)
+    ]
+    for copy in copies:
+        copy.start()
     side = 1 - core_ref[0]
     column = lax.broadcasted_iota(jnp.int32, (SHARD * DEPTH, MAIN), 1)
     take_main = ordered(SHARD * DEPTH, DEPTH, column, False)
@@ -176,6 +184,7 @@
     rows_ref[...] = rows[1]
     units = own_ref.shape[2]
     for index in range(2):
+        copies[index].wait()
         for start in range(0, units, PADDED):
             part = jnp.dot(
                 rows[0][:, :WIDTH],
@@ -238,11 +247,15 @@
     return jnp.concatenate([main, last], axis=0)
 
 
-def down_kernel(core_ref, hidden_ref, own_ref, other_ref, send_ref):
+def down_kernel(core_ref, hidden_ref, own_hbm, other_ref, send_ref, own_ref, sem):
+    copy = pltpu.make_async_copy(own_hbm, own_ref, sem)
+    copy.start()
     core = core_ref[0]
     hidden = gathered_hidden(hidden_ref)
     chips = EXPERTS // 2
-    for ref, where in ((own_ref, 1 - core), (other_ref, core)):
+    for ref, where in ((other_ref, core), (own_ref, 1 - core)):
+        if ref is own_ref:
+            copy.wait()
         down = jnp.concatenate(
             [ref[...], jnp.zeros((PADDED - WIDTH, ref.shape[1]), BF16)], axis=0
         )
@@ -306,12 +319,13 @@
     w_down = w_down[0].T
     scalar = pl.BlockSpec(memory_space=pltpu.SMEM)
     whole = pl.BlockSpec(memory_space=pltpu.VMEM)
+    anywhere = pl.BlockSpec(memory_space=pl.ANY)
     packed = (PAIR * EXPERTS, 32, 128)
 
     own_in = lax.ppermute(w_in, everyone, turn)
-    send = call(
+    send, mark = call(
         dispatch_kernel,
-        jax.ShapeDtypeStruct(packed, BF16),
+        (jax.ShapeDtypeStruct(packed, BF16), jax.ShapeDtypeStruct((8, 128), F32)),
         in_specs=[pl.BlockSpec(memory_space=pltpu.HBM)] * 2,
         scratch_shapes=[
             pltpu.VMEM(ids.shape, jnp.int32),
@@ -326,7 +340,7 @@
     arrived = lax.all_to_all(
         send, everyone, 0, 0, axis_index_groups=along_plane, tiled=True
     )
-    own_in, w_down, arrived = lax.optimization_barrier((own_in, w_down, arrived))
+    own_in, w_down, mark = lax.optimization_barrier((own_in, w_down, mark))
     other_in = lax.ppermute(own_in, "expert", cores)
     own_down = lax.ppermute(w_down, everyone, turn)
     partial, rows = call(
@@ -335,8 +349,12 @@
             jax.ShapeDtypeStruct((SHARD * DEPTH, 2 * hidden_units), F32),
             jax.ShapeDtypeStruct((SHARD * DEPTH, PADDED), BF16),
         ),
-        in_specs=[scalar, whole, whole],
-    )(core, arrived, own_in)
+        in_specs=[scalar, whole, anywhere],
+        scratch_shapes=[pltpu.VMEM(own_in.shape, BF16), pltpu.SemaphoreType.DMA((2,))],
+        cost_estimate=pl.CostEstimate(
+            flops=50 * 10**9, bytes_accessed=4 * 1024 * 1024, transcendentals=0
+        ),
+    )(core, arrived, pltpu.with_memory_space_constraint(own_in, pltpu.HBM))
     terms = call(
         other_gate_up_kernel, jax.ShapeDtypeStruct((SHARD * DEPTH, 2 * hidden_units), BF16)
     )(partial, rows, other_in)
@@ -353,15 +371,16 @@
     send = call(
         down_kernel,
         jax.ShapeDtypeStruct((EXPERTS, 2, 32, 128), BF16),
-        in_specs=[scalar, whole, whole, whole],
-    )(core, hidden, own_down, other_down)
+        in_specs=[scalar, whole, anywhere, whole],
+        scratch_shapes=[pltpu.VMEM(own_down.shape, BF16), pltpu.SemaphoreType.DMA],
+    )(core, hidden, pltpu.with_memory_space_constraint(own_down, pltpu.HBM), other_down)
     back = lax.all_to_all(send, everyone, 0, 0, axis_index_groups=along_core, tiled=True)
     came = lax.ppermute(back[:, 1], "expert", cores)
     weights = call(
         weights_kernel,
         jax.ShapeDtypeStruct((PAIR, ROWS, 2 * count), BF16),
-        in_specs=[scalar, whole, whole],
-    )(core, ids, combine)
+        in_specs=[scalar, whole, whole, whole],
+    )(core, mark, ids, combine)
     partial = call(kept_kernel, jax.ShapeDtypeStruct((WIDTH, 2 * count), F32))(back, weights)
     routed = call(combine_kernel, jax.ShapeDtypeStruct((WIDTH, count), BF16))(
         partial, came, weights

time: 128 us -> 127 us (level)
  blocking collectives: 75.2 us -> 42.7 us
  starting transfers between devices: 29.9 us -> 48.1 us
  waiting for transfers between devices: 9.21 us -> 21.4 us
    all_to_all x1 -> x0, blocking collectives: 31.3 us -> none  [local(): lax.all_to_all(send, everyone, 0, 0, axis_index_groups=along_plane, tiled...]
    ppermute x1, waiting for transfers between devices: 0.01 us -> 12.5 us  [local(): own_in = lax.ppermute(w_in, everyone, turn)]
    all_to_all x0 -> x1, starting transfers between devices: none -> 10.2 us  [local(): lax.all_to_all(send, everyone, 0, 0, axis_index_groups=along_plane, tiled...]
    ppermute x1, starting transfers between devices: 2.64 us -> 10.2 us  [local(): other_in = lax.ppermute(own_in, 'expert', cores)]
    unnamed x1, blocking collectives: 23.7 us -> 20.5 us
    all_to_all x1, blocking collectives: 20.2 us -> 22.1 us  [local(): lax.all_to_all(send, everyone, 0, 0, axis_index_groups=along_core, tiled=...]
    pallas_call x1, Pallas kernels: 2.34 us -> 0.9 us  [local(): call(other_gate_up_kernel, jax.ShapeDtypeStruct((SHARD * DEPTH, 2 * hidde...]
  transfers between devices with their start and end apart: 7 -> 8, of which waited for: 3 -> 3; matrix products, arithmetic and copies ran while one was open for 20% -> 17% of each run, Pallas kernels for 5% -> 6%
where the time goes in v6:
time: 127 us
  starting transfers between devices  48.1 us (38%)
  blocking collectives  42.7 us (34%)
  waiting for transfers between devices  21.4 us (17%)
  Pallas kernels  12 us (9%)
  local copies, waits for them, and re-layouts  1.66 us (1%)
    all_to_all x1, blocking collectives, local(): lax.all_to_all(send, everyone, 0, 0, axis_index_groups=along_core, tiled=...  22.1 us
    unnamed x1, blocking collectives  20.5 us
    ppermute x1, waiting for transfers between devices, local(): own_in = lax.ppermute(w_in, everyone, turn)  12.5 us
    ppermute x1, starting transfers between devices, local(): other_in = lax.ppermute(own_in, 'expert', cores)  10.2 us
    all_to_all x1, starting transfers between devices, local(): lax.all_to_all(send, everyone, 0, 0, axis_index_groups=along_plane, tiled...  10.2 us
    ppermute x1, starting transfers between devices, local(): came = lax.ppermute(back[:, 1], 'expert', cores)  8.24 us
    all_to_all x1, waiting for transfers between devices, local(): lax.all_to_all(hidden, 'group', 0, 0, axis_index_groups=along_z, tiled=True)  6.55 us
    ppermute x1, starting transfers between devices, local(): other_down = lax.ppermute(own_down, 'expert', cores)  6.09 us
  transfers between devices with their start and end apart: 8, of which 3 were waited for; matrix products, arithmetic and copies ran while one was open for 17% of the time, Pallas kernels for 6%

profile of v6, /device:TPU:1, one launch (start us, length us, event | category | flops | bytes accessed | tf_op | source)
XLA Modules:
  0.0 126.6 jit_solution(3091431689714791783)
XLA Ops:
  0.0 3.9 %collective-permute-start = (bf16[2,448,1024]{2,1,0:T(8,128)(2,1)}, bf16[2,448,1024]{2,1,0:T(8,128)(2,1)}, u32[]{:S(2)}, u32[]{:S(2)}) collective-permute-start(bf16[2,448,1024]{2,1,0:T(8,128)(2,1)} %bitcast.22), channel_id=1, source_target_pairs={{0,1},{1,257},{2,3},{3,259},{4,5},{5,261},{6,7},{7,263},{8,9},{9,2... | collective-permute-start | bytes 5505032 | tf_op jit(solution)/shard_map/ppermute | solution.py:325
  3.9 2.6 %shard_map.55 = (bf16[64,32,128]{2,1,0:T(8,128)(2,1)}, f32[8,128]{1,0:T(8,128)S(1)}) custom-call(s32[8,384]{1,0:T(8,128)} %bitcast.18, bf16[448,384]{1,0:T(8,128)(2,1)} %bitcast.21), custom_call_target="tpu_custom_call" | custom-call | tf_op jit(solution)/shard_map/pallas_call | solution.py:326
  6.6 10.2 %all-to-all-start = ((bf16[64,32,128]{2,1,0:T(8,128)(2,1)}), bf16[64,32,128]{2,1,0:T(8,128)(2,1)S(1)}, u32[]{:S(2)}, u32[]{:S(2)}) async-start(bf16[64,32,128]{2,1,0:T(8,128)(2,1)} %get-tuple-element.14), calls=%async_computation | async-start | bytes 1048576 | tf_op jit(solution)/shard_map/all_to_all | solution.py:340
  16.7 12.5 %collective-permute-done.own_hbm = bf16[2,448,1024]{2,1,0:T(8,128)(2,1)} collective-permute-done((bf16[2,448,1024]{2,1,0:T(8,128)(2,1)}, bf16[2,448,1024]{2,1,0:T(8,128)(2,1)}, u32[]{:S(2)}, u32[]{:S(2)}) %collective-permute-start) | collective-permute-done | bytes 1835040 | tf_op jit(solution)/shard_map/ppermute | solution.py:325
  29.3 10.2 %collective-permute-start.1 = (bf16[2,448,1024]{2,1,0:T(8,128)(2,1)}, bf16[2,448,1024]{2,1,0:T(8,128)(2,1)S(1)}, u32[]{:S(2)}, u32[]{:S(2)}) collective-permute-start(bf16[2,448,1024]{2,1,0:T(8,128)(2,1)} %collective-permute-done.own_hbm), channel_id=1, source_target_pairs={{0,1},{1,0},{2,3},{3,2},{4,5},{5,4},{6,7},{7,6},{8,9},{9,8},{10,11... | collective-permute-start | bytes 5505032 | tf_op jit(solution)/shard_map/ppermute | solution.py:344
  39.5 1.9 %collective-permute-start.2 = (bf16[448,1024]{1,0:T(8,128)(2,1)}, bf16[448,1024]{1,0:T(8,128)(2,1)}, u32[]{:S(2)}, u32[]{:S(2)}) collective-permute-start(bf16[448,1024]{1,0:T(8,128)(2,1)} %bitcast.23), channel_id=1, source_target_pairs={{0,1},{1,257},{2,3},{3,259},{4,5},{5,261},{6,7},{7,263},{8,9},{9,2... | collective-permute-start | bytes 2752520 | tf_op jit(solution)/shard_map/ppermute | solution.py:345
  41.4 0.0 all-to-all-done.arrived_ref
  41.4 2.6 %shard_map.56 = (f32[312,2048]{1,0:T(8,128)S(1)}, bf16[312,512]{1,0:T(8,128)(2,1)S(1)}) custom-call(s32[1]{0:T(128)} %bitcast.core_ref, bf16[64,32,128]{2,1,0:T(8,128)(2,1)S(1)} %all-to-all-done.arrived_ref, bf16[2,448,1024]{2,1,0:T(8,128)(2,1)} %collective-permute-done.own_hbm), custom_call_target="tpu_custom_call" | custom-call | flops 49999998976 | bytes 4194304 | tf_op jit(solution)/shard_map/pallas_call | solution.py:346
  44.0 0.0 collective-permute-done.1.other_ref
  44.0 0.9 shard_map.57
  44.9 20.5 %fusion = bf16[40,2048]{1,0:T(8,128)(2,1)S(1)} fusion(bf16[312,2048]{1,0:T(8,128)(2,1)S(1)} %shard_map.57), kind=kCustom, calls=%all-reduce-scatter | all-reduce-scatter fusion | flops 655361 | bytes 1443840
  65.5 2.2 %collective-permute-start.5 = (bf16[7,2048]{1,0:T(8,128)(2,1)S(1)}, bf16[7,2048]{1,0:T(8,128)(2,1)S(1)}, u32[]{:S(2)}, u32[]{:S(2)}) collective-permute-start(bf16[7,2048]{1,0:T(8,128)(2,1)S(1)} %slice.5), channel_id=1, source_target_pairs={{0,32},{32,64},{64,96},{96,128},{128,160},{160,192},{192,224},{256... | collective-permute-start | bytes 86024
  67.7 1.3 %dynamic-slice.4 = u32[1]{0:T(128)} dynamic-slice(u32[512]{0:T(512)} %constant.10, u32[]{:S(6)} %partition-id.2), dynamic_slice_sizes={1} | dynamic-slice | bytes 12
  69.6 0.0 collective-permute-done.5
  69.6 0.2 concatenate
  69.9 0.1 constant_dynamic-slice_fusion.sums_ref
  69.9 0.0 collective-permute-done.2.own_hbm
  69.9 1.0 shard_map.58
  71.0 5.4 %all-to-all-start.1 = ((bf16[8,32,1152]{2,1,0:T(8,128)(2,1)}), bf16[8,32,1152]{2,1,0:T(8,128)(2,1)S(1)}, u32[]{:S(2)}, u32[]{:S(2)}) async-start(bf16[8,32,1152]{2,1,0:T(8,128)(2,1)} %shard_map.58), calls=%async_computation.1 | async-start | bytes 1179648 | tf_op jit(solution)/shard_map/all_to_all | solution.py:370
  76.4 6.1 %collective-permute-start.3 = (bf16[448,1024]{1,0:T(8,128)(2,1)}, bf16[448,1024]{1,0:T(8,128)(2,1)S(1)}, u32[]{:S(2)}, u32[]{:S(2)}) collective-permute-start(bf16[448,1024]{1,0:T(8,128)(2,1)} %collective-permute-done.2.own_hbm), channel_id=1, source_target_pairs={{0,1},{1,0},{2,3},{3,2},{4,5},{5,4},{6,7},{7,6},{8,9},{9,8},{10,11... | collective-permute-start | bytes 2752520 | tf_op jit(solution)/shard_map/ppermute | solution.py:365
  82.5 2.3 %collective-permute-done.3.other_ref = bf16[448,1024]{1,0:T(8,128)(2,1)S(1)} collective-permute-done((bf16[448,1024]{1,0:T(8,128)(2,1)}, bf16[448,1024]{1,0:T(8,128)(2,1)S(1)}, u32[]{:S(2)}, u32[]{:S(2)}) %collective-permute-start.3) | collective-permute-done | bytes 917536 | tf_op jit(solution)/shard_map/ppermute | solution.py:365
  84.7 6.6 %all-to-all-done.1.hidden_ref = bf16[8,32,1152]{2,1,0:T(8,128)(2,1)S(1)} async-done(((bf16[8,32,1152]{2,1,0:T(8,128)(2,1)}), bf16[8,32,1152]{2,1,0:T(8,128)(2,1)S(1)}, u32[]{:S(2)}, u32[]{:S(2)}) %all-to-all-start.1) | async-done | bytes 589856 | tf_op jit(solution)/shard_map/all_to_all | solution.py:370
  91.3 2.0 %shard_map.59 = bf16[32,2,32,128]{3,2,1,0:T(8,128)(2,1)S(1)} custom-call(s32[1]{0:T(128)} %bitcast.core_ref, bf16[8,32,1152]{2,1,0:T(8,128)(2,1)S(1)} %all-to-all-done.1.hidden_ref, bf16[448,1024]{1,0:T(8,128)(2,1)} %collective-permute-done.2.own_hbm, bf16[448,1024]{1,0:T(8,128)(2,1)S(1)} %collective-permute-done.3.other_ref), custom_call_target="tpu_custom_call" | custom-call | tf_op jit(solution)/shard_map/pallas_call | solution.py:371
  93.3 0.0 copy-start
  93.3 0.0 copy-start.1
  93.3 22.1 %all_to_all.15.back_ref = bf16[32,2,32,128]{3,2,1,0:T(8,128)(2,1)S(1)} all-to-all(bf16[32,2,32,128]{3,2,1,0:T(8,128)(2,1)S(1)} %shard_map.59), channel_id=1, replica_groups={{0,2,4,6,8,10,12,14,16,18,20,22,24,26,28,30,256,258,260,262,264,266,268..., dimensions={0} | all-to-all | bytes 1048576 | tf_op jit(solution)/shard_map/all_to_all | solution.py:377
  115.5 8.2 %collective-permute-start.4 = (bf16[32,32,128]{2,1,0:T(8,128)(2,1)S(1)}, bf16[32,32,128]{2,1,0:T(8,128)(2,1)S(1)}, u32[]{:S(2)}, u32[]{:S(2)}) collective-permute-start(bf16[32,32,128]{2,1,0:T(8,128)(2,1)S(1)} %slice_bitcast_fusion), channel_id=1, source_target_pairs={{0,1},{1,0},{2,3},{3,2},{4,5},{5,4},{6,7},{7,6},{8,9},{9,8},{10,11... | collective-permute-start | bytes 786440 | tf_op jit(solution)/shard_map/ppermute | solution.py:378
  123.7 0.0 copy-done
  123.7 0.5 shard_map.60.weights_ref
  124.2 0.8 shard_map.61.partial_ref
  125.1 0.0 collective-permute-done.4.came_ref
  125.1 1.6 %shard_map.62 = bf16[448,384]{1,0:T(8,128)(2,1)} custom-call(f32[448,768]{1,0:T(8,128)S(1)} %shard_map.61.partial_ref, bf16[32,32,128]{2,1,0:T(8,128)(2,1)S(1)} %collective-permute-done.4.came_ref, bf16[2,288,768]{2,1,0:T(8,128)(2,1)S(1)} %shard_map.60.weights_ref), custom_call_target="tpu_custom_call" | custom-call | tf_op jit(solution)/shard_map/pallas_call | solution.py:385
  (3 shorter events, 0.0 us)
Async XLA Ops:
  0.0 29.3 %collective-permute-start = (bf16[2,448,1024]{2,1,0:T(8,128)(2,1)}, bf16[2,448,1024]{2,1,0:T(8,128)(2,1)}, u32[]{:S(2)}, u32[]{:S(2)}) collective-permute-start(bf16[2,448,1024]{2,1,0:T(8,128)(2,1)} %bitcast.22), channel_id=1, source_target_pairs={{0,1},{1,257},{2,3},{3,259},{4,5},{5,261},{6,7},{7,263},{8,9},{9,2... | collective-permute-start | bytes 5505032 | tf_op jit(solution)/shard_map/ppermute | solution.py:325
  6.6 34.8 %all-to-all-start = ((bf16[64,32,128]{2,1,0:T(8,128)(2,1)}), bf16[64,32,128]{2,1,0:T(8,128)(2,1)S(1)}, u32[]{:S(2)}, u32[]{:S(2)}) async-start(bf16[64,32,128]{2,1,0:T(8,128)(2,1)} %get-tuple-element.14), calls=%async_computation | async-start | bytes 1048576 | tf_op jit(solution)/shard_map/all_to_all | solution.py:340
  29.3 14.7 %collective-permute-start.1 = (bf16[2,448,1024]{2,1,0:T(8,128)(2,1)}, bf16[2,448,1024]{2,1,0:T(8,128)(2,1)S(1)}, u32[]{:S(2)}, u32[]{:S(2)}) collective-permute-start(bf16[2,448,1024]{2,1,0:T(8,128)(2,1)} %collective-permute-done.own_hbm), channel_id=1, source_target_pairs={{0,1},{1,0},{2,3},{3,2},{4,5},{5,4},{6,7},{7,6},{8,9},{9,8},{10,11... | collective-permute-start | bytes 5505032 | tf_op jit(solution)/shard_map/ppermute | solution.py:344
  39.5 30.5 %collective-permute-start.2 = (bf16[448,1024]{1,0:T(8,128)(2,1)}, bf16[448,1024]{1,0:T(8,128)(2,1)}, u32[]{:S(2)}, u32[]{:S(2)}) collective-permute-start(bf16[448,1024]{1,0:T(8,128)(2,1)} %bitcast.23), channel_id=1, source_target_pairs={{0,1},{1,257},{2,3},{3,259},{4,5},{5,261},{6,7},{7,263},{8,9},{9,2... | collective-permute-start | bytes 2752520 | tf_op jit(solution)/shard_map/ppermute | solution.py:345
  65.5 4.1 %collective-permute-start.5 = (bf16[7,2048]{1,0:T(8,128)(2,1)S(1)}, bf16[7,2048]{1,0:T(8,128)(2,1)S(1)}, u32[]{:S(2)}, u32[]{:S(2)}) collective-permute-start(bf16[7,2048]{1,0:T(8,128)(2,1)S(1)} %slice.5), channel_id=1, source_target_pairs={{0,32},{32,64},{64,96},{96,128},{128,160},{160,192},{192,224},{256... | collective-permute-start | bytes 86024
  71.0 20.3 %all-to-all-start.1 = ((bf16[8,32,1152]{2,1,0:T(8,128)(2,1)}), bf16[8,32,1152]{2,1,0:T(8,128)(2,1)S(1)}, u32[]{:S(2)}, u32[]{:S(2)}) async-start(bf16[8,32,1152]{2,1,0:T(8,128)(2,1)} %shard_map.58), calls=%async_computation.1 | async-start | bytes 1179648 | tf_op jit(solution)/shard_map/all_to_all | solution.py:370
  76.4 8.4 %collective-permute-start.3 = (bf16[448,1024]{1,0:T(8,128)(2,1)}, bf16[448,1024]{1,0:T(8,128)(2,1)S(1)}, u32[]{:S(2)}, u32[]{:S(2)}) collective-permute-start(bf16[448,1024]{1,0:T(8,128)(2,1)} %collective-permute-done.2.own_hbm), channel_id=1, source_target_pairs={{0,1},{1,0},{2,3},{3,2},{4,5},{5,4},{6,7},{7,6},{8,9},{9,8},{10,11... | collective-permute-start | bytes 2752520 | tf_op jit(solution)/shard_map/ppermute | solution.py:365
  93.3 30.4 %copy-start = (s32[384,8]{0,1:T(8,128)S(1)}, s32[384,8]{0,1:T(8,128)}, u32[]{:S(2)}) copy-start(s32[384,8]{0,1:T(8,128)} %param.6) | copy-start | bytes 36868
  93.3 30.4 %copy-start.1 = (f32[384,8]{0,1:T(8,128)S(1)}, f32[384,8]{0,1:T(8,128)}, u32[]{:S(2)}) copy-start(f32[384,8]{0,1:T(8,128)} %param.7) | copy-start | bytes 36868
  115.5 9.6 %collective-permute-start.4 = (bf16[32,32,128]{2,1,0:T(8,128)(2,1)S(1)}, bf16[32,32,128]{2,1,0:T(8,128)(2,1)S(1)}, u32[]{:S(2)}, u32[]{:S(2)}) collective-permute-start(bf16[32,32,128]{2,1,0:T(8,128)(2,1)S(1)} %slice_bitcast_fusion), channel_id=1, source_target_pairs={{0,1},{1,0},{2,3},{3,2},{4,5},{5,4},{6,7},{7,6},{8,9},{9,8},{10,11... | collective-permute-start | bytes 786440 | tf_op jit(solution)/shard_map/ppermute | solution.py:378

commit v7 on v6

--- a/solution.py
+++ b/solution.py
@@ -340,7 +340,8 @@
     arrived = lax.all_to_all(
         send, everyone, 0, 0, axis_index_groups=along_plane, tiled=True
     )
-    own_in, w_down, mark = lax.optimization_barrier((own_in, w_down, mark))
+    w_down, mark = lax.optimization_barrier((w_down, mark))
+    own_in, mark = lax.optimization_barrier((own_in, mark))
     other_in = lax.ppermute(own_in, "expert", cores)
     own_down = lax.ppermute(w_down, everyone, turn)
     partial, rows = call(
@@ -368,6 +369,12 @@
         hidden_kernel, jax.ShapeDtypeStruct((DEPTH, mains, hidden_units + 128), BF16)
     )(sums)
     hidden = lax.all_to_all(hidden, "group", 0, 0, axis_index_groups=along_z, tiled=True)
+    weights = call(
+        weights_kernel,
+        jax.ShapeDtypeStruct((PAIR, ROWS, 2 * count), BF16),
+        in_specs=[scalar, whole, whole, whole],
+    )(core, mark, ids, combine)
+    hidden, weights = lax.optimization_barrier((hidden, weights))
     send = call(
         down_kernel,
         jax.ShapeDtypeStruct((EXPERTS, 2, 32, 128), BF16),
@@ -376,11 +383,6 @@
     )(core, hidden, pltpu.with_memory_space_constraint(own_down, pltpu.HBM), other_down)
     back = lax.all_to_all(send, everyone, 0, 0, axis_index_groups=along_core, tiled=True)
     came = lax.ppermute(back[:, 1], "expert", cores)
-    weights = call(
-        weights_kernel,
-        jax.ShapeDtypeStruct((PAIR, ROWS, 2 * count), BF16),
-        in_specs=[scalar, whole, whole, whole],
-    )(core, mark, ids, combine)
     partial = call(kept_kernel, jax.ShapeDtypeStruct((WIDTH, 2 * count), F32))(back, weights)
     routed = call(combine_kernel, jax.ShapeDtypeStruct((WIDTH, count), BF16))(
         partial, came, weights

time: 127 us -> 125 us (0.984)
  waiting for transfers between devices: 21.4 us -> 17.1 us
  starting transfers between devices: 48.1 us -> 50 us
    ppermute x1, waiting for transfers between devices: 12.5 us -> 9.13 us  [local(): own_in = lax.ppermute(w_in, everyone, turn)]
    ppermute x1, waiting for transfers between devices: 2.29 us -> 0.01 us  [local(): other_down = lax.ppermute(own_down, 'expert', cores)]
    ppermute x1, starting transfers between devices: 1.92 us -> 3.4 us  [local(): own_down = lax.ppermute(w_down, everyone, turn)]
  transfers between devices with their start and end apart: 8 -> 8, of which waited for: 3 -> 4; matrix products, arithmetic and copies ran while one was open for 17% -> 18% of each run, Pallas kernels for 6% -> 6%
where the time goes in v7:
time: 125 us
  starting transfers between devices  50 us (40%)
  blocking collectives  43.4 us (35%)
  waiting for transfers between devices  17.1 us (14%)
  Pallas kernels  12 us (10%)
  local copies, waits for them, and re-layouts  1.66 us (1%)
    all_to_all x1, blocking collectives, local(): lax.all_to_all(send, everyone, 0, 0, axis_index_groups=along_core, tiled=...  22.9 us
    unnamed x1, blocking collectives  20.5 us
    ppermute x1, starting transfers between devices, local(): other_in = lax.ppermute(own_in, 'expert', cores)  10.2 us
    all_to_all x1, starting transfers between devices, local(): lax.all_to_all(send, everyone, 0, 0, axis_index_groups=along_plane, tiled...  10.2 us
    ppermute x1, waiting for transfers between devices, local(): own_in = lax.ppermute(w_in, everyone, turn)  9.13 us
    ppermute x1, starting transfers between devices, local(): came = lax.ppermute(back[:, 1], 'expert', cores)  8.42 us
    all_to_all x1, waiting for transfers between devices, local(): lax.all_to_all(hidden, 'group', 0, 0, axis_index_groups=along_z, tiled=True)  6.68 us
    ppermute x1, starting transfers between devices, local(): other_down = lax.ppermute(own_down, 'expert', cores)  6.51 us
  transfers between devices with their start and end apart: 8, of which 4 were waited for; matrix products, arithmetic and copies ran while one was open for 18% of the time, Pallas kernels for 6%

profile of v7, /device:TPU:1, one launch (start us, length us, event | category | flops | bytes accessed | tf_op | source)
XLA Modules:
  0.0 124.9 jit_solution(5282944124999617779)
XLA Ops:
  0.0 3.9 %collective-permute-start = (bf16[2,448,1024]{2,1,0:T(8,128)(2,1)}, bf16[2,448,1024]{2,1,0:T(8,128)(2,1)}, u32[]{:S(2)}, u32[]{:S(2)}) collective-permute-start(bf16[2,448,1024]{2,1,0:T(8,128)(2,1)} %bitcast.22), channel_id=1, source_target_pairs={{0,1},{1,257},{2,3},{3,259},{4,5},{5,261},{6,7},{7,263},{8,9},{9,2... | collective-permute-start | bytes 5505032 | tf_op jit(solution)/shard_map/ppermute | solution.py:325
  3.9 2.6 %shard_map.55 = (bf16[64,32,128]{2,1,0:T(8,128)(2,1)}, f32[8,128]{1,0:T(8,128)S(1)}) custom-call(s32[8,384]{1,0:T(8,128)} %bitcast.18, bf16[448,384]{1,0:T(8,128)(2,1)} %bitcast.21), custom_call_target="tpu_custom_call" | custom-call | tf_op jit(solution)/shard_map/pallas_call | solution.py:326
  6.6 10.2 %all-to-all-start = ((bf16[64,32,128]{2,1,0:T(8,128)(2,1)}), bf16[64,32,128]{2,1,0:T(8,128)(2,1)S(1)}, u32[]{:S(2)}, u32[]{:S(2)}) async-start(bf16[64,32,128]{2,1,0:T(8,128)(2,1)} %get-tuple-element.17), calls=%async_computation | async-start | bytes 1048576 | tf_op jit(solution)/shard_map/all_to_all | solution.py:340
  16.7 3.4 %collective-permute-start.2 = (bf16[448,1024]{1,0:T(8,128)(2,1)}, bf16[448,1024]{1,0:T(8,128)(2,1)}, u32[]{:S(2)}, u32[]{:S(2)}) collective-permute-start(bf16[448,1024]{1,0:T(8,128)(2,1)} %bitcast.6), channel_id=1, source_target_pairs={{0,1},{1,257},{2,3},{3,259},{4,5},{5,261},{6,7},{7,263},{8,9},{9,2... | collective-permute-start | bytes 2752520 | tf_op jit(solution)/shard_map/ppermute | solution.py:346
  20.1 9.1 %collective-permute-done.own_hbm = bf16[2,448,1024]{2,1,0:T(8,128)(2,1)} collective-permute-done((bf16[2,448,1024]{2,1,0:T(8,128)(2,1)}, bf16[2,448,1024]{2,1,0:T(8,128)(2,1)}, u32[]{:S(2)}, u32[]{:S(2)}) %collective-permute-start) | collective-permute-done | bytes 1835040 | tf_op jit(solution)/shard_map/ppermute | solution.py:325
  29.3 10.2 %collective-permute-start.1 = (bf16[2,448,1024]{2,1,0:T(8,128)(2,1)}, bf16[2,448,1024]{2,1,0:T(8,128)(2,1)S(1)}, u32[]{:S(2)}, u32[]{:S(2)}) collective-permute-start(bf16[2,448,1024]{2,1,0:T(8,128)(2,1)} %collective-permute-done.own_hbm), channel_id=1, source_target_pairs={{0,1},{1,0},{2,3},{3,2},{4,5},{5,4},{6,7},{7,6},{8,9},{9,8},{10,11... | collective-permute-start | bytes 5505032 | tf_op jit(solution)/shard_map/ppermute | solution.py:345
  39.5 0.0 all-to-all-done.arrived_ref
  39.5 2.6 %shard_map.56 = (f32[312,2048]{1,0:T(8,128)S(1)}, bf16[312,512]{1,0:T(8,128)(2,1)S(1)}) custom-call(s32[1]{0:T(128)} %bitcast.core_ref, bf16[64,32,128]{2,1,0:T(8,128)(2,1)S(1)} %all-to-all-done.arrived_ref, bf16[2,448,1024]{2,1,0:T(8,128)(2,1)} %collective-permute-done.own_hbm), custom_call_target="tpu_custom_call" | custom-call | flops 49999998976 | bytes 4194304 | tf_op jit(solution)/shard_map/pallas_call | solution.py:347
  42.1 1.0 collective-permute-done.1.other_ref
  43.1 0.9 shard_map.57
  44.0 20.5 %fusion = bf16[40,2048]{1,0:T(8,128)(2,1)S(1)} fusion(bf16[312,2048]{1,0:T(8,128)(2,1)S(1)} %shard_map.57), kind=kCustom, calls=%all-reduce-scatter | all-reduce-scatter fusion | flops 655361 | bytes 1443840
  64.5 0.0 copy-start
  64.5 0.0 copy-start.1
  64.5 2.2 %collective-permute-start.5 = (bf16[7,2048]{1,0:T(8,128)(2,1)S(1)}, bf16[7,2048]{1,0:T(8,128)(2,1)S(1)}, u32[]{:S(2)}, u32[]{:S(2)}) collective-permute-start(bf16[7,2048]{1,0:T(8,128)(2,1)S(1)} %slice.5), channel_id=1, source_target_pairs={{0,32},{32,64},{64,96},{96,128},{128,160},{160,192},{192,224},{256... | collective-permute-start | bytes 86024
  66.7 1.3 %dynamic-slice.4 = u32[1]{0:T(128)} dynamic-slice(u32[512]{0:T(512)} %constant.10, u32[]{:S(6)} %partition-id.2), dynamic_slice_sizes={1} | dynamic-slice | bytes 12
  68.7 0.0 collective-permute-done.5
  68.7 0.2 concatenate
  69.0 0.1 constant_dynamic-slice_fusion.sums_ref
  69.0 0.0 collective-permute-done.2.own_hbm
  69.0 1.0 shard_map.58
  70.0 5.1 %all-to-all-start.1 = ((bf16[8,32,1152]{2,1,0:T(8,128)(2,1)}), bf16[8,32,1152]{2,1,0:T(8,128)(2,1)S(1)}, u32[]{:S(2)}, u32[]{:S(2)}) async-start(bf16[8,32,1152]{2,1,0:T(8,128)(2,1)} %shard_map.58), calls=%async_computation.1 | async-start | bytes 1179648 | tf_op jit(solution)/shard_map/all_to_all | solution.py:371
  75.2 6.5 %collective-permute-start.3 = (bf16[448,1024]{1,0:T(8,128)(2,1)}, bf16[448,1024]{1,0:T(8,128)(2,1)S(1)}, u32[]{:S(2)}, u32[]{:S(2)}) collective-permute-start(bf16[448,1024]{1,0:T(8,128)(2,1)} %collective-permute-done.2.own_hbm), channel_id=1, source_target_pairs={{0,1},{1,0},{2,3},{3,2},{4,5},{5,4},{6,7},{7,6},{8,9},{9,8},{10,11... | collective-permute-start | bytes 2752520 | tf_op jit(solution)/shard_map/ppermute | solution.py:366
  81.7 0.0 copy-done
  81.7 0.5 shard_map.59.weights_ref
  82.2 6.7 %all-to-all-done.1.hidden_ref = bf16[8,32,1152]{2,1,0:T(8,128)(2,1)S(1)} async-done(((bf16[8,32,1152]{2,1,0:T(8,128)(2,1)}), bf16[8,32,1152]{2,1,0:T(8,128)(2,1)S(1)}, u32[]{:S(2)}, u32[]{:S(2)}) %all-to-all-start.1) | async-done | bytes 589856 | tf_op jit(solution)/shard_map/all_to_all | solution.py:371
  88.9 0.0 collective-permute-done.3.other_ref
  88.9 2.0 %shard_map.60 = bf16[32,2,32,128]{3,2,1,0:T(8,128)(2,1)S(1)} custom-call(s32[1]{0:T(128)} %bitcast.core_ref, bf16[8,32,1152]{2,1,0:T(8,128)(2,1)S(1)} %all-to-all-done.1.hidden_ref, bf16[448,1024]{1,0:T(8,128)(2,1)} %collective-permute-done.2.own_hbm, bf16[448,1024]{1,0:T(8,128)(2,1)S(1)} %collective-permute-done.3.other_ref), custom_call_target="tpu_custom_call" | custom-call | tf_op jit(solution)/shard_map/pallas_call | solution.py:378
  90.9 22.9 %all_to_all.15.back_ref = bf16[32,2,32,128]{3,2,1,0:T(8,128)(2,1)S(1)} all-to-all(bf16[32,2,32,128]{3,2,1,0:T(8,128)(2,1)S(1)} %shard_map.60), channel_id=1, replica_groups={{0,2,4,6,8,10,12,14,16,18,20,22,24,26,28,30,256,258,260,262,264,266,268..., dimensions={0} | all-to-all | bytes 1048576 | tf_op jit(solution)/shard_map/all_to_all | solution.py:384
  113.7 8.4 %collective-permute-start.4 = (bf16[32,32,128]{2,1,0:T(8,128)(2,1)S(1)}, bf16[32,32,128]{2,1,0:T(8,128)(2,1)S(1)}, u32[]{:S(2)}, u32[]{:S(2)}) collective-permute-start(bf16[32,32,128]{2,1,0:T(8,128)(2,1)S(1)} %slice_bitcast_fusion), channel_id=1, source_target_pairs={{0,1},{1,0},{2,3},{3,2},{4,5},{5,4},{6,7},{7,6},{8,9},{9,8},{10,11... | collective-permute-start | bytes 786440 | tf_op jit(solution)/shard_map/ppermute | solution.py:385
  122.2 0.8 shard_map.61.partial_ref
  123.0 0.3 collective-permute-done.4.came_ref
  123.3 1.6 %shard_map.62 = bf16[448,384]{1,0:T(8,128)(2,1)} custom-call(f32[448,768]{1,0:T(8,128)S(1)} %shard_map.61.partial_ref, bf16[32,32,128]{2,1,0:T(8,128)(2,1)S(1)} %collective-permute-done.4.came_ref, bf16[2,288,768]{2,1,0:T(8,128)(2,1)S(1)} %shard_map.59.weights_ref), custom_call_target="tpu_custom_call" | custom-call | tf_op jit(solution)/shard_map/pallas_call | solution.py:387
  (3 shorter events, 0.0 us)
Async XLA Ops:
  0.0 29.3 %collective-permute-start = (bf16[2,448,1024]{2,1,0:T(8,128)(2,1)}, bf16[2,448,1024]{2,1,0:T(8,128)(2,1)}, u32[]{:S(2)}, u32[]{:S(2)}) collective-permute-start(bf16[2,448,1024]{2,1,0:T(8,128)(2,1)} %bitcast.22), channel_id=1, source_target_pairs={{0,1},{1,257},{2,3},{3,259},{4,5},{5,261},{6,7},{7,263},{8,9},{9,2... | collective-permute-start | bytes 5505032 | tf_op jit(solution)/shard_map/ppermute | solution.py:325
  6.6 32.9 %all-to-all-start = ((bf16[64,32,128]{2,1,0:T(8,128)(2,1)}), bf16[64,32,128]{2,1,0:T(8,128)(2,1)S(1)}, u32[]{:S(2)}, u32[]{:S(2)}) async-start(bf16[64,32,128]{2,1,0:T(8,128)(2,1)} %get-tuple-element.17), calls=%async_computation | async-start | bytes 1048576 | tf_op jit(solution)/shard_map/all_to_all | solution.py:340
  16.7 52.3 %collective-permute-start.2 = (bf16[448,1024]{1,0:T(8,128)(2,1)}, bf16[448,1024]{1,0:T(8,128)(2,1)}, u32[]{:S(2)}, u32[]{:S(2)}) collective-permute-start(bf16[448,1024]{1,0:T(8,128)(2,1)} %bitcast.6), channel_id=1, source_target_pairs={{0,1},{1,257},{2,3},{3,259},{4,5},{5,261},{6,7},{7,263},{8,9},{9,2... | collective-permute-start | bytes 2752520 | tf_op jit(solution)/shard_map/ppermute | solution.py:346
  29.3 13.8 %collective-permute-start.1 = (bf16[2,448,1024]{2,1,0:T(8,128)(2,1)}, bf16[2,448,1024]{2,1,0:T(8,128)(2,1)S(1)}, u32[]{:S(2)}, u32[]{:S(2)}) collective-permute-start(bf16[2,448,1024]{2,1,0:T(8,128)(2,1)} %collective-permute-done.own_hbm), channel_id=1, source_target_pairs={{0,1},{1,0},{2,3},{3,2},{4,5},{5,4},{6,7},{7,6},{8,9},{9,8},{10,11... | collective-permute-start | bytes 5505032 | tf_op jit(solution)/shard_map/ppermute | solution.py:345
  64.5 17.2 %copy-start = (s32[384,8]{0,1:T(8,128)S(1)}, s32[384,8]{0,1:T(8,128)}, u32[]{:S(2)}) copy-start(s32[384,8]{0,1:T(8,128)} %param.6) | copy-start | bytes 36868
  64.5 17.2 %copy-start.1 = (f32[384,8]{0,1:T(8,128)S(1)}, f32[384,8]{0,1:T(8,128)}, u32[]{:S(2)}) copy-start(f32[384,8]{0,1:T(8,128)} %param.7) | copy-start | bytes 36868
  64.5 4.2 %collective-permute-start.5 = (bf16[7,2048]{1,0:T(8,128)(2,1)S(1)}, bf16[7,2048]{1,0:T(8,128)(2,1)S(1)}, u32[]{:S(2)}, u32[]{:S(2)}) collective-permute-start(bf16[7,2048]{1,0:T(8,128)(2,1)S(1)} %slice.5), channel_id=1, source_target_pairs={{0,32},{32,64},{64,96},{96,128},{128,160},{160,192},{192,224},{256... | collective-permute-start | bytes 86024
  70.0 18.9 %all-to-all-start.1 = ((bf16[8,32,1152]{2,1,0:T(8,128)(2,1)}), bf16[8,32,1152]{2,1,0:T(8,128)(2,1)S(1)}, u32[]{:S(2)}, u32[]{:S(2)}) async-start(bf16[8,32,1152]{2,1,0:T(8,128)(2,1)} %shard_map.58), calls=%async_computation.1 | async-start | bytes 1179648 | tf_op jit(solution)/shard_map/all_to_all | solution.py:371
  75.2 13.7 %collective-permute-start.3 = (bf16[448,1024]{1,0:T(8,128)(2,1)}, bf16[448,1024]{1,0:T(8,128)(2,1)S(1)}, u32[]{:S(2)}, u32[]{:S(2)}) collective-permute-start(bf16[448,1024]{1,0:T(8,128)(2,1)} %collective-permute-done.2.own_hbm), channel_id=1, source_target_pairs={{0,1},{1,0},{2,3},{3,2},{4,5},{5,4},{6,7},{7,6},{8,9},{9,8},{10,11... | collective-permute-start | bytes 2752520 | tf_op jit(solution)/shard_map/ppermute | solution.py:366
  113.7 9.6 %collective-permute-start.4 = (bf16[32,32,128]{2,1,0:T(8,128)(2,1)S(1)}, bf16[32,32,128]{2,1,0:T(8,128)(2,1)S(1)}, u32[]{:S(2)}, u32[]{:S(2)}) collective-permute-start(bf16[32,32,128]{2,1,0:T(8,128)(2,1)S(1)} %slice_bitcast_fusion), channel_id=1, source_target_pairs={{0,1},{1,0},{2,3},{3,2},{4,5},{5,4},{6,7},{7,6},{8,9},{9,8},{10,11... | collective-permute-start | bytes 786440 | tf_op jit(solution)/shard_map/ppermute | solution.py:385

commit v8 on v7

--- a/solution.py
+++ b/solution.py
@@ -122,8 +122,10 @@
         send_ref[EXPERTS * chip : EXPERTS * chip + EXPERTS] = pack(main[rows], last[rows])
 
 
-def weights_kernel(core_ref, mark_ref, ids_ref, combine_ref, weights_ref):
+def weights_kernel(core_ref, mark_ref, ids_ref, combine_ref, down_ref, weights_ref, padded_ref):
     del mark_ref
+    padded_ref[:WIDTH] = down_ref[...]
+    padded_ref[WIDTH:] = jnp.zeros((PADDED - WIDTH, down_ref.shape[1]), BF16)
     core = core_ref[0]
     index = lax.broadcasted_iota(jnp.int32, (PAIR * EXPERTS, ids_ref.shape[1]), 0)
     label = 2 * (index & 15) + ((index >> 4) & 1)
@@ -247,18 +249,14 @@
     return jnp.concatenate([main, last], axis=0)
 
 
-def down_kernel(core_ref, hidden_ref, own_hbm, other_ref, send_ref, own_ref, sem):
-    copy = pltpu.make_async_copy(own_hbm, own_ref, sem)
-    copy.start()
+def down_kernel(core_ref, hidden_ref, own_ref, other_ref, send_ref):
     core = core_ref[0]
     hidden = gathered_hidden(hidden_ref)
     chips = EXPERTS // 2
-    for ref, where in ((other_ref, core), (own_ref, 1 - core)):
-        if ref is own_ref:
-            copy.wait()
-        down = jnp.concatenate(
-            [ref[...], jnp.zeros((PADDED - WIDTH, ref.shape[1]), BF16)], axis=0
-        )
+    other = jnp.concatenate(
+        [other_ref[...], jnp.zeros((PADDED - WIDTH, other_ref.shape[1]), BF16)], axis=0
+    )
+    for down, where in ((other, core), (own_ref[...], 1 - core)):
         result = lax.dot_general(hidden, down, NT, preferred_element_type=F32).astype(BF16)
         last = jnp.dot(spread(EXPERTS), result[MAIN:], preferred_element_type=F32)
         blocks = pack(result[:MAIN].astype(F32), last).reshape(chips, 2, 32, 128)
@@ -369,18 +367,20 @@
         hidden_kernel, jax.ShapeDtypeStruct((DEPTH, mains, hidden_units + 128), BF16)
     )(sums)
     hidden = lax.all_to_all(hidden, "group", 0, 0, axis_index_groups=along_z, tiled=True)
-    weights = call(
+    weights, own_padded = call(
         weights_kernel,
-        jax.ShapeDtypeStruct((PAIR, ROWS, 2 * count), BF16),
-        in_specs=[scalar, whole, whole, whole],
-    )(core, mark, ids, combine)
-    hidden, weights = lax.optimization_barrier((hidden, weights))
+        (
+            jax.ShapeDtypeStruct((PAIR, ROWS, 2 * count), BF16),
+            jax.ShapeDtypeStruct((PADDED, hidden_units), BF16),
+        ),
+        in_specs=[scalar, whole, whole, whole, whole],
+    )(core, mark, ids, combine, own_down)
+    hidden, weights, own_padded = lax.optimization_barrier((hidden, weights, own_padded))
     send = call(
         down_kernel,
         jax.ShapeDtypeStruct((EXPERTS, 2, 32, 128), BF16),
-        in_specs=[scalar, whole, anywhere, whole],
-        scratch_shapes=[pltpu.VMEM(own_down.shape, BF16), pltpu.SemaphoreType.DMA],
-    )(core, hidden, pltpu.with_memory_space_constraint(own_down, pltpu.HBM), other_down)
+        in_specs=[scalar, whole, whole, whole],
+    )(core, hidden, own_padded, other_down)
     back = lax.all_to_all(send, everyone, 0, 0, axis_index_groups=along_core, tiled=True)
     came = lax.ppermute(back[:, 1], "expert", cores)
     partial = call(kept_kernel, jax.ShapeDtypeStruct((WIDTH, 2 * count), F32))(back, weights)

time: 125 us -> 125 us (level)
  transfers between devices with their start and end apart: 8 -> 8, of which waited for: 4 -> 4; matrix products, arithmetic and copies ran while one was open for 18% -> 18% of each run, Pallas kernels for 6% -> 7%
where the time goes in v8:
time: 125 us; the launch traced here: 124 us
  starting transfers between devices  50 us (40%)
  blocking collectives  43.4 us (35%)
  waiting for transfers between devices  15.9 us (13%)
  Pallas kernels  12.6 us (10%)
  local copies, waits for them, and re-layouts  1.62 us (1%)
    all_to_all x1, blocking collectives, local(): lax.all_to_all(send, everyone, 0, 0, axis_index_groups=along_core, tiled=...  22.9 us
    unnamed x1, blocking collectives  20.5 us
    ppermute x1, starting transfers between devices, local(): other_in = lax.ppermute(own_in, 'expert', cores)  10.2 us
    all_to_all x1, starting transfers between devices, local(): lax.all_to_all(send, everyone, 0, 0, axis_index_groups=along_plane, tiled...  10.2 us
    ppermute x1, waiting for transfers between devices, local(): own_in = lax.ppermute(w_in, everyone, turn)  9.13 us
    ppermute x1, starting transfers between devices, local(): came = lax.ppermute(back[:, 1], 'expert', cores)  8.42 us
    ppermute x1, starting transfers between devices, local(): other_down = lax.ppermute(own_down, 'expert', cores)  6.51 us
    all_to_all x1, waiting for transfers between devices, local(): lax.all_to_all(hidden, 'group', 0, 0, axis_index_groups=along_z, tiled=True)  5.44 us
  transfers between devices with their start and end apart: 8, of which 4 were waited for; matrix products, arithmetic and copies ran while one was open for 18% of the time, Pallas kernels for 7%

profile of v8, /device:TPU:1, one launch (start us, length us, event | category | flops | bytes accessed | tf_op | source)
XLA Modules:
  0.0 124.3 jit_solution(2256061831213623704)
XLA Ops:
  0.0 3.9 %collective-permute-start = (bf16[2,448,1024]{2,1,0:T(8,128)(2,1)}, bf16[2,448,1024]{2,1,0:T(8,128)(2,1)}, u32[]{:S(2)}, u32[]{:S(2)}) collective-permute-start(bf16[2,448,1024]{2,1,0:T(8,128)(2,1)} %bitcast.22), channel_id=1, source_target_pairs={{0,1},{1,257},{2,3},{3,259},{4,5},{5,261},{6,7},{7,263},{8,9},{9,2... | collective-permute-start | bytes 5505032 | tf_op jit(solution)/shard_map/ppermute | solution.py:323
  3.9 2.6 %shard_map.55 = (bf16[64,32,128]{2,1,0:T(8,128)(2,1)}, f32[8,128]{1,0:T(8,128)S(1)}) custom-call(s32[8,384]{1,0:T(8,128)} %bitcast.18, bf16[448,384]{1,0:T(8,128)(2,1)} %bitcast.21), custom_call_target="tpu_custom_call" | custom-call | tf_op jit(solution)/shard_map/pallas_call | solution.py:324
  6.6 10.2 %all-to-all-start = ((bf16[64,32,128]{2,1,0:T(8,128)(2,1)}), bf16[64,32,128]{2,1,0:T(8,128)(2,1)S(1)}, u32[]{:S(2)}, u32[]{:S(2)}) async-start(bf16[64,32,128]{2,1,0:T(8,128)(2,1)} %get-tuple-element.20), calls=%async_computation | async-start | bytes 1048576 | tf_op jit(solution)/shard_map/all_to_all | solution.py:338
  16.7 3.4 %collective-permute-start.2 = (bf16[448,1024]{1,0:T(8,128)(2,1)}, bf16[448,1024]{1,0:T(8,128)(2,1)}, u32[]{:S(2)}, u32[]{:S(2)}) collective-permute-start(bf16[448,1024]{1,0:T(8,128)(2,1)} %bitcast.6), channel_id=1, source_target_pairs={{0,1},{1,257},{2,3},{3,259},{4,5},{5,261},{6,7},{7,263},{8,9},{9,2... | collective-permute-start | bytes 2752520 | tf_op jit(solution)/shard_map/ppermute | solution.py:344
  20.1 9.1 %collective-permute-done.own_hbm = bf16[2,448,1024]{2,1,0:T(8,128)(2,1)} collective-permute-done((bf16[2,448,1024]{2,1,0:T(8,128)(2,1)}, bf16[2,448,1024]{2,1,0:T(8,128)(2,1)}, u32[]{:S(2)}, u32[]{:S(2)}) %collective-permute-start) | collective-permute-done | bytes 1835040 | tf_op jit(solution)/shard_map/ppermute | solution.py:323
  29.3 10.2 %collective-permute-start.1 = (bf16[2,448,1024]{2,1,0:T(8,128)(2,1)}, bf16[2,448,1024]{2,1,0:T(8,128)(2,1)S(1)}, u32[]{:S(2)}, u32[]{:S(2)}) collective-permute-start(bf16[2,448,1024]{2,1,0:T(8,128)(2,1)} %collective-permute-done.own_hbm), channel_id=1, source_target_pairs={{0,1},{1,0},{2,3},{3,2},{4,5},{5,4},{6,7},{7,6},{8,9},{9,8},{10,11... | collective-permute-start | bytes 5505032 | tf_op jit(solution)/shard_map/ppermute | solution.py:343
  39.5 0.0 all-to-all-done.arrived_ref
  39.5 2.6 %shard_map.56 = (f32[312,2048]{1,0:T(8,128)S(1)}, bf16[312,512]{1,0:T(8,128)(2,1)S(1)}) custom-call(s32[1]{0:T(128)} %bitcast.core_ref, bf16[64,32,128]{2,1,0:T(8,128)(2,1)S(1)} %all-to-all-done.arrived_ref, bf16[2,448,1024]{2,1,0:T(8,128)(2,1)} %collective-permute-done.own_hbm), custom_call_target="tpu_custom_call" | custom-call | flops 49999998976 | bytes 4194304 | tf_op jit(solution)/shard_map/pallas_call | solution.py:345
  42.1 1.0 collective-permute-done.1.other_ref
  43.1 0.9 shard_map.57
  44.0 20.5 %fusion = bf16[40,2048]{1,0:T(8,128)(2,1)S(1)} fusion(bf16[312,2048]{1,0:T(8,128)(2,1)S(1)} %shard_map.57), kind=kCustom, calls=%all-reduce-scatter | all-reduce-scatter fusion | flops 655361 | bytes 1443840
  64.5 0.0 copy-start
  64.5 0.0 copy-start.1
  64.5 2.2 %collective-permute-start.5 = (bf16[7,2048]{1,0:T(8,128)(2,1)S(1)}, bf16[7,2048]{1,0:T(8,128)(2,1)S(1)}, u32[]{:S(2)}, u32[]{:S(2)}) collective-permute-start(bf16[7,2048]{1,0:T(8,128)(2,1)S(1)} %slice.5), channel_id=1, source_target_pairs={{0,32},{32,64},{64,96},{96,128},{128,160},{160,192},{192,224},{256... | collective-permute-start | bytes 86024
  66.7 1.3 %dynamic-slice.4 = u32[1]{0:T(128)} dynamic-slice(u32[512]{0:T(512)} %constant.10, u32[]{:S(6)} %partition-id.2), dynamic_slice_sizes={1} | dynamic-slice | bytes 12
  68.7 0.0 collective-permute-done.5
  68.7 0.2 concatenate
  68.9 0.1 constant_dynamic-slice_fusion.sums_ref
  69.0 0.0 collective-permute-done.2.down_ref
  69.0 1.0 shard_map.58
  70.0 5.2 %all-to-all-start.1 = ((bf16[8,32,1152]{2,1,0:T(8,128)(2,1)}), bf16[8,32,1152]{2,1,0:T(8,128)(2,1)S(1)}, u32[]{:S(2)}, u32[]{:S(2)}) async-start(bf16[8,32,1152]{2,1,0:T(8,128)(2,1)} %shard_map.58), calls=%async_computation.1 | async-start | bytes 1179648 | tf_op jit(solution)/shard_map/all_to_all | solution.py:369
  75.2 6.5 %collective-permute-start.3 = (bf16[448,1024]{1,0:T(8,128)(2,1)}, bf16[448,1024]{1,0:T(8,128)(2,1)S(1)}, u32[]{:S(2)}, u32[]{:S(2)}) collective-permute-start(bf16[448,1024]{1,0:T(8,128)(2,1)} %collective-permute-done.2.down_ref), channel_id=1, source_target_pairs={{0,1},{1,0},{2,3},{3,2},{4,5},{5,4},{6,7},{7,6},{8,9},{9,8},{10,11... | collective-permute-start | bytes 2752520 | tf_op jit(solution)/shard_map/ppermute | solution.py:364
  81.7 0.0 copy-done
  81.7 1.7 %shard_map.59 = (bf16[2,288,768]{2,1,0:T(8,128)(2,1)S(1)}, bf16[512,1024]{1,0:T(8,128)(2,1)S(1)}) custom-call(s32[1]{0:T(128)} %bitcast.core_ref, f32[8,128]{1,0:T(8,128)S(1)} %get-tuple-element.28.mark_ref, s32[8,384]{1,0:T(8,128)S(1)} %bitcast.19, f32[8,384]{1,0:T(8,128)S(1)} %bitcast.20, bf16[448,1024]{1,0:T(8,128)(2,1)} %collective-permute-done.2.down_ref), custom_call_target="tpu_custom_call" | custom-call | tf_op jit(solution)/shard_map/pallas_call | solution.py:370
  83.5 5.4 %all-to-all-done.1.hidden_ref = bf16[8,32,1152]{2,1,0:T(8,128)(2,1)S(1)} async-done(((bf16[8,32,1152]{2,1,0:T(8,128)(2,1)}), bf16[8,32,1152]{2,1,0:T(8,128)(2,1)S(1)}, u32[]{:S(2)}, u32[]{:S(2)}) %all-to-all-start.1) | async-done | bytes 589856 | tf_op jit(solution)/shard_map/all_to_all | solution.py:369
  88.9 0.0 collective-permute-done.3.other_ref
  88.9 1.4 %shard_map.60 = bf16[32,2,32,128]{3,2,1,0:T(8,128)(2,1)S(1)} custom-call(s32[1]{0:T(128)} %bitcast.core_ref, bf16[8,32,1152]{2,1,0:T(8,128)(2,1)S(1)} %all-to-all-done.1.hidden_ref, bf16[512,1024]{1,0:T(8,128)(2,1)S(1)} %get-tuple-element.33.own_ref, bf16[448,1024]{1,0:T(8,128)(2,1)S(1)} %collective-permute-done.3.other_ref), custom_call_target="tpu_custom_call" | custom-call | tf_op jit(solution)/shard_map/pallas_call | solution.py:379
  90.3 22.9 %all_to_all.15.back_ref = bf16[32,2,32,128]{3,2,1,0:T(8,128)(2,1)S(1)} all-to-all(bf16[32,2,32,128]{3,2,1,0:T(8,128)(2,1)S(1)} %shard_map.60), channel_id=1, replica_groups={{0,2,4,6,8,10,12,14,16,18,20,22,24,26,28,30,256,258,260,262,264,266,268..., dimensions={0} | all-to-all | bytes 1048576 | tf_op jit(solution)/shard_map/all_to_all | solution.py:384
  113.2 8.4 %collective-permute-start.4 = (bf16[32,32,128]{2,1,0:T(8,128)(2,1)S(1)}, bf16[32,32,128]{2,1,0:T(8,128)(2,1)S(1)}, u32[]{:S(2)}, u32[]{:S(2)}) collective-permute-start(bf16[32,32,128]{2,1,0:T(8,128)(2,1)S(1)} %slice_bitcast_fusion), channel_id=1, source_target_pairs={{0,1},{1,0},{2,3},{3,2},{4,5},{5,4},{6,7},{7,6},{8,9},{9,8},{10,11... | collective-permute-start | bytes 786440 | tf_op jit(solution)/shard_map/ppermute | solution.py:385
  121.6 0.8 shard_map.61.partial_ref
  122.4 0.3 collective-permute-done.4.came_ref
  122.7 1.6 %shard_map.62 = bf16[448,384]{1,0:T(8,128)(2,1)} custom-call(f32[448,768]{1,0:T(8,128)S(1)} %shard_map.61.partial_ref, bf16[32,32,128]{2,1,0:T(8,128)(2,1)S(1)} %collective-permute-done.4.came_ref, bf16[2,288,768]{2,1,0:T(8,128)(2,1)S(1)} %get-tuple-element.34.weights_ref), custom_call_target="tpu_custom_call" | custom-call | tf_op jit(solution)/shard_map/pallas_call | solution.py:387
  (3 shorter events, 0.0 us)
Async XLA Ops:
  0.0 29.3 %collective-permute-start = (bf16[2,448,1024]{2,1,0:T(8,128)(2,1)}, bf16[2,448,1024]{2,1,0:T(8,128)(2,1)}, u32[]{:S(2)}, u32[]{:S(2)}) collective-permute-start(bf16[2,448,1024]{2,1,0:T(8,128)(2,1)} %bitcast.22), channel_id=1, source_target_pairs={{0,1},{1,257},{2,3},{3,259},{4,5},{5,261},{6,7},{7,263},{8,9},{9,2... | collective-permute-start | bytes 5505032 | tf_op jit(solution)/shard_map/ppermute | solution.py:323
  6.6 32.9 %all-to-all-start = ((bf16[64,32,128]{2,1,0:T(8,128)(2,1)}), bf16[64,32,128]{2,1,0:T(8,128)(2,1)S(1)}, u32[]{:S(2)}, u32[]{:S(2)}) async-start(bf16[64,32,128]{2,1,0:T(8,128)(2,1)} %get-tuple-element.20), calls=%async_computation | async-start | bytes 1048576 | tf_op jit(solution)/shard_map/all_to_all | solution.py:338
  16.7 52.3 %collective-permute-start.2 = (bf16[448,1024]{1,0:T(8,128)(2,1)}, bf16[448,1024]{1,0:T(8,128)(2,1)}, u32[]{:S(2)}, u32[]{:S(2)}) collective-permute-start(bf16[448,1024]{1,0:T(8,128)(2,1)} %bitcast.6), channel_id=1, source_target_pairs={{0,1},{1,257},{2,3},{3,259},{4,5},{5,261},{6,7},{7,263},{8,9},{9,2... | collective-permute-start | bytes 2752520 | tf_op jit(solution)/shard_map/ppermute | solution.py:344
  29.3 13.8 %collective-permute-start.1 = (bf16[2,448,1024]{2,1,0:T(8,128)(2,1)}, bf16[2,448,1024]{2,1,0:T(8,128)(2,1)S(1)}, u32[]{:S(2)}, u32[]{:S(2)}) collective-permute-start(bf16[2,448,1024]{2,1,0:T(8,128)(2,1)} %collective-permute-done.own_hbm), channel_id=1, source_target_pairs={{0,1},{1,0},{2,3},{3,2},{4,5},{5,4},{6,7},{7,6},{8,9},{9,8},{10,11... | collective-permute-start | bytes 5505032 | tf_op jit(solution)/shard_map/ppermute | solution.py:343
  64.5 17.2 %copy-start = (s32[384,8]{0,1:T(8,128)S(1)}, s32[384,8]{0,1:T(8,128)}, u32[]{:S(2)}) copy-start(s32[384,8]{0,1:T(8,128)} %param.6) | copy-start | bytes 36868
  64.5 17.2 %copy-start.1 = (f32[384,8]{0,1:T(8,128)S(1)}, f32[384,8]{0,1:T(8,128)}, u32[]{:S(2)}) copy-start(f32[384,8]{0,1:T(8,128)} %param.7) | copy-start | bytes 36868
  64.5 4.1 %collective-permute-start.5 = (bf16[7,2048]{1,0:T(8,128)(2,1)S(1)}, bf16[7,2048]{1,0:T(8,128)(2,1)S(1)}, u32[]{:S(2)}, u32[]{:S(2)}) collective-permute-start(bf16[7,2048]{1,0:T(8,128)(2,1)S(1)} %slice.5), channel_id=1, source_target_pairs={{0,32},{32,64},{64,96},{96,128},{128,160},{160,192},{192,224},{256... | collective-permute-start | bytes 86024
  70.0 18.9 %all-to-all-start.1 = ((bf16[8,32,1152]{2,1,0:T(8,128)(2,1)}), bf16[8,32,1152]{2,1,0:T(8,128)(2,1)S(1)}, u32[]{:S(2)}, u32[]{:S(2)}) async-start(bf16[8,32,1152]{2,1,0:T(8,128)(2,1)} %shard_map.58), calls=%async_computation.1 | async-start | bytes 1179648 | tf_op jit(solution)/shard_map/all_to_all | solution.py:369
  75.2 13.7 %collective-permute-start.3 = (bf16[448,1024]{1,0:T(8,128)(2,1)}, bf16[448,1024]{1,0:T(8,128)(2,1)S(1)}, u32[]{:S(2)}, u32[]{:S(2)}) collective-permute-start(bf16[448,1024]{1,0:T(8,128)(2,1)} %collective-permute-done.2.down_ref), channel_id=1, source_target_pairs={{0,1},{1,0},{2,3},{3,2},{4,5},{5,4},{6,7},{7,6},{8,9},{9,8},{10,11... | collective-permute-start | bytes 2752520 | tf_op jit(solution)/shard_map/ppermute | solution.py:364
  113.2 9.6 %collective-permute-start.4 = (bf16[32,32,128]{2,1,0:T(8,128)(2,1)S(1)}, bf16[32,32,128]{2,1,0:T(8,128)(2,1)S(1)}, u32[]{:S(2)}, u32[]{:S(2)}) collective-permute-start(bf16[32,32,128]{2,1,0:T(8,128)(2,1)S(1)} %slice_bitcast_fusion), channel_id=1, source_target_pairs={{0,1},{1,0},{2,3},{3,2},{4,5},{5,4},{6,7},{7,6},{8,9},{9,8},{10,11... | collective-permute-start | bytes 786440 | tf_op jit(solution)/shard_map/ppermute | solution.py:385

commit v9 on v8

--- a/solution.py
+++ b/solution.py
@@ -265,19 +265,27 @@
         send_ref[at, pl.ds(1 - core, 1)] = blocks[:, 1:2]
 
 
+def both_parts(rows, weights):
+    routed = lax.dot_general(rows, weights, TN, preferred_element_type=F32)
+    count = routed.shape[1] // 2
+    return routed[:, :count] + routed[:, count:]
+
+
 def kept_kernel(back_ref, weights_ref, partial_ref):
-    partial_ref[...] = lax.dot_general(
-        unpack(back_ref[:, 0]), weights_ref[0], TN, preferred_element_type=F32
-    )[:WIDTH]
-
-
-def combine_kernel(partial_ref, came_ref, weights_ref, out_ref):
-    routed = partial_ref[...]
-    routed += lax.dot_general(
-        unpack(came_ref[...]), weights_ref[1], TN, preferred_element_type=F32
-    )[:WIDTH]
-    count = out_ref.shape[1]
-    out_ref[...] = (routed[:, :count] + routed[:, count:]).astype(BF16)
+    partial_ref[...] = both_parts(unpack(back_ref[:, 0]), weights_ref[0])[:WIDTH]
+
+
+def combine_kernel(partial_ref, came_ref, weights_ref, out_hbm, out_ref, sems):
+    rows = unpack(came_ref[...])
+    copies = []
+    for number, (start, stop) in enumerate(((0, 256), (256, WIDTH))):
+        routed = partial_ref[start:stop] + both_parts(rows[:, start:stop], weights_ref[1])
+        out_ref[start:stop] = routed.astype(BF16)
+        at = pl.ds(start, stop - start)
+        copies.append(pltpu.make_async_copy(out_ref.at[at], out_hbm.at[at], sems.at[number]))
+        copies[number].start()
+    for copy in copies:
+        copy.wait()
 
 
 def call(kernel, out, **more):
@@ -383,10 +391,13 @@
     )(core, hidden, own_padded, other_down)
     back = lax.all_to_all(send, everyone, 0, 0, axis_index_groups=along_core, tiled=True)
     came = lax.ppermute(back[:, 1], "expert", cores)
-    partial = call(kept_kernel, jax.ShapeDtypeStruct((WIDTH, 2 * count), F32))(back, weights)
-    routed = call(combine_kernel, jax.ShapeDtypeStruct((WIDTH, count), BF16))(
-        partial, came, weights
-    )
+    partial = call(kept_kernel, jax.ShapeDtypeStruct((WIDTH, count), F32))(back, weights)
+    routed = call(
+        combine_kernel,
+        jax.ShapeDtypeStruct((WIDTH, count), BF16),
+        out_specs=anywhere,
+        scratch_shapes=[pltpu.VMEM((WIDTH, count), BF16), pltpu.SemaphoreType.DMA((2,))],
+    )(partial, came, weights)
     return routed.T
 
 

time: 125 us -> 125 us (level)
  no operation moved by 1% of the time
where the time goes in v9:
time: 125 us; the launch traced here: 124 us
  starting transfers between devices  50 us (40%)
  blocking collectives  43.4 us (35%)
  waiting for transfers between devices  15.9 us (13%)
  Pallas kernels  12.6 us (10%)
  local copies, waits for them, and re-layouts  1.62 us (1%)
    all_to_all x1, blocking collectives, local(): lax.all_to_all(send, everyone, 0, 0, axis_index_groups=along_core, tiled=...  22.9 us
    unnamed x1, blocking collectives  20.5 us
    ppermute x1, starting transfers between devices, local(): other_in = lax.ppermute(own_in, 'expert', cores)  10.2 us
    all_to_all x1, starting transfers between devices, local(): lax.all_to_all(send, everyone, 0, 0, axis_index_groups=along_plane, tiled...  10.2 us
    ppermute x1, waiting for transfers between devices, local(): own_in = lax.ppermute(w_in, everyone, turn)  9.13 us
    ppermute x1, starting transfers between devices, local(): came = lax.ppermute(back[:, 1], 'expert', cores)  8.42 us
    ppermute x1, starting transfers between devices, local(): other_down = lax.ppermute(own_down, 'expert', cores)  6.51 us
    all_to_all x1, waiting for transfers between devices, local(): lax.all_to_all(hidden, 'group', 0, 0, axis_index_groups=along_z, tiled=True)  5.44 us
  transfers between devices with their start and end apart: 8, of which 4 were waited for; matrix products, arithmetic and copies ran while one was open for 18% of the time, Pallas kernels for 7%

profile of v9, /device:TPU:1, one launch (start us, length us, event | category | flops | bytes accessed | tf_op | source)
XLA Modules:
  0.0 124.2 jit_solution(16461458010388644027)
XLA Ops:
  0.0 3.9 %collective-permute-start = (bf16[2,448,1024]{2,1,0:T(8,128)(2,1)}, bf16[2,448,1024]{2,1,0:T(8,128)(2,1)}, u32[]{:S(2)}, u32[]{:S(2)}) collective-permute-start(bf16[2,448,1024]{2,1,0:T(8,128)(2,1)} %bitcast.22), channel_id=1, source_target_pairs={{0,1},{1,257},{2,3},{3,259},{4,5},{5,261},{6,7},{7,263},{8,9},{9,2... | collective-permute-start | bytes 5505032 | tf_op jit(solution)/shard_map/ppermute | solution.py:331
  3.9 2.6 %shard_map.55 = (bf16[64,32,128]{2,1,0:T(8,128)(2,1)}, f32[8,128]{1,0:T(8,128)S(1)}) custom-call(s32[8,384]{1,0:T(8,128)} %bitcast.18, bf16[448,384]{1,0:T(8,128)(2,1)} %bitcast.21), custom_call_target="tpu_custom_call" | custom-call | tf_op jit(solution)/shard_map/pallas_call | solution.py:332
  6.6 10.2 %all-to-all-start = ((bf16[64,32,128]{2,1,0:T(8,128)(2,1)}), bf16[64,32,128]{2,1,0:T(8,128)(2,1)S(1)}, u32[]{:S(2)}, u32[]{:S(2)}) async-start(bf16[64,32,128]{2,1,0:T(8,128)(2,1)} %get-tuple-element.20), calls=%async_computation | async-start | bytes 1048576 | tf_op jit(solution)/shard_map/all_to_all | solution.py:346
  16.7 3.4 %collective-permute-start.2 = (bf16[448,1024]{1,0:T(8,128)(2,1)}, bf16[448,1024]{1,0:T(8,128)(2,1)}, u32[]{:S(2)}, u32[]{:S(2)}) collective-permute-start(bf16[448,1024]{1,0:T(8,128)(2,1)} %bitcast.23), channel_id=1, source_target_pairs={{0,1},{1,257},{2,3},{3,259},{4,5},{5,261},{6,7},{7,263},{8,9},{9,2... | collective-permute-start | bytes 2752520 | tf_op jit(solution)/shard_map/ppermute | solution.py:352
  20.1 9.1 %collective-permute-done.own_hbm = bf16[2,448,1024]{2,1,0:T(8,128)(2,1)} collective-permute-done((bf16[2,448,1024]{2,1,0:T(8,128)(2,1)}, bf16[2,448,1024]{2,1,0:T(8,128)(2,1)}, u32[]{:S(2)}, u32[]{:S(2)}) %collective-permute-start) | collective-permute-done | bytes 1835040 | tf_op jit(solution)/shard_map/ppermute | solution.py:331
  29.3 10.2 %collective-permute-start.1 = (bf16[2,448,1024]{2,1,0:T(8,128)(2,1)}, bf16[2,448,1024]{2,1,0:T(8,128)(2,1)S(1)}, u32[]{:S(2)}, u32[]{:S(2)}) collective-permute-start(bf16[2,448,1024]{2,1,0:T(8,128)(2,1)} %collective-permute-done.own_hbm), channel_id=1, source_target_pairs={{0,1},{1,0},{2,3},{3,2},{4,5},{5,4},{6,7},{7,6},{8,9},{9,8},{10,11... | collective-permute-start | bytes 5505032 | tf_op jit(solution)/shard_map/ppermute | solution.py:351
  39.5 0.0 all-to-all-done.arrived_ref
  39.5 2.6 %shard_map.56 = (f32[312,2048]{1,0:T(8,128)S(1)}, bf16[312,512]{1,0:T(8,128)(2,1)S(1)}) custom-call(s32[1]{0:T(128)} %bitcast.core_ref, bf16[64,32,128]{2,1,0:T(8,128)(2,1)S(1)} %all-to-all-done.arrived_ref, bf16[2,448,1024]{2,1,0:T(8,128)(2,1)} %collective-permute-done.own_hbm), custom_call_target="tpu_custom_call" | custom-call | flops 49999998976 | bytes 4194304 | tf_op jit(solution)/shard_map/pallas_call | solution.py:353
  42.1 1.0 collective-permute-done.1.other_ref
  43.1 0.9 shard_map.57
  44.0 0.0 copy-start
  44.0 0.0 copy-start.1
  44.0 20.5 %fusion = bf16[40,2048]{1,0:T(8,128)(2,1)S(1)} fusion(bf16[312,2048]{1,0:T(8,128)(2,1)S(1)} %shard_map.57), kind=kCustom, calls=%all-reduce-scatter | all-reduce-scatter fusion | flops 655361 | bytes 1443840
  64.5 2.2 %collective-permute-start.5 = (bf16[7,2048]{1,0:T(8,128)(2,1)S(1)}, bf16[7,2048]{1,0:T(8,128)(2,1)S(1)}, u32[]{:S(2)}, u32[]{:S(2)}) collective-permute-start(bf16[7,2048]{1,0:T(8,128)(2,1)S(1)} %slice.5), channel_id=1, source_target_pairs={{0,32},{32,64},{64,96},{96,128},{128,160},{160,192},{192,224},{256... | collective-permute-start | bytes 86024
  66.7 1.3 %dynamic-slice.4 = u32[1]{0:T(128)} dynamic-slice(u32[512]{0:T(512)} %constant.10, u32[]{:S(6)} %partition-id.2), dynamic_slice_sizes={1} | dynamic-slice | bytes 12
  68.7 0.0 collective-permute-done.5
  68.7 0.2 concatenate
  68.9 0.1 constant_dynamic-slice_fusion.sums_ref
  69.0 0.0 collective-permute-done.2.down_ref
  69.0 1.0 shard_map.58
  70.0 5.2 %all-to-all-start.1 = ((bf16[8,32,1152]{2,1,0:T(8,128)(2,1)}), bf16[8,32,1152]{2,1,0:T(8,128)(2,1)S(1)}, u32[]{:S(2)}, u32[]{:S(2)}) async-start(bf16[8,32,1152]{2,1,0:T(8,128)(2,1)} %shard_map.58), calls=%async_computation.1 | async-start | bytes 1179648 | tf_op jit(solution)/shard_map/all_to_all | solution.py:377
  75.2 6.5 %collective-permute-start.3 = (bf16[448,1024]{1,0:T(8,128)(2,1)}, bf16[448,1024]{1,0:T(8,128)(2,1)S(1)}, u32[]{:S(2)}, u32[]{:S(2)}) collective-permute-start(bf16[448,1024]{1,0:T(8,128)(2,1)} %collective-permute-done.2.down_ref), channel_id=1, source_target_pairs={{0,1},{1,0},{2,3},{3,2},{4,5},{5,4},{6,7},{7,6},{8,9},{9,8},{10,11... | collective-permute-start | bytes 2752520 | tf_op jit(solution)/shard_map/ppermute | solution.py:372
  81.7 0.0 copy-done
  81.7 1.7 %shard_map.59 = (bf16[2,288,768]{2,1,0:T(8,128)(2,1)S(1)}, bf16[512,1024]{1,0:T(8,128)(2,1)S(1)}) custom-call(s32[1]{0:T(128)} %bitcast.core_ref, f32[8,128]{1,0:T(8,128)S(1)} %get-tuple-element.28.mark_ref, s32[8,384]{1,0:T(8,128)S(1)} %bitcast.19, f32[8,384]{1,0:T(8,128)S(1)} %bitcast.20, bf16[448,1024]{1,0:T(8,128)(2,1)} %collective-permute-done.2.down_ref), custom_call_target="tpu_custom_call" | custom-call | tf_op jit(solution)/shard_map/pallas_call | solution.py:378
  83.5 5.4 %all-to-all-done.1.hidden_ref = bf16[8,32,1152]{2,1,0:T(8,128)(2,1)S(1)} async-done(((bf16[8,32,1152]{2,1,0:T(8,128)(2,1)}), bf16[8,32,1152]{2,1,0:T(8,128)(2,1)S(1)}, u32[]{:S(2)}, u32[]{:S(2)}) %all-to-all-start.1) | async-done | bytes 589856 | tf_op jit(solution)/shard_map/all_to_all | solution.py:377
  88.9 0.0 collective-permute-done.3.other_ref
  88.9 1.4 %shard_map.60 = bf16[32,2,32,128]{3,2,1,0:T(8,128)(2,1)S(1)} custom-call(s32[1]{0:T(128)} %bitcast.core_ref, bf16[8,32,1152]{2,1,0:T(8,128)(2,1)S(1)} %all-to-all-done.1.hidden_ref, bf16[512,1024]{1,0:T(8,128)(2,1)S(1)} %get-tuple-element.33.own_ref, bf16[448,1024]{1,0:T(8,128)(2,1)S(1)} %collective-permute-done.3.other_ref), custom_call_target="tpu_custom_call" | custom-call | tf_op jit(solution)/shard_map/pallas_call | solution.py:387
  90.3 22.9 %all_to_all.15.back_ref = bf16[32,2,32,128]{3,2,1,0:T(8,128)(2,1)S(1)} all-to-all(bf16[32,2,32,128]{3,2,1,0:T(8,128)(2,1)S(1)} %shard_map.60), channel_id=1, replica_groups={{0,2,4,6,8,10,12,14,16,18,20,22,24,26,28,30,256,258,260,262,264,266,268..., dimensions={0} | all-to-all | bytes 1048576 | tf_op jit(solution)/shard_map/all_to_all | solution.py:392
  113.2 8.4 %collective-permute-start.4 = (bf16[32,32,128]{2,1,0:T(8,128)(2,1)S(1)}, bf16[32,32,128]{2,1,0:T(8,128)(2,1)S(1)}, u32[]{:S(2)}, u32[]{:S(2)}) collective-permute-start(bf16[32,32,128]{2,1,0:T(8,128)(2,1)S(1)} %slice_bitcast_fusion), channel_id=1, source_target_pairs={{0,1},{1,0},{2,3},{3,2},{4,5},{5,4},{6,7},{7,6},{8,9},{9,8},{10,11... | collective-permute-start | bytes 786440 | tf_op jit(solution)/shard_map/ppermute | solution.py:393
  121.6 0.8 shard_map.61.partial_ref
  122.4 0.3 collective-permute-done.4.came_ref
  122.7 1.5 %shard_map.62 = bf16[448,384]{1,0:T(8,128)(2,1)} custom-call(f32[448,384]{1,0:T(8,128)S(1)} %shard_map.61.partial_ref, bf16[32,32,128]{2,1,0:T(8,128)(2,1)S(1)} %collective-permute-done.4.came_ref, bf16[2,288,768]{2,1,0:T(8,128)(2,1)S(1)} %get-tuple-element.34.weights_ref), custom_call_target="tpu_custom_call" | custom-call | tf_op jit(solution)/shard_map/pallas_call | solution.py:395
  (3 shorter events, 0.0 us)
Async XLA Ops:
  0.0 29.3 %collective-permute-start = (bf16[2,448,1024]{2,1,0:T(8,128)(2,1)}, bf16[2,448,1024]{2,1,0:T(8,128)(2,1)}, u32[]{:S(2)}, u32[]{:S(2)}) collective-permute-start(bf16[2,448,1024]{2,1,0:T(8,128)(2,1)} %bitcast.22), channel_id=1, source_target_pairs={{0,1},{1,257},{2,3},{3,259},{4,5},{5,261},{6,7},{7,263},{8,9},{9,2... | collective-permute-start | bytes 5505032 | tf_op jit(solution)/shard_map/ppermute | solution.py:331
  6.6 32.9 %all-to-all-start = ((bf16[64,32,128]{2,1,0:T(8,128)(2,1)}), bf16[64,32,128]{2,1,0:T(8,128)(2,1)S(1)}, u32[]{:S(2)}, u32[]{:S(2)}) async-start(bf16[64,32,128]{2,1,0:T(8,128)(2,1)} %get-tuple-element.20), calls=%async_computation | async-start | bytes 1048576 | tf_op jit(solution)/shard_map/all_to_all | solution.py:346
  16.7 52.3 %collective-permute-start.2 = (bf16[448,1024]{1,0:T(8,128)(2,1)}, bf16[448,1024]{1,0:T(8,128)(2,1)}, u32[]{:S(2)}, u32[]{:S(2)}) collective-permute-start(bf16[448,1024]{1,0:T(8,128)(2,1)} %bitcast.23), channel_id=1, source_target_pairs={{0,1},{1,257},{2,3},{3,259},{4,5},{5,261},{6,7},{7,263},{8,9},{9,2... | collective-permute-start | bytes 2752520 | tf_op jit(solution)/shard_map/ppermute | solution.py:352
  29.3 13.8 %collective-permute-start.1 = (bf16[2,448,1024]{2,1,0:T(8,128)(2,1)}, bf16[2,448,1024]{2,1,0:T(8,128)(2,1)S(1)}, u32[]{:S(2)}, u32[]{:S(2)}) collective-permute-start(bf16[2,448,1024]{2,1,0:T(8,128)(2,1)} %collective-permute-done.own_hbm), channel_id=1, source_target_pairs={{0,1},{1,0},{2,3},{3,2},{4,5},{5,4},{6,7},{7,6},{8,9},{9,8},{10,11... | collective-permute-start | bytes 5505032 | tf_op jit(solution)/shard_map/ppermute | solution.py:351
  44.0 37.7 %copy-start = (s32[384,8]{0,1:T(8,128)S(1)}, s32[384,8]{0,1:T(8,128)}, u32[]{:S(2)}) copy-start(s32[384,8]{0,1:T(8,128)} %param.6) | copy-start | bytes 36868
  44.0 37.7 %copy-start.1 = (f32[384,8]{0,1:T(8,128)S(1)}, f32[384,8]{0,1:T(8,128)}, u32[]{:S(2)}) copy-start(f32[384,8]{0,1:T(8,128)} %param.7) | copy-start | bytes 36868
  64.5 4.1 %collective-permute-start.5 = (bf16[7,2048]{1,0:T(8,128)(2,1)S(1)}, bf16[7,2048]{1,0:T(8,128)(2,1)S(1)}, u32[]{:S(2)}, u32[]{:S(2)}) collective-permute-start(bf16[7,2048]{1,0:T(8,128)(2,1)S(1)} %slice.5), channel_id=1, source_target_pairs={{0,32},{32,64},{64,96},{96,128},{128,160},{160,192},{192,224},{256... | collective-permute-start | bytes 86024
  70.0 18.9 %all-to-all-start.1 = ((bf16[8,32,1152]{2,1,0:T(8,128)(2,1)}), bf16[8,32,1152]{2,1,0:T(8,128)(2,1)S(1)}, u32[]{:S(2)}, u32[]{:S(2)}) async-start(bf16[8,32,1152]{2,1,0:T(8,128)(2,1)} %shard_map.58), calls=%async_computation.1 | async-start | bytes 1179648 | tf_op jit(solution)/shard_map/all_to_all | solution.py:377
  75.2 13.7 %collective-permute-start.3 = (bf16[448,1024]{1,0:T(8,128)(2,1)}, bf16[448,1024]{1,0:T(8,128)(2,1)S(1)}, u32[]{:S(2)}, u32[]{:S(2)}) collective-permute-start(bf16[448,1024]{1,0:T(8,128)(2,1)} %collective-permute-done.2.down_ref), channel_id=1, source_target_pairs={{0,1},{1,0},{2,3},{3,2},{4,5},{5,4},{6,7},{7,6},{8,9},{9,8},{10,11... | collective-permute-start | bytes 2752520 | tf_op jit(solution)/shard_map/ppermute | solution.py:372
  113.2 9.6 %collective-permute-start.4 = (bf16[32,32,128]{2,1,0:T(8,128)(2,1)S(1)}, bf16[32,32,128]{2,1,0:T(8,128)(2,1)S(1)}, u32[]{:S(2)}, u32[]{:S(2)}) collective-permute-start(bf16[32,32,128]{2,1,0:T(8,128)(2,1)S(1)} %slice_bitcast_fusion), channel_id=1, source_target_pairs={{0,1},{1,0},{2,3},{3,2},{4,5},{5,4},{6,7},{7,6},{8,9},{9,8},{10,11... | collective-permute-start | bytes 786440 | tf_op jit(solution)/shard_map/ppermute | solution.py:393

commit v10 on v9

--- a/solution.py
+++ b/solution.py
@@ -253,11 +253,15 @@
     core = core_ref[0]
     hidden = gathered_hidden(hidden_ref)
     chips = EXPERTS // 2
-    other = jnp.concatenate(
-        [other_ref[...], jnp.zeros((PADDED - WIDTH, other_ref.shape[1]), BF16)], axis=0
-    )
-    for down, where in ((other, core), (own_ref[...], 1 - core)):
-        result = lax.dot_general(hidden, down, NT, preferred_element_type=F32).astype(BF16)
+    whole_tiles = WIDTH // 128 * 128
+    tail = jnp.concatenate(
+        [other_ref[whole_tiles:], jnp.zeros((PADDED - WIDTH, other_ref.shape[1]), BF16)], axis=0
+    )
+    for downs, where in (((other_ref[:whole_tiles], tail), core), ((own_ref[...],), 1 - core)):
+        result = [
+            lax.dot_general(hidden, down, NT, preferred_element_type=F32) for down in downs
+        ]
+        result = jnp.concatenate(result, axis=1).astype(BF16)
         last = jnp.dot(spread(EXPERTS), result[MAIN:], preferred_element_type=F32)
         blocks = pack(result[:MAIN].astype(F32), last).reshape(chips, 2, 32, 128)
         at = pl.ds(where * chips, chips)

time: 125 us -> 125 us (level)
  no operation moved by 1% of the time
where the time goes in v10:
time: 125 us
  starting transfers between devices  50 us (40%)
  blocking collectives  43.4 us (35%)
  waiting for transfers between devices  15.9 us (13%)
  Pallas kernels  12.9 us (10%)
  local copies, waits for them, and re-layouts  1.62 us (1%)
    all_to_all x1, blocking collectives, local(): lax.all_to_all(send, everyone, 0, 0, axis_index_groups=along_core, tiled=...  22.9 us
    unnamed x1, blocking collectives  20.5 us
    ppermute x1, starting transfers between devices, local(): other_in = lax.ppermute(own_in, 'expert', cores)  10.2 us
    all_to_all x1, starting transfers between devices, local(): lax.all_to_all(send, everyone, 0, 0, axis_index_groups=along_plane, tiled...  10.2 us
    ppermute x1, waiting for transfers between devices, local(): own_in = lax.ppermute(w_in, everyone, turn)  9.13 us
    ppermute x1, starting transfers between devices, local(): came = lax.ppermute(back[:, 1], 'expert', cores)  8.42 us
    ppermute x1, starting transfers between devices, local(): other_down = lax.ppermute(own_down, 'expert', cores)  6.51 us
    all_to_all x1, waiting for transfers between devices, local(): lax.all_to_all(hidden, 'group', 0, 0, axis_index_groups=along_z, tiled=True)  5.44 us
  transfers between devices with their start and end apart: 8, of which 4 were waited for; matrix products, arithmetic and copies ran while one was open for 18% of the time, Pallas kernels for 7%

profile of v10, /device:TPU:1, one launch (start us, length us, event | category | flops | bytes accessed | tf_op | source)
XLA Modules:
  0.0 124.6 jit_solution(15950997690367339072)
XLA Ops:
  0.0 3.9 %collective-permute-start = (bf16[2,448,1024]{2,1,0:T(8,128)(2,1)}, bf16[2,448,1024]{2,1,0:T(8,128)(2,1)}, u32[]{:S(2)}, u32[]{:S(2)}) collective-permute-start(bf16[2,448,1024]{2,1,0:T(8,128)(2,1)} %bitcast.22), channel_id=1, source_target_pairs={{0,1},{1,257},{2,3},{3,259},{4,5},{5,261},{6,7},{7,263},{8,9},{9,2... | collective-permute-start | bytes 5505032 | tf_op jit(solution)/shard_map/ppermute | solution.py:335
  3.9 2.6 %shard_map.55 = (bf16[64,32,128]{2,1,0:T(8,128)(2,1)}, f32[8,128]{1,0:T(8,128)S(1)}) custom-call(s32[8,384]{1,0:T(8,128)} %bitcast.18, bf16[448,384]{1,0:T(8,128)(2,1)} %bitcast.21), custom_call_target="tpu_custom_call" | custom-call | tf_op jit(solution)/shard_map/pallas_call | solution.py:336
  6.6 10.2 %all-to-all-start = ((bf16[64,32,128]{2,1,0:T(8,128)(2,1)}), bf16[64,32,128]{2,1,0:T(8,128)(2,1)S(1)}, u32[]{:S(2)}, u32[]{:S(2)}) async-start(bf16[64,32,128]{2,1,0:T(8,128)(2,1)} %get-tuple-element.20), calls=%async_computation | async-start | bytes 1048576 | tf_op jit(solution)/shard_map/all_to_all | solution.py:350
  16.7 3.4 %collective-permute-start.2 = (bf16[448,1024]{1,0:T(8,128)(2,1)}, bf16[448,1024]{1,0:T(8,128)(2,1)}, u32[]{:S(2)}, u32[]{:S(2)}) collective-permute-start(bf16[448,1024]{1,0:T(8,128)(2,1)} %bitcast.23), channel_id=1, source_target_pairs={{0,1},{1,257},{2,3},{3,259},{4,5},{5,261},{6,7},{7,263},{8,9},{9,2... | collective-permute-start | bytes 2752520 | tf_op jit(solution)/shard_map/ppermute | solution.py:356
  20.1 9.1 %collective-permute-done.own_hbm = bf16[2,448,1024]{2,1,0:T(8,128)(2,1)} collective-permute-done((bf16[2,448,1024]{2,1,0:T(8,128)(2,1)}, bf16[2,448,1024]{2,1,0:T(8,128)(2,1)}, u32[]{:S(2)}, u32[]{:S(2)}) %collective-permute-start) | collective-permute-done | bytes 1835040 | tf_op jit(solution)/shard_map/ppermute | solution.py:335
  29.3 10.2 %collective-permute-start.1 = (bf16[2,448,1024]{2,1,0:T(8,128)(2,1)}, bf16[2,448,1024]{2,1,0:T(8,128)(2,1)S(1)}, u32[]{:S(2)}, u32[]{:S(2)}) collective-permute-start(bf16[2,448,1024]{2,1,0:T(8,128)(2,1)} %collective-permute-done.own_hbm), channel_id=1, source_target_pairs={{0,1},{1,0},{2,3},{3,2},{4,5},{5,4},{6,7},{7,6},{8,9},{9,8},{10,11... | collective-permute-start | bytes 5505032 | tf_op jit(solution)/shard_map/ppermute | solution.py:355
  39.5 0.0 all-to-all-done.arrived_ref
  39.5 2.6 %shard_map.56 = (f32[312,2048]{1,0:T(8,128)S(1)}, bf16[312,512]{1,0:T(8,128)(2,1)S(1)}) custom-call(s32[1]{0:T(128)} %bitcast.core_ref, bf16[64,32,128]{2,1,0:T(8,128)(2,1)S(1)} %all-to-all-done.arrived_ref, bf16[2,448,1024]{2,1,0:T(8,128)(2,1)} %collective-permute-done.own_hbm), custom_call_target="tpu_custom_call" | custom-call | flops 49999998976 | bytes 4194304 | tf_op jit(solution)/shard_map/pallas_call | solution.py:357
  42.1 1.0 collective-permute-done.1.other_ref
  43.1 0.9 shard_map.57
  44.0 0.0 copy-start
  44.0 0.0 copy-start.1
  44.0 20.5 %fusion = bf16[40,2048]{1,0:T(8,128)(2,1)S(1)} fusion(bf16[312,2048]{1,0:T(8,128)(2,1)S(1)} %shard_map.57), kind=kCustom, calls=%all-reduce-scatter | all-reduce-scatter fusion | flops 655361 | bytes 1443840
  64.5 2.2 %collective-permute-start.5 = (bf16[7,2048]{1,0:T(8,128)(2,1)S(1)}, bf16[7,2048]{1,0:T(8,128)(2,1)S(1)}, u32[]{:S(2)}, u32[]{:S(2)}) collective-permute-start(bf16[7,2048]{1,0:T(8,128)(2,1)S(1)} %slice.5), channel_id=1, source_target_pairs={{0,32},{32,64},{64,96},{96,128},{128,160},{160,192},{192,224},{256... | collective-permute-start | bytes 86024
  66.7 1.3 %dynamic-slice.4 = u32[1]{0:T(128)} dynamic-slice(u32[512]{0:T(512)} %constant.10, u32[]{:S(6)} %partition-id.2), dynamic_slice_sizes={1} | dynamic-slice | bytes 12
  68.7 0.0 collective-permute-done.5
  68.7 0.2 concatenate
  68.9 0.1 constant_dynamic-slice_fusion.sums_ref
  69.0 0.0 collective-permute-done.2.down_ref
  69.0 1.0 shard_map.58
  70.0 5.2 %all-to-all-start.1 = ((bf16[8,32,1152]{2,1,0:T(8,128)(2,1)}), bf16[8,32,1152]{2,1,0:T(8,128)(2,1)S(1)}, u32[]{:S(2)}, u32[]{:S(2)}) async-start(bf16[8,32,1152]{2,1,0:T(8,128)(2,1)} %shard_map.58), calls=%async_computation.1 | async-start | bytes 1179648 | tf_op jit(solution)/shard_map/all_to_all | solution.py:381
  75.2 6.5 %collective-permute-start.3 = (bf16[448,1024]{1,0:T(8,128)(2,1)}, bf16[448,1024]{1,0:T(8,128)(2,1)S(1)}, u32[]{:S(2)}, u32[]{:S(2)}) collective-permute-start(bf16[448,1024]{1,0:T(8,128)(2,1)} %collective-permute-done.2.down_ref), channel_id=1, source_target_pairs={{0,1},{1,0},{2,3},{3,2},{4,5},{5,4},{6,7},{7,6},{8,9},{9,8},{10,11... | collective-permute-start | bytes 2752520 | tf_op jit(solution)/shard_map/ppermute | solution.py:376
  81.7 0.0 copy-done
  81.7 1.7 %shard_map.59 = (bf16[2,288,768]{2,1,0:T(8,128)(2,1)S(1)}, bf16[512,1024]{1,0:T(8,128)(2,1)S(1)}) custom-call(s32[1]{0:T(128)} %bitcast.core_ref, f32[8,128]{1,0:T(8,128)S(1)} %get-tuple-element.28.mark_ref, s32[8,384]{1,0:T(8,128)S(1)} %bitcast.19, f32[8,384]{1,0:T(8,128)S(1)} %bitcast.20, bf16[448,1024]{1,0:T(8,128)(2,1)} %collective-permute-done.2.down_ref), custom_call_target="tpu_custom_call" | custom-call | tf_op jit(solution)/shard_map/pallas_call | solution.py:382
  83.5 5.4 %all-to-all-done.1.hidden_ref = bf16[8,32,1152]{2,1,0:T(8,128)(2,1)S(1)} async-done(((bf16[8,32,1152]{2,1,0:T(8,128)(2,1)}), bf16[8,32,1152]{2,1,0:T(8,128)(2,1)S(1)}, u32[]{:S(2)}, u32[]{:S(2)}) %all-to-all-start.1) | async-done | bytes 589856 | tf_op jit(solution)/shard_map/all_to_all | solution.py:381
  88.9 0.0 collective-permute-done.3.other_ref
  88.9 1.7 %shard_map.60 = bf16[32,2,32,128]{3,2,1,0:T(8,128)(2,1)S(1)} custom-call(s32[1]{0:T(128)} %bitcast.core_ref, bf16[8,32,1152]{2,1,0:T(8,128)(2,1)S(1)} %all-to-all-done.1.hidden_ref, bf16[512,1024]{1,0:T(8,128)(2,1)S(1)} %get-tuple-element.33.own_ref, bf16[448,1024]{1,0:T(8,128)(2,1)S(1)} %collective-permute-done.3.other_ref), custom_call_target="tpu_custom_call" | custom-call | tf_op jit(solution)/shard_map/pallas_call | solution.py:391
  90.6 22.9 %all_to_all.15.back_ref = bf16[32,2,32,128]{3,2,1,0:T(8,128)(2,1)S(1)} all-to-all(bf16[32,2,32,128]{3,2,1,0:T(8,128)(2,1)S(1)} %shard_map.60), channel_id=1, replica_groups={{0,2,4,6,8,10,12,14,16,18,20,22,24,26,28,30,256,258,260,262,264,266,268..., dimensions={0} | all-to-all | bytes 1048576 | tf_op jit(solution)/shard_map/all_to_all | solution.py:396
  113.5 8.4 %collective-permute-start.4 = (bf16[32,32,128]{2,1,0:T(8,128)(2,1)S(1)}, bf16[32,32,128]{2,1,0:T(8,128)(2,1)S(1)}, u32[]{:S(2)}, u32[]{:S(2)}) collective-permute-start(bf16[32,32,128]{2,1,0:T(8,128)(2,1)S(1)} %slice_bitcast_fusion), channel_id=1, source_target_pairs={{0,1},{1,0},{2,3},{3,2},{4,5},{5,4},{6,7},{7,6},{8,9},{9,8},{10,11... | collective-permute-start | bytes 786440 | tf_op jit(solution)/shard_map/ppermute | solution.py:397
  121.9 0.8 shard_map.61.partial_ref
  122.8 0.3 collective-permute-done.4.came_ref
  123.1 1.5 %shard_map.62 = bf16[448,384]{1,0:T(8,128)(2,1)} custom-call(f32[448,384]{1,0:T(8,128)S(1)} %shard_map.61.partial_ref, bf16[32,32,128]{2,1,0:T(8,128)(2,1)S(1)} %collective-permute-done.4.came_ref, bf16[2,288,768]{2,1,0:T(8,128)(2,1)S(1)} %get-tuple-element.34.weights_ref), custom_call_target="tpu_custom_call" | custom-call | tf_op jit(solution)/shard_map/pallas_call | solution.py:399
  (3 shorter events, 0.0 us)
Async XLA Ops:
  0.0 29.3 %collective-permute-start = (bf16[2,448,1024]{2,1,0:T(8,128)(2,1)}, bf16[2,448,1024]{2,1,0:T(8,128)(2,1)}, u32[]{:S(2)}, u32[]{:S(2)}) collective-permute-start(bf16[2,448,1024]{2,1,0:T(8,128)(2,1)} %bitcast.22), channel_id=1, source_target_pairs={{0,1},{1,257},{2,3},{3,259},{4,5},{5,261},{6,7},{7,263},{8,9},{9,2... | collective-permute-start | bytes 5505032 | tf_op jit(solution)/shard_map/ppermute | solution.py:335
  6.6 32.9 %all-to-all-start = ((bf16[64,32,128]{2,1,0:T(8,128)(2,1)}), bf16[64,32,128]{2,1,0:T(8,128)(2,1)S(1)}, u32[]{:S(2)}, u32[]{:S(2)}) async-start(bf16[64,32,128]{2,1,0:T(8,128)(2,1)} %get-tuple-element.20), calls=%async_computation | async-start | bytes 1048576 | tf_op jit(solution)/shard_map/all_to_all | solution.py:350
  16.7 52.3 %collective-permute-start.2 = (bf16[448,1024]{1,0:T(8,128)(2,1)}, bf16[448,1024]{1,0:T(8,128)(2,1)}, u32[]{:S(2)}, u32[]{:S(2)}) collective-permute-start(bf16[448,1024]{1,0:T(8,128)(2,1)} %bitcast.23), channel_id=1, source_target_pairs={{0,1},{1,257},{2,3},{3,259},{4,5},{5,261},{6,7},{7,263},{8,9},{9,2... | collective-permute-start | bytes 2752520 | tf_op jit(solution)/shard_map/ppermute | solution.py:356
  29.3 13.8 %collective-permute-start.1 = (bf16[2,448,1024]{2,1,0:T(8,128)(2,1)}, bf16[2,448,1024]{2,1,0:T(8,128)(2,1)S(1)}, u32[]{:S(2)}, u32[]{:S(2)}) collective-permute-start(bf16[2,448,1024]{2,1,0:T(8,128)(2,1)} %collective-permute-done.own_hbm), channel_id=1, source_target_pairs={{0,1},{1,0},{2,3},{3,2},{4,5},{5,4},{6,7},{7,6},{8,9},{9,8},{10,11... | collective-permute-start | bytes 5505032 | tf_op jit(solution)/shard_map/ppermute | solution.py:355
  44.0 37.7 %copy-start = (s32[384,8]{0,1:T(8,128)S(1)}, s32[384,8]{0,1:T(8,128)}, u32[]{:S(2)}) copy-start(s32[384,8]{0,1:T(8,128)} %param.6) | copy-start | bytes 36868
  44.0 37.7 %copy-start.1 = (f32[384,8]{0,1:T(8,128)S(1)}, f32[384,8]{0,1:T(8,128)}, u32[]{:S(2)}) copy-start(f32[384,8]{0,1:T(8,128)} %param.7) | copy-start | bytes 36868
  64.5 4.1 %collective-permute-start.5 = (bf16[7,2048]{1,0:T(8,128)(2,1)S(1)}, bf16[7,2048]{1,0:T(8,128)(2,1)S(1)}, u32[]{:S(2)}, u32[]{:S(2)}) collective-permute-start(bf16[7,2048]{1,0:T(8,128)(2,1)S(1)} %slice.5), channel_id=1, source_target_pairs={{0,32},{32,64},{64,96},{96,128},{128,160},{160,192},{192,224},{256... | collective-permute-start | bytes 86024
  70.0 18.9 %all-to-all-start.1 = ((bf16[8,32,1152]{2,1,0:T(8,128)(2,1)}), bf16[8,32,1152]{2,1,0:T(8,128)(2,1)S(1)}, u32[]{:S(2)}, u32[]{:S(2)}) async-start(bf16[8,32,1152]{2,1,0:T(8,128)(2,1)} %shard_map.58), calls=%async_computation.1 | async-start | bytes 1179648 | tf_op jit(solution)/shard_map/all_to_all | solution.py:381
  75.2 13.7 %collective-permute-start.3 = (bf16[448,1024]{1,0:T(8,128)(2,1)}, bf16[448,1024]{1,0:T(8,128)(2,1)S(1)}, u32[]{:S(2)}, u32[]{:S(2)}) collective-permute-start(bf16[448,1024]{1,0:T(8,128)(2,1)} %collective-permute-done.2.down_ref), channel_id=1, source_target_pairs={{0,1},{1,0},{2,3},{3,2},{4,5},{5,4},{6,7},{7,6},{8,9},{9,8},{10,11... | collective-permute-start | bytes 2752520 | tf_op jit(solution)/shard_map/ppermute | solution.py:376
  113.5 9.6 %collective-permute-start.4 = (bf16[32,32,128]{2,1,0:T(8,128)(2,1)S(1)}, bf16[32,32,128]{2,1,0:T(8,128)(2,1)S(1)}, u32[]{:S(2)}, u32[]{:S(2)}) collective-permute-start(bf16[32,32,128]{2,1,0:T(8,128)(2,1)S(1)} %slice_bitcast_fusion), channel_id=1, source_target_pairs={{0,1},{1,0},{2,3},{3,2},{4,5},{5,4},{6,7},{7,6},{8,9},{9,8},{10,11... | collective-permute-start | bytes 786440 | tf_op jit(solution)/shard_map/ppermute | solution.py:397
